TPU v7x, 32 devices: a whole 2x2x4 slice. The times are simulated.
32 devices in a mesh: row: 4 (over y, x), col: 8 (over z, core).
Axes of the slice: x: 2, y: 2, z: 4, core: 2. Of those that a mesh axis runs over, the one named last changes fastest.
Arguments:
- i_list: int32 [2], replicated, may hold values from 0 to 127
- pairs: int32 [2, 2], replicated, may hold values from 0 to 127
- vir_offsets: int32 [2], replicated, may hold values from 0 to 1008, as said below
- occ_energy: float32 [128], replicated, may hold values from -2 to -0.5
- vir_energy: float32 [1024], replicated, may hold values from 0.5 to 5
- amplitudes: bfloat16 [2, 1024, 1024], P(None, 'row', 'col'), may hold values from -4 to 4
- integrals: bfloat16 [2, 1024, 16, 128], P(None, 'row', 'col'), may hold values from -1.25 to 1.25
Outputs:
- density: bfloat16 [2, 1024, 16, 128], P(None, 'row', 'col')
- amp_grad: bfloat16 [2, 1024, 1024], P(None, 'row', 'col')
Inputs may be any that keep to these rules, and one draw needn't show every extreme that they name: `vir_offsets`: the first entry is a multiple of 128 and at most 896; the second is at most 1008.
All inputs are finite; a program needn't handle non-finite values.
Results may differ from a plain program's by a relative error of at most 0.012.
Values may be sent and summed in bfloat16 or wider, within the bound.
No kernel may reach another device: no remote copies, remote signals or barrier semaphores. Data moves between devices by JAX's collectives and lax.ppermute only.
A program may use at most 64 MiB of HBM per device.

v0:
```python
import jax
import jax.numpy as jnp
from jax import lax
from jax.sharding import PartitionSpec as P


def pick_energy(index_values, energies):
    table = jnp.arange(energies.shape[0], dtype=jnp.int32)
    onehot = (index_values[..., None] == table).astype(jnp.float32)
    return jnp.sum(onehot * energies, axis=-1)


def local(i_list, pairs, vir_offsets, occ_energy, vir_energy, amplitudes, integrals):
    n_pair = amplitudes.shape[0]
    block_c = amplitudes.shape[1]
    width = vir_energy.shape[0]
    n_i = integrals.shape[0]
    block_d = integrals.shape[1]
    width_b = integrals.shape[2]
    width_a = integrals.shape[3]
    tile = width_b * width_a
    row_pos = lax.axis_index("row")
    col_pos = lax.axis_index("col")
    amp_full = lax.all_gather(amplitudes, "col", axis=2, tiled=True)
    amp_rows = amp_full.reshape(n_pair * block_c, width)
    occ_sum = (
        pick_energy(i_list, occ_energy)[:, None]
        + pick_energy(pairs[:, 0], occ_energy)[None, :]
        + pick_energy(pairs[:, 1], occ_energy)[None, :]
    )
    e_c = lax.dynamic_slice_in_dim(vir_energy, row_pos * block_c, block_c)
    e_b = lax.dynamic_slice_in_dim(vir_energy, vir_offsets[1] + col_pos * width_b, width_b)
    e_a = lax.dynamic_slice_in_dim(vir_energy, vir_offsets[0], width_a)
    base = -(e_c[:, None, None] + e_b[None, :, None] + e_a[None, None, :]).reshape(block_c, tile)
    grad_sum = jnp.zeros((n_pair, block_c, width), jnp.float32)
    dens_list = []
    for slot in range(n_i):
        ints_full = lax.all_gather(integrals[slot], "row", axis=0, tiled=True).reshape(width, tile)
        triples = jnp.einsum("pcd,dx->pcx", amp_full, ints_full, preferred_element_type=jnp.float32)
        scaled = (triples / (occ_sum[slot][:, None, None] + base[None])).astype(jnp.bfloat16)
        z_rows = scaled.reshape(n_pair * block_c, tile)
        dens_part = lax.psum_scatter(
            lax.dot_general(
                amp_rows, z_rows, (((0,), (0,)), ((), ())), preferred_element_type=jnp.float32
            ).astype(jnp.bfloat16),
            "row",
            scatter_dimension=0,
            tiled=True,
        )
        dens_list.append(dens_part.reshape(block_d, width_b, width_a))
        grad_sum = grad_sum + jnp.einsum(
            "pcx,dx->pcd", scaled, ints_full, preferred_element_type=jnp.float32
        )
    density = jnp.stack(dens_list)
    amp_grad = lax.psum_scatter(grad_sum, "col", scatter_dimension=2, tiled=True).astype(
        jnp.bfloat16
    )
    return (density, amp_grad)


def solution(mesh):
    return jax.shard_map(
        local,
        mesh=mesh,
        in_specs=(P(), P(), P(), P(), P(), P(None, "row", "col"), P(None, "row", "col", None)),
        out_specs=(P(None, "row", "col", None), P(None, "row", "col")),
        check_vma=False,
    )
```

profile of v0, /device:TPU:0, one launch (start us, length us, event | category | flops | bytes accessed | tf_op | source)
XLA Modules:
  0.0 137.5 jit_solution(2323614224044647246)
XLA Ops:
  7.2 0.0 copy-start.1
  7.2 0.0 copy-start.2
  7.2 0.0 copy-start.3
  7.2 0.0 all-gather.4.cloned.1.call-start
  7.2 0.7 all-gather.4.cloned.1.call-update
  7.9 0.0 reduce-scatter.4.cloned.1.call-start
  8.0 1.3 fusion.10
  11.2 0.8 dynamic_slice.9
  12.7 0.8 dynamic_slice.11
  13.4 0.8 dynamic_slice.10
  14.2 1.1 slice_bitcast_fusion.1
  15.3 11.5 %all-gather = bf16[1,1024,2,128]{3,2,0,1:T(2,128)(2,1)S(1)} all-gather(bf16[1,256,2,128]{3,2,0,1:T(2,128)(2,1)S(1)} %get-tuple-element.7), channel_id=2, replica_groups=mesh['row'=4,'col'=8] {'row'}, dimensions={1}, use_global_device_ids=true | all-gather | bytes 655360 | tf_op jit(solution)/shard_map/all_gather | solution.py:38
  26.8 0.3 reshape.85
  27.2 0.0 copy-done.1
  27.2 0.2 slice_reduce_fusion.1
  27.4 0.0 copy-done.2
  27.4 0.0 copy-done.3
  27.4 0.2 fusion.7
  27.6 0.1 add_add_fusion
  27.7 0.1 broadcast_add_fusion
  27.8 0.3 add.125
  28.2 8.2 %all-gather.4.cloned.1.call-done = bf16[2,256,1024]{2,1,0:T(8,128)(2,1)} async-done(((bf16[2,256,128]{2,1,0:T(8,128)(2,1)}), bf16[2,256,1024]{2,1,0:T(8,128)(2,1)}) %all-gather.4.cloned.1.call-update) | async-done | bytes 1048592 | tf_op jit(solution)/shard_map/all_gather | solution.py:24
  36.3 0.0 copy-start
  36.3 1.8 %fusion.4 = bf16[2,256,256]{2,1,0:T(8,128)(2,1)S(1)} fusion(bf16[2,256,1024]{2,1,0:T(8,128)(2,1)} %all-gather.4.cloned.1.call-done, bf16[1024,256,1]{1,0,2:T(8,128)(2,1)S(1)} %reshape.85, f32[256,256]{1,0:T(8,128)S(1)} %fusion.6, f32[2]{0:T(128)S(1)} %get-tuple-element.9), kind=kOutput, calls=%fused_computation.9 | convolution fusion | flops 268828672 | bytes 2097160 | tf_op jit(solution)/shard_map/pcd,dx->pcx/dot_general | solution.py:39
  38.1 0.0 copy-done
  38.1 1.3 fusion.3
  39.4 0.0 reduce-scatter.4.cloned.1.call-update
  39.4 0.0 reduce-scatter.6.cloned.1.call-start
  39.5 10.4 %all-gather.1 = bf16[1,1024,2,128]{3,2,0,1:T(2,128)(2,1)S(1)} all-gather(bf16[1,256,2,128]{3,2,0,1:T(2,128)(2,1)S(1)} %get-tuple-element.8), channel_id=3, replica_groups=mesh['row'=4,'col'=8] {'row'}, dimensions={1}, use_global_device_ids=true | all-gather | bytes 655360 | tf_op jit(solution)/shard_map/all_gather | solution.py:38
  49.8 0.3 reshape.87
  50.2 0.4 fusion.5
  50.6 1.3 fusion.2
  51.9 0.0 reduce-scatter.6.cloned.1.call-update
  51.9 0.0 reduce-scatter.8.cloned.1.call-start
  51.9 0.5 fusion.11
  52.4 1.8 %convolution_add_fusion = f32[2,256,1024]{2,1,0:T(8,128)} fusion(f32[2,256,1024]{2,1,0:T(8,128)S(1)} %fusion.11, bf16[2,256,256]{2,1,0:T(8,128)(2,1)S(1)} %fusion.5, bf16[1024,256,1]{1,0,2:T(8,128)(2,1)S(1)} %reshape.87), kind=kOutput, calls=%fused_computation | convolution fusion | flops 268959744 | bytes 4980736 | tf_op jit(solution)/shard_map/pcx,dx->pcd/dot_general | solution.py:51
  54.2 0.0 reduce-scatter.8.cloned.1.call-update
  54.3 9.2 %reduce-scatter.4.cloned.1.call-done = bf16[256,256]{0,1:T(8,128)(2,1)} async-done(((bf16[1024,256]{0,1:T(8,128)(2,1)}), bf16[256,256]{0,1:T(8,128)(2,1)}) %reduce-scatter.4.cloned.1.call-update) | async-done | bytes 131088 | tf_op jit(solution)/shard_map/reduce_scatter | solution.py:42
  63.4 1.0 copy.23
  64.4 26.8 %reduce-scatter.6.cloned.1.call-done = bf16[256,256]{0,1:T(8,128)(2,1)} async-done(((bf16[1024,256]{0,1:T(8,128)(2,1)}), bf16[256,256]{0,1:T(8,128)(2,1)}) %reduce-scatter.6.cloned.1.call-update) | async-done | bytes 131088 | tf_op jit(solution)/shard_map/reduce_scatter | solution.py:42
  91.3 1.0 copy.24
  92.3 1.1 pad_maximum_fusion
  93.4 35.9 %reduce-scatter.8.cloned.1.call-done = f32[2,256,128]{2,1,0:T(8,128)} async-done(((f32[2,256,1024]{2,1,0:T(8,128)}), f32[2,256,128]{2,1,0:T(8,128)}) %reduce-scatter.8.cloned.1.call-update) | async-done | bytes 262160 | tf_op jit(solution)/shard_map/reduce_scatter | solution.py:55
  129.3 1.6 %convert_element_type.30 = bf16[2,256,128]{2,1,0:T(8,128)(2,1)} convert(f32[2,256,128]{2,1,0:T(8,128)} %reduce-scatter.8.cloned.1.call-done) | non-fusion elementwise | flops 65536 | bytes 393216 | tf_op jit(solution)/shard_map/convert_element_type | solution.py:55
  (3 shorter events, 0.0 us)
Async XLA Ops:
  7.2 20.0 %copy-start.1 = (s32[2,2]{1,0:T(2,128)S(1)}, s32[2,2]{1,0:T(2,128)}, u32[]{:S(2)}) copy-start(s32[2,2]{1,0:T(2,128)} %param.8) | copy-start | bytes 52
  7.2 20.2 %copy-start.2 = (f32[128]{0:T(128)S(1)}, f32[128]{0:T(128)}, u32[]{:S(2)}) copy-start(f32[128]{0:T(128)} %param.10) | copy-start | bytes 1540
  7.2 20.2 %copy-start.3 = (s32[2]{0:T(128)S(1)}, s32[2]{0:T(128)}, u32[]{:S(2)}) copy-start(s32[2]{0:T(128)} %param.7) | copy-start | bytes 28
  7.2 29.1 %all-gather.4.cloned.1.call-start = ((), (), s32[]{:S(2)}) async-start(), calls=%async_computation.3 | async-start | bytes 1179648 | tf_op jit(solution)/shard_map/all_gather | solution.py:24
  7.9 55.5 %reduce-scatter.4.cloned.1.call-start = ((), (), s32[]{:S(2)}) async-start(), calls=%async_computation.4 | async-start | bytes 655360 | tf_op jit(solution)/shard_map/reduce_scatter | solution.py:42
  36.3 1.8 %copy-start = (bf16[2,256,1024]{2,1,0:T(8,128)(2,1)S(1)}, bf16[2,256,1024]{2,1,0:T(8,128)(2,1)}, u32[]{:S(2)}) copy-start(bf16[2,256,1024]{2,1,0:T(8,128)(2,1)} %all-gather.4.cloned.1.call-done) | copy-start | bytes 3145732
  39.4 51.9 %reduce-scatter.6.cloned.1.call-start = ((), (), s32[]{:S(2)}) async-start(), calls=%async_computation.5 | async-start | bytes 655360 | tf_op jit(solution)/shard_map/reduce_scatter | solution.py:42
  51.9 77.4 %reduce-scatter.8.cloned.1.call-start = ((), (), s32[]{:S(2)}) async-start(), calls=%async_computation.6 | async-start | bytes 2359296 | tf_op jit(solution)/shard_map/reduce_scatter | solution.py:55
Sparse Core Ops, SparseCore 0:
  9.6 26.6 all-gather.3
  39.5 23.8 reduce-scatter.3
  66.5 24.7 reduce-scatter.5
  93.4 35.8 reduce-scatter.7
where the time goes:
time: 138 us; the launch traced here: 137 us
  waiting for transfers between devices  80.8 us (59%)
  blocking collectives  21.9 us (16%)
  between operations  16.5 us (12%)
  local copies, waits for them, and re-layouts  7.98 us (6%)
  matrix products  7.04 us (5%)
  other arithmetic  3.11 us (2%)
    reduce_scatter x2, waiting for transfers between devices, local(): lax.psum_scatter(lax.dot_general(amp_rows, z_rows, (((0,), (0,)), ((), ()...  36 us
    reduce_scatter x1, waiting for transfers between devices, local(): lax.psum_scatter(grad_sum, 'col', scatter_dimension=2, tiled=True)  35.9 us
    all_gather x2, blocking collectives, local(): lax.all_gather(integrals[slot], 'row', axis=0, tiled=True)  21.9 us
    all_gather x1, waiting for transfers between devices, local(): amp_full = lax.all_gather(amplitudes, 'col', axis=2, tiled=True)  8.17 us
  transfers between devices with their start and end apart: 4, of which 4 were waited for; matrix products, arithmetic and copies ran while one was open for 10% of the time, Pallas kernels for 0%

commit v1 on v0

--- a/solution.py
+++ b/solution.py
@@ -1,7 +1,14 @@
+import functools
+
 import jax
 import jax.numpy as jnp
 from jax import lax
+from jax.experimental import pallas as pl
+from jax.experimental.pallas import tpu as pltpu
 from jax.sharding import PartitionSpec as P
+
+CORES = 2
+LANES = 128
 
 
 def pick_energy(index_values, energies):
@@ -10,7 +17,7 @@
     return jnp.sum(onehot * energies, axis=-1)
 
 
-def local(i_list, pairs, vir_offsets, occ_energy, vir_energy, amplitudes, integrals):
+def gathered(i_list, pairs, vir_offsets, occ_energy, vir_energy, amplitudes, integrals):
     n_pair = amplitudes.shape[0]
     block_c = amplitudes.shape[1]
     width = vir_energy.shape[0]
@@ -58,7 +65,196 @@
     return (density, amp_grad)
 
 
+def products(n_row, n_chip, *refs):
+    refs = list(refs)
+    i_list, pairs, vir_offsets, occ_energy, vir_smem, vir_rows = refs[:6]
+    mine = refs[6 : 6 + n_chip]
+    other = refs[6 + n_chip : 6 + 2 * n_chip]
+    ints = refs[6 + 2 * n_chip : 6 + 2 * n_chip + n_row]
+    outs = refs[6 + 2 * n_chip + n_row :]
+    dens_out = outs[:n_row]
+    grad_mine, grad_other, amp_full, ints_full = outs[n_row:]
+    n_pair, block_c, width = amp_full.shape
+    n_i, _, tile = ints_full.shape
+    sub_d = mine[0].shape[2]
+    block_d = ints[0].shape[1]
+    width_b = tile // LANES
+    row_pos = lax.axis_index("row")
+    col_pos = lax.axis_index("col")
+    chip_pos = col_pos // CORES
+    core_pos = col_pos % CORES
+    for step in range(n_chip):
+        base_d = (chip_pos ^ step) * (CORES * sub_d)
+        at_mine = pl.multiple_of(base_d + core_pos * sub_d, sub_d)
+        at_other = pl.multiple_of(base_d + (1 - core_pos) * sub_d, sub_d)
+        amp_full[:, :, pl.ds(at_mine, sub_d)] = mine[step][...]
+        amp_full[:, :, pl.ds(at_other, sub_d)] = other[step][...]
+    for step in range(n_row):
+        at = pl.multiple_of((row_pos ^ step) * block_d, block_d)
+        ints_full[:, pl.ds(at, block_d), :] = ints[step][...]
+
+    rows_c = block_c // LANES
+    e_c = vir_rows[pl.ds(row_pos * rows_c, rows_c), :]
+    e_c = jnp.concatenate(
+        [jnp.broadcast_to(e_c[k : k + 1, :], (LANES, LANES)).T for k in range(rows_c)], axis=0
+    )
+    e_a = vir_rows[pl.ds(vir_offsets[0] // LANES, 1), :]
+    base = []
+    for b in range(width_b):
+        e_b = vir_smem[vir_offsets[1] + col_pos * width_b + b]
+        base.append(-((e_c + e_b) + e_a))
+    base = jnp.concatenate(base, axis=1)
+
+    scaled = []
+    for slot in range(n_i):
+        for pair in range(n_pair):
+            occ = (
+                occ_energy[i_list[slot]]
+                + occ_energy[pairs[pair, 0]]
+                + occ_energy[pairs[pair, 1]]
+            )
+            triples = jnp.dot(amp_full[pair], ints_full[slot], preferred_element_type=jnp.float32)
+            scaled.append((triples / (occ + base)).astype(jnp.bfloat16))
+
+    for step in range(n_chip):
+        base_d = (chip_pos ^ step) * (CORES * sub_d)
+        for core, out in ((core_pos, grad_mine), (1 - core_pos, grad_other)):
+            at = pl.multiple_of(base_d + core * sub_d, sub_d)
+            for pair in range(n_pair):
+                total = None
+                for slot in range(n_i):
+                    part = lax.dot_general(
+                        scaled[slot * n_pair + pair],
+                        ints_full[slot, pl.ds(at, sub_d), :],
+                        (((1,), (1,)), ((), ())),
+                        preferred_element_type=jnp.float32,
+                    )
+                    total = part if total is None else total + part
+                out[step, pair] = total.astype(out.dtype)
+
+    for step in range(n_row):
+        at = pl.multiple_of((row_pos ^ step) * block_d, block_d)
+        for slot in range(n_i):
+            total = None
+            for pair in range(n_pair):
+                part = lax.dot_general(
+                    amp_full[pair, :, pl.ds(at, block_d)],
+                    scaled[slot * n_pair + pair],
+                    (((0,), (0,)), ((), ())),
+                    preferred_element_type=jnp.float32,
+                )
+                total = part if total is None else total + part
+            dens_out[step][slot] = total.astype(dens_out[step].dtype)
+
+
+def core_sums(n_chip, own, received, kept, *outs):
+    kept[...] = own[0] + received[0].astype(jnp.float32)
+    for step in range(1, n_chip):
+        total = own[step] + received[step].astype(jnp.float32)
+        outs[step - 1][...] = total.astype(outs[step - 1].dtype)
+
+
+def exchanged(n_row, n_col, *args):
+    i_list, pairs, vir_offsets, occ_energy, vir_energy, amplitudes, integrals = args
+    n_pair, block_c, sub_d = amplitudes.shape
+    n_i, block_d, width_b, width_a = integrals.shape
+    width = vir_energy.shape[0]
+    tile = width_b * width_a
+    n_chip = n_col // CORES
+
+    def over_row(value, mask):
+        return lax.ppermute(value, "row", [(k, k ^ mask) for k in range(n_row)])
+
+    def over_chips(value, mask):
+        return lax.ppermute(value, "col", [(k, k ^ (CORES * mask)) for k in range(n_col)])
+
+    def over_cores(value):
+        return lax.ppermute(value, "col", [(k, k ^ 1) for k in range(n_col)])
+
+    ints_own = integrals.reshape(n_i, block_d, tile)
+    mine = [amplitudes] + [over_chips(amplitudes, step) for step in range(1, n_chip)]
+    ints = [ints_own] + [over_row(ints_own, step) for step in range(1, n_row)]
+    other = [over_cores(value) for value in mine]
+
+    vmem = pl.BlockSpec(memory_space=pltpu.VMEM)
+    smem = pl.BlockSpec(memory_space=pltpu.SMEM)
+    f32, bf16 = jnp.float32, jnp.bfloat16
+    flops = 6 * n_i * n_pair * block_c * width * tile
+    results = pl.pallas_call(
+        functools.partial(products, n_row, n_chip),
+        out_shape=[
+            jax.ShapeDtypeStruct((n_i, block_d, tile), f32 if step == 0 else bf16)
+            for step in range(n_row)
+        ]
+        + [
+            jax.ShapeDtypeStruct((n_chip, n_pair, block_c, sub_d), f32),
+            jax.ShapeDtypeStruct((n_chip, n_pair, block_c, sub_d), bf16),
+        ],
+        in_specs=[smem] * 5 + [vmem] * (1 + 2 * n_chip + n_row),
+        out_specs=[vmem] * (n_row + 2),
+        scratch_shapes=[
+            pltpu.VMEM((n_pair, block_c, width), bf16),
+            pltpu.VMEM((n_i, width, tile), bf16),
+        ],
+        compiler_params=pltpu.CompilerParams(vmem_limit_bytes=40 * 2**20),
+        cost_estimate=pl.CostEstimate(flops=flops, bytes_accessed=8 * 2**20, transcendentals=0),
+        name="products",
+    )(
+        i_list,
+        pairs,
+        vir_offsets,
+        occ_energy,
+        vir_energy,
+        vir_energy.reshape(width // LANES, LANES),
+        *mine,
+        *other,
+        *ints,
+    )
+    dens = results[:n_row]
+    grad_mine, grad_other = results[n_row:]
+    block = (n_pair, block_c, sub_d)
+    grads = pl.pallas_call(
+        functools.partial(core_sums, n_chip),
+        out_shape=[
+            jax.ShapeDtypeStruct(block, f32 if step == 0 else bf16) for step in range(n_chip)
+        ],
+        in_specs=[vmem] * 2,
+        out_specs=[vmem] * n_chip,
+        compiler_params=pltpu.CompilerParams(vmem_limit_bytes=24 * 2**20),
+        name="core_sums",
+    )(grad_mine, over_cores(grad_other))
+    dens_in = [over_row(dens[step], step) for step in range(1, n_row)]
+    grad_in = [over_chips(grads[step], step) for step in range(1, n_chip)]
+    density = dens[0]
+    for value in dens_in:
+        density = density + value.astype(f32)
+    amp_grad = grads[0]
+    for value in grad_in:
+        amp_grad = amp_grad + value.astype(f32)
+    return (
+        density.astype(bf16).reshape(n_i, block_d, width_b, width_a),
+        amp_grad.astype(bf16),
+    )
+
+
 def solution(mesh):
+    n_row, n_col = mesh.shape["row"], mesh.shape["col"]
+
+    def local(*args):
+        block_c, sub_d = args[5].shape[1:]
+        block_d, _, width_a = args[6].shape[1:]
+        whole_tiles = (
+            width_a == LANES
+            and sub_d % LANES == 0
+            and block_c % LANES == 0
+            and block_d % LANES == 0
+            and n_row & (n_row - 1) == 0
+            and n_col & (n_col - 1) == 0
+        )
+        if whole_tiles:
+            return exchanged(n_row, n_col, *args)
+        return gathered(*args)
+
     return jax.shard_map(
         local,
         mesh=mesh,

time: 138 us -> 46.5 us (0.34)
  waiting for transfers between devices: 80.8 us -> 18.5 us
  blocking collectives: 21.9 us -> 0 us
  starting transfers between devices: 0.16 us -> 20.8 us
  between operations: 16.5 us -> 0.74 us
  matrix products: 7.04 us -> 0 us
  local copies, waits for them, and re-layouts: 7.98 us -> 1.94 us
  Pallas kernels: 0 us -> 3.52 us
  other arithmetic: 3.11 us -> 0.84 us
    reduce_scatter x3 -> x0, waiting for transfers between devices: 71.9 us -> none  [the longest x2 36 us: local(): lax.psum_scatter(lax.dot_general(amp_rows, z_rows, (((0,), (0,)), ((), ()...]
    all_gather x2 -> x0, blocking collectives: 21.9 us -> none  [local(): lax.all_gather(integrals[slot], 'row', axis=0, tiled=True)]
    ppermute x0 -> x17, starting transfers between devices: none -> 20.8 us  [the longest x6 11 us: over_chips(): lax.ppermute(value, 'col', [(k, k ^ CORES * mask) for k in range(n_col)])]
    ppermute x0 -> x17, waiting for transfers between devices: none -> 18.5 us  [the longest x6 10.7 us: over_row(): return lax.ppermute(value, 'row', [(k, k ^ mask) for k in range(n_row)])]
    all_gather x1 -> x0, waiting for transfers between devices: 8.17 us -> none  [local(): amp_full = lax.all_gather(amplitudes, 'col', axis=2, tiled=True)]
    dot_general x6 -> x0, matrix products: 7.04 us -> none  [the longest x2 2.55 us: local(): lax.dot_general(amp_rows, z_rows, (((0,), (0,)), ((), ())), preferred_ele...]
    pallas_call x0 -> x2, Pallas kernels: none -> 3.52 us  [the longest x1 3.43 us: exchanged(): pl.pallas_call(functools.partial(products, n_row, n_chip), out_shape=[jax...]
    dynamic_slice x3 -> x0, local copies, waits for them, and re-layouts: 2.29 us -> none  [the longest x1 0.77 us: local(): e_c = lax.dynamic_slice_in_dim(vir_energy, row_pos * block_c, block_c)]
  transfers between devices with their start and end apart: 4 -> 17, of which waited for: 4 -> 8; matrix products, arithmetic and copies ran while one was open for 10% -> 4% of each run, Pallas kernels for 0% -> 0%
where the time goes in v1:
time: 46.5 us; the launch traced here: 46.4 us
  starting transfers between devices  20.8 us (45%)
  waiting for transfers between devices  18.5 us (40%)
  Pallas kernels  3.52 us (8%)
  local copies, waits for them, and re-layouts  1.94 us (4%)
  other arithmetic  0.84 us (2%)
  between operations  0.74 us (2%)
    ppermute x6, starting transfers between devices, over_chips(): lax.ppermute(value, 'col', [(k, k ^ CORES * mask) for k in range(n_col)])  11 us
    ppermute x6, waiting for transfers between devices, over_row(): return lax.ppermute(value, 'row', [(k, k ^ mask) for k in range(n_row)])  10.7 us
    ppermute x6, starting transfers between devices, over_row(): return lax.ppermute(value, 'row', [(k, k ^ mask) for k in range(n_row)])  9.22 us
    ppermute x6, waiting for transfers between devices, over_chips(): lax.ppermute(value, 'col', [(k, k ^ CORES * mask) for k in range(n_col)])  6.74 us
    pallas_call x1, Pallas kernels, exchanged(): pl.pallas_call(functools.partial(products, n_row, n_chip), out_shape=[jax...  3.43 us
    reshape x1, local copies, waits for them, and re-layouts, exchanged(): ints_own = integrals.reshape(n_i, block_d, tile)  1.15 us
    ppermute x5, waiting for transfers between devices, over_cores(): return lax.ppermute(value, 'col', [(k, k ^ 1) for k in range(n_col)])  1.03 us
  transfers between devices with their start and end apart: 17, of which 8 were waited for; matrix products, arithmetic and copies ran while one was open for 4% of the time, Pallas kernels for 0%

profile of v1, /device:TPU:0, one launch (start us, length us, event | category | flops | bytes accessed | tf_op | source)
XLA Modules:
  0.0 46.4 jit_solution(1350562532523856725)
XLA Ops:
  0.6 0.0 copy-start
  0.6 0.0 copy-start.1
  0.7 5.1 %collective-permute-start.2 = (bf16[2,256,128]{2,1,0:T(8,128)(2,1)}, bf16[2,256,128]{2,1,0:T(8,128)(2,1)S(1)}, u32[]{:S(2)}, u32[]{:S(2)}) collective-permute-start(bf16[2,256,128]{2,1,0:T(8,128)(2,1)} %refs_6_.1), channel_id=1, source_target_pairs={{0,6},{1,7},{2,4},{3,5},{4,2},{5,3},{6,0},{7,1},{8,14},{9,15},{10,... | collective-permute-start | bytes 393224 | tf_op jit(solution)/shard_map/ppermute | solution.py:169
  5.8 0.0 collective-permute-start.1
  5.8 0.6 %collective-permute-start = (bf16[2,256,128]{2,1,0:T(8,128)(2,1)}, bf16[2,256,128]{2,1,0:T(8,128)(2,1)S(1)}, u32[]{:S(2)}, u32[]{:S(2)}) collective-permute-start(bf16[2,256,128]{2,1,0:T(8,128)(2,1)} %refs_6_.1), channel_id=1, source_target_pairs={{0,2},{1,3},{2,0},{3,1},{4,6},{5,7},{6,4},{7,5},{8,10},{9,11},{10,... | collective-permute-start | bytes 393224 | tf_op jit(solution)/shard_map/ppermute | solution.py:169
  6.4 0.0 collective-permute-start.3
  6.4 1.1 %reshape.14.refs_14_ = bf16[2,256,256]{2,1,0:T(8,128)(2,1)S(1)} reshape(bf16[2,256,2,128]{3,2,1,0:T(2,128)(2,1)} %param.13) | data formatting | bytes 524288 | tf_op jit(solution)/shard_map/reshape | solution.py:174
  7.6 0.0 copy-start.2
  7.6 0.0 copy-start.3
  7.6 2.7 %collective-permute-start.9 = (bf16[2,256,256]{2,1,0:T(8,128)(2,1)S(1)}, bf16[2,256,256]{2,1,0:T(8,128)(2,1)S(1)}, u32[]{:S(2)}, u32[]{:S(2)}) collective-permute-start(bf16[2,256,256]{2,1,0:T(8,128)(2,1)S(1)} %reshape.14.refs_14_), channel_id=1, source_target_pairs={{0,24},{8,16},{16,8},{24,0},{1,25},{9,17},{17,9},{25,1},{2,26},{10... | collective-permute-start | bytes 786440 | tf_op jit(solution)/shard_map/ppermute | solution.py:166
  10.2 0.2 collective-permute-done.2.refs_9_
  10.4 0.1 collective-permute-start.6
  10.5 6.6 %collective-permute-done.1.refs_8_ = bf16[2,256,128]{2,1,0:T(8,128)(2,1)S(1)} collective-permute-done((bf16[2,256,128]{2,1,0:T(8,128)(2,1)}, bf16[2,256,128]{2,1,0:T(8,128)(2,1)S(1)}, u32[]{:S(2)}, u32[]{:S(2)}) %collective-permute-start.1) | collective-permute-done | bytes 131104 | tf_op jit(solution)/shard_map/ppermute | solution.py:169
  17.1 1.5 %collective-permute-start.8 = (bf16[2,256,256]{2,1,0:T(8,128)(2,1)S(1)}, bf16[2,256,256]{2,1,0:T(8,128)(2,1)S(1)}, u32[]{:S(2)}, u32[]{:S(2)}) collective-permute-start(bf16[2,256,256]{2,1,0:T(8,128)(2,1)S(1)} %reshape.14.refs_14_), channel_id=1, source_target_pairs={{0,16},{8,24},{16,0},{24,8},{1,17},{9,25},{17,1},{25,9},{2,18},{10... | collective-permute-start | bytes 786440 | tf_op jit(solution)/shard_map/ppermute | solution.py:166
  18.6 0.0 collective-permute-done.refs_7_
  18.6 1.5 %collective-permute-start.7 = (bf16[2,256,256]{2,1,0:T(8,128)(2,1)S(1)}, bf16[2,256,256]{2,1,0:T(8,128)(2,1)S(1)}, u32[]{:S(2)}, u32[]{:S(2)}) collective-permute-start(bf16[2,256,256]{2,1,0:T(8,128)(2,1)S(1)} %reshape.14.refs_14_), channel_id=1, source_target_pairs={{0,8},{8,0},{16,24},{24,16},{1,9},{9,1},{17,25},{25,17},{2,10},{10... | collective-permute-start | bytes 786440 | tf_op jit(solution)/shard_map/ppermute | solution.py:166
  20.1 0.0 collective-permute-done.3.refs_10_
  20.1 0.0 collective-permute-start.5
  20.1 0.0 collective-permute-done.6.refs_13_
  20.1 0.5 %collective-permute-start.4 = (bf16[2,256,128]{2,1,0:T(8,128)(2,1)S(1)}, bf16[2,256,128]{2,1,0:T(8,128)(2,1)S(1)}, u32[]{:S(2)}, u32[]{:S(2)}) collective-permute-start(bf16[2,256,128]{2,1,0:T(8,128)(2,1)S(1)} %collective-permute-done.refs_7_), channel_id=1, source_target_pairs={{0,1},{1,0},{2,3},{3,2},{4,5},{5,4},{6,7},{7,6},{8,9},{9,8},{10,11... | collective-permute-start | bytes 393224 | tf_op jit(solution)/shard_map/ppermute | solution.py:172
  20.6 0.8 %collective-permute-done.5.refs_12_ = bf16[2,256,128]{2,1,0:T(8,128)(2,1)S(1)} collective-permute-done((bf16[2,256,128]{2,1,0:T(8,128)(2,1)S(1)}, bf16[2,256,128]{2,1,0:T(8,128)(2,1)S(1)}, u32[]{:S(2)}, u32[]{:S(2)}) %collective-permute-start.5) | collective-permute-done | bytes 131104 | tf_op jit(solution)/shard_map/ppermute | solution.py:172
  21.4 0.2 collective-permute-done.4.refs_11_
  21.6 0.0 collective-permute-done.9.refs_17_
  21.6 2.8 %collective-permute-done.8.refs_16_ = bf16[2,256,256]{2,1,0:T(8,128)(2,1)S(1)} collective-permute-done((bf16[2,256,256]{2,1,0:T(8,128)(2,1)S(1)}, bf16[2,256,256]{2,1,0:T(8,128)(2,1)S(1)}, u32[]{:S(2)}, u32[]{:S(2)}) %collective-permute-start.8) | collective-permute-done | bytes 262176 | tf_op jit(solution)/shard_map/ppermute | solution.py:166
  24.4 1.2 %collective-permute-done.7.refs_15_ = bf16[2,256,256]{2,1,0:T(8,128)(2,1)S(1)} collective-permute-done((bf16[2,256,256]{2,1,0:T(8,128)(2,1)S(1)}, bf16[2,256,256]{2,1,0:T(8,128)(2,1)S(1)}, u32[]{:S(2)}, u32[]{:S(2)}) %collective-permute-start.7) | collective-permute-done | bytes 262176 | tf_op jit(solution)/shard_map/ppermute | solution.py:166
  25.7 0.0 copy-done
  25.7 0.0 copy-done.1
  25.7 0.0 copy-done.4
  25.7 0.0 copy-done.5
  25.7 3.4 %products.1 = (f32[2,256,256]{2,1,0:T(8,128)S(1)}, bf16[2,256,256]{2,1,0:T(8,128)(2,1)S(1)}, bf16[2,256,256]{2,1,0:T(8,128)(2,1)S(1)}, bf16[2,256,256]{2,1,0:T(8...) custom-call(s32[2]{0:T(128)S(1)} %copy-done.3, s32[2,2]{1,0:T(2,128)S(1)} %copy-done.2, ...), custom_call_target="tpu_custom_call" | custom-call | flops 1610612736 | bytes 8388608 | tf_op jit(solution)/shard_map/products/pallas_call | solution.py:183
  29.1 0.1 collective-permute-start.13
  29.2 1.6 %collective-permute-start.10 = (bf16[2,256,256]{2,1,0:T(8,128)(2,1)S(1)}, bf16[2,256,256]{2,1,0:T(8,128)(2,1)S(1)}, u32[]{:S(2)}, u32[]{:S(2)}) collective-permute-start(bf16[2,256,256]{2,1,0:T(8,128)(2,1)S(1)} %get-tuple-element.13), channel_id=1, source_target_pairs={{0,8},{8,0},{16,24},{24,16},{1,9},{9,1},{17,25},{25,17},{2,10},{10... | collective-permute-start | bytes 786440 | tf_op jit(solution)/shard_map/ppermute | solution.py:166
  30.8 0.5 %collective-permute-start.11 = (bf16[2,256,256]{2,1,0:T(8,128)(2,1)S(1)}, bf16[2,256,256]{2,1,0:T(8,128)(2,1)S(1)}, u32[]{:S(2)}, u32[]{:S(2)}) collective-permute-start(bf16[2,256,256]{2,1,0:T(8,128)(2,1)S(1)} %get-tuple-element.14), channel_id=1, source_target_pairs={{0,16},{8,24},{16,0},{24,8},{1,17},{9,25},{17,1},{25,9},{2,18},{10... | collective-permute-start | bytes 786440 | tf_op jit(solution)/shard_map/ppermute | solution.py:166
  31.3 1.5 %collective-permute-start.12 = (bf16[2,256,256]{2,1,0:T(8,128)(2,1)S(1)}, bf16[2,256,256]{2,1,0:T(8,128)(2,1)S(1)}, u32[]{:S(2)}, u32[]{:S(2)}) collective-permute-start(bf16[2,256,256]{2,1,0:T(8,128)(2,1)S(1)} %get-tuple-element.15), channel_id=1, source_target_pairs={{0,24},{8,16},{16,8},{24,0},{1,25},{9,17},{17,9},{25,1},{2,26},{10... | collective-permute-start | bytes 786440 | tf_op jit(solution)/shard_map/ppermute | solution.py:166
  32.8 0.0 collective-permute-done.13.received
  32.8 0.1 core_sums.1
  32.9 0.1 collective-permute-start.14
  33.0 2.8 %collective-permute-start.15 = (bf16[2,256,128]{2,1,0:T(8,128)(2,1)S(1)}, bf16[2,256,128]{2,1,0:T(8,128)(2,1)S(1)}, u32[]{:S(2)}, u32[]{:S(2)}) collective-permute-start(bf16[2,256,128]{2,1,0:T(8,128)(2,1)S(1)} %get-tuple-element.20), channel_id=1, source_target_pairs={{0,4},{1,5},{2,6},{3,7},{4,0},{5,1},{6,2},{7,3},{8,12},{9,13},{10,... | collective-permute-start | bytes 393224 | tf_op jit(solution)/shard_map/ppermute | solution.py:169
  35.8 2.6 %collective-permute-done.10 = bf16[2,256,256]{2,1,0:T(8,128)(2,1)S(1)} collective-permute-done((bf16[2,256,256]{2,1,0:T(8,128)(2,1)S(1)}, bf16[2,256,256]{2,1,0:T(8,128)(2,1)S(1)}, u32[]{:S(2)}, u32[]{:S(2)}) %collective-permute-start.10) | collective-permute-done | bytes 262176 | tf_op jit(solution)/shard_map/ppermute | solution.py:166
  38.4 2.3 %collective-permute-start.16 = (bf16[2,256,128]{2,1,0:T(8,128)(2,1)S(1)}, bf16[2,256,128]{2,1,0:T(8,128)(2,1)S(1)}, u32[]{:S(2)}, u32[]{:S(2)}) collective-permute-start(bf16[2,256,128]{2,1,0:T(8,128)(2,1)S(1)} %get-tuple-element.21), channel_id=1, source_target_pairs={{0,6},{1,7},{2,4},{3,5},{4,2},{5,3},{6,0},{7,1},{8,14},{9,15},{10,... | collective-permute-start | bytes 393224 | tf_op jit(solution)/shard_map/ppermute | solution.py:169
  40.7 4.1 %collective-permute-done.11 = bf16[2,256,256]{2,1,0:T(8,128)(2,1)S(1)} collective-permute-done((bf16[2,256,256]{2,1,0:T(8,128)(2,1)S(1)}, bf16[2,256,256]{2,1,0:T(8,128)(2,1)S(1)}, u32[]{:S(2)}, u32[]{:S(2)}) %collective-permute-start.11) | collective-permute-done | bytes 262176 | tf_op jit(solution)/shard_map/ppermute | solution.py:166
  44.8 0.0 collective-permute-done.12
  44.8 0.1 add_convert_fusion
  44.9 0.8 %reshape.15 = bf16[2,256,2,128]{3,2,1,0:T(2,128)(2,1)} reshape(bf16[2,256,256]{2,1,0:T(8,128)(2,1)S(1)} %add_convert_fusion) | data formatting | bytes 524288 | tf_op jit(solution)/shard_map/reshape | solution.py:235
  45.7 0.0 collective-permute-done.14
  45.7 0.0 collective-permute-done.15
  45.7 0.0 collective-permute-done.16
  45.7 0.7 %add_convert_fusion.1 = bf16[2,256,128]{2,1,0:T(8,128)(2,1)} fusion(bf16[2,256,128]{2,1,0:T(8,128)(2,1)S(1)} %collective-permute-done.16, bf16[2,256,128]{2,1,0:T(8,128)(2,1)S(1)} %collective-permute-done.15, f32[2,256,128]{2,1,0:T(8,128)S(1)} %get-tuple-element.18, bf16[2,256,128]{2,1,0:T(8,128)(2,1)S(1)} %collective-permute-done.14), kind=kLoop, calls=%fused_computation.1 | loop fusion | flops 458752 | bytes 786432 | tf_op jit(solution)/shard_map/convert_element_type | solution.py:236
  (4 shorter events, 0.0 us)
Async XLA Ops:
  0.6 25.0 %copy-start = (bf16[2,256,128]{2,1,0:T(8,128)(2,1)S(1)}, bf16[2,256,128]{2,1,0:T(8,128)(2,1)}, u32[]{:S(2)}) copy-start(bf16[2,256,128]{2,1,0:T(8,128)(2,1)} %refs_6_.1) | copy-start | bytes 393220
  0.6 25.0 %copy-start.1 = (f32[1024]{0:T(1024)S(1)}, f32[1024]{0:T(1024)}, u32[]{:S(2)}) copy-start(f32[1024]{0:T(1024)} %refs_4_.1) | copy-start | bytes 12292
  0.7 9.8 %collective-permute-start.2 = (bf16[2,256,128]{2,1,0:T(8,128)(2,1)}, bf16[2,256,128]{2,1,0:T(8,128)(2,1)S(1)}, u32[]{:S(2)}, u32[]{:S(2)}) collective-permute-start(bf16[2,256,128]{2,1,0:T(8,128)(2,1)} %refs_6_.1), channel_id=1, source_target_pairs={{0,6},{1,7},{2,4},{3,5},{4,2},{5,3},{6,0},{7,1},{8,14},{9,15},{10,... | collective-permute-start | bytes 393224 | tf_op jit(solution)/shard_map/ppermute | solution.py:169
  5.8 11.3 %collective-permute-start.1 = (bf16[2,256,128]{2,1,0:T(8,128)(2,1)}, bf16[2,256,128]{2,1,0:T(8,128)(2,1)S(1)}, u32[]{:S(2)}, u32[]{:S(2)}) collective-permute-start(bf16[2,256,128]{2,1,0:T(8,128)(2,1)} %refs_6_.1), channel_id=1, source_target_pairs={{0,4},{1,5},{2,6},{3,7},{4,0},{5,1},{6,2},{7,3},{8,12},{9,13},{10,... | collective-permute-start | bytes 393224 | tf_op jit(solution)/shard_map/ppermute | solution.py:169
  5.8 12.8 %collective-permute-start = (bf16[2,256,128]{2,1,0:T(8,128)(2,1)}, bf16[2,256,128]{2,1,0:T(8,128)(2,1)S(1)}, u32[]{:S(2)}, u32[]{:S(2)}) collective-permute-start(bf16[2,256,128]{2,1,0:T(8,128)(2,1)} %refs_6_.1), channel_id=1, source_target_pairs={{0,2},{1,3},{2,0},{3,1},{4,6},{5,7},{6,4},{7,5},{8,10},{9,11},{10,... | collective-permute-start | bytes 393224 | tf_op jit(solution)/shard_map/ppermute | solution.py:169
  6.4 13.7 %collective-permute-start.3 = (bf16[2,256,128]{2,1,0:T(8,128)(2,1)}, bf16[2,256,128]{2,1,0:T(8,128)(2,1)S(1)}, u32[]{:S(2)}, u32[]{:S(2)}) collective-permute-start(bf16[2,256,128]{2,1,0:T(8,128)(2,1)} %refs_6_.1), channel_id=1, source_target_pairs={{0,1},{1,0},{2,3},{3,2},{4,5},{5,4},{6,7},{7,6},{8,9},{9,8},{10,11... | collective-permute-start | bytes 393224 | tf_op jit(solution)/shard_map/ppermute | solution.py:172
  6.4 19.3 %copy-start.4 = (s32[2]{0:T(128)S(1)}, s32[2]{0:T(128)}, u32[]{:S(2)}) copy-start(s32[2]{0:T(128)} %refs_2_.1) | copy-start | bytes 28
  6.4 19.3 %copy-start.5 = (f32[128]{0:T(128)S(1)}, f32[128]{0:T(128)}, u32[]{:S(2)}) copy-start(f32[128]{0:T(128)} %refs_3_.1) | copy-start | bytes 1540
  7.6 18.1 %copy-start.2 = (s32[2,2]{1,0:T(2,128)S(1)}, s32[2,2]{1,0:T(2,128)}, u32[]{:S(2)}) copy-start(s32[2,2]{1,0:T(2,128)} %refs_1_.1) | copy-start | bytes 52
  7.6 18.1 %copy-start.3 = (s32[2]{0:T(128)S(1)}, s32[2]{0:T(128)}, u32[]{:S(2)}) copy-start(s32[2]{0:T(128)} %refs_0_.1) | copy-start | bytes 28
  7.6 14.0 %collective-permute-start.9 = (bf16[2,256,256]{2,1,0:T(8,128)(2,1)S(1)}, bf16[2,256,256]{2,1,0:T(8,128)(2,1)S(1)}, u32[]{:S(2)}, u32[]{:S(2)}) collective-permute-start(bf16[2,256,256]{2,1,0:T(8,128)(2,1)S(1)} %reshape.14.refs_14_), channel_id=1, source_target_pairs={{0,24},{8,16},{16,8},{24,0},{1,25},{9,17},{17,9},{25,1},{2,26},{10... | collective-permute-start | bytes 786440 | tf_op jit(solution)/shard_map/ppermute | solution.py:166
  10.4 9.7 %collective-permute-start.6 = (bf16[2,256,128]{2,1,0:T(8,128)(2,1)S(1)}, bf16[2,256,128]{2,1,0:T(8,128)(2,1)S(1)}, u32[]{:S(2)}, u32[]{:S(2)}) collective-permute-start(bf16[2,256,128]{2,1,0:T(8,128)(2,1)S(1)} %collective-permute-done.2.refs_9_), channel_id=1, source_target_pairs={{0,1},{1,0},{2,3},{3,2},{4,5},{5,4},{6,7},{7,6},{8,9},{9,8},{10,11... | collective-permute-start | bytes 393224 | tf_op jit(solution)/shard_map/ppermute | solution.py:172
  17.1 7.4 %collective-permute-start.8 = (bf16[2,256,256]{2,1,0:T(8,128)(2,1)S(1)}, bf16[2,256,256]{2,1,0:T(8,128)(2,1)S(1)}, u32[]{:S(2)}, u32[]{:S(2)}) collective-permute-start(bf16[2,256,256]{2,1,0:T(8,128)(2,1)S(1)} %reshape.14.refs_14_), channel_id=1, source_target_pairs={{0,16},{8,24},{16,0},{24,8},{1,17},{9,25},{17,1},{25,9},{2,18},{10... | collective-permute-start | bytes 786440 | tf_op jit(solution)/shard_map/ppermute | solution.py:166
  18.6 7.1 %collective-permute-start.7 = (bf16[2,256,256]{2,1,0:T(8,128)(2,1)S(1)}, bf16[2,256,256]{2,1,0:T(8,128)(2,1)S(1)}, u32[]{:S(2)}, u32[]{:S(2)}) collective-permute-start(bf16[2,256,256]{2,1,0:T(8,128)(2,1)S(1)} %reshape.14.refs_14_), channel_id=1, source_target_pairs={{0,8},{8,0},{16,24},{24,16},{1,9},{9,1},{17,25},{25,17},{2,10},{10... | collective-permute-start | bytes 786440 | tf_op jit(solution)/shard_map/ppermute | solution.py:166
  20.1 1.3 %collective-permute-start.5 = (bf16[2,256,128]{2,1,0:T(8,128)(2,1)S(1)}, bf16[2,256,128]{2,1,0:T(8,128)(2,1)S(1)}, u32[]{:S(2)}, u32[]{:S(2)}) collective-permute-start(bf16[2,256,128]{2,1,0:T(8,128)(2,1)S(1)} %collective-permute-done.1.refs_8_), channel_id=1, source_target_pairs={{0,1},{1,0},{2,3},{3,2},{4,5},{5,4},{6,7},{7,6},{8,9},{9,8},{10,11... | collective-permute-start | bytes 393224 | tf_op jit(solution)/shard_map/ppermute | solution.py:172
  20.1 1.5 %collective-permute-start.4 = (bf16[2,256,128]{2,1,0:T(8,128)(2,1)S(1)}, bf16[2,256,128]{2,1,0:T(8,128)(2,1)S(1)}, u32[]{:S(2)}, u32[]{:S(2)}) collective-permute-start(bf16[2,256,128]{2,1,0:T(8,128)(2,1)S(1)} %collective-permute-done.refs_7_), channel_id=1, source_target_pairs={{0,1},{1,0},{2,3},{3,2},{4,5},{5,4},{6,7},{7,6},{8,9},{9,8},{10,11... | collective-permute-start | bytes 393224 | tf_op jit(solution)/shard_map/ppermute | solution.py:172
  29.1 3.6 %collective-permute-start.13 = (bf16[4,2,256,128]{3,2,1,0:T(8,128)(2,1)S(1)}, bf16[4,2,256,128]{3,2,1,0:T(8,128)(2,1)S(1)}, u32[]{:S(2)}, u32[]{:S(2)}) collective-permute-start(bf16[4,2,256,128]{3,2,1,0:T(8,128)(2,1)S(1)} %get-tuple-element.17), channel_id=1, source_target_pairs={{0,1},{1,0},{2,3},{3,2},{4,5},{5,4},{6,7},{7,6},{8,9},{9,8},{10,11... | collective-permute-start | bytes 1572872 | tf_op jit(solution)/shard_map/ppermute | solution.py:172
  29.2 9.2 %collective-permute-start.10 = (bf16[2,256,256]{2,1,0:T(8,128)(2,1)S(1)}, bf16[2,256,256]{2,1,0:T(8,128)(2,1)S(1)}, u32[]{:S(2)}, u32[]{:S(2)}) collective-permute-start(bf16[2,256,256]{2,1,0:T(8,128)(2,1)S(1)} %get-tuple-element.13), channel_id=1, source_target_pairs={{0,8},{8,0},{16,24},{24,16},{1,9},{9,1},{17,25},{25,17},{2,10},{10... | collective-permute-start | bytes 786440 | tf_op jit(solution)/shard_map/ppermute | solution.py:166
  30.8 14.0 %collective-permute-start.11 = (bf16[2,256,256]{2,1,0:T(8,128)(2,1)S(1)}, bf16[2,256,256]{2,1,0:T(8,128)(2,1)S(1)}, u32[]{:S(2)}, u32[]{:S(2)}) collective-permute-start(bf16[2,256,256]{2,1,0:T(8,128)(2,1)S(1)} %get-tuple-element.14), channel_id=1, source_target_pairs={{0,16},{8,24},{16,0},{24,8},{1,17},{9,25},{17,1},{25,9},{2,18},{10... | collective-permute-start | bytes 786440 | tf_op jit(solution)/shard_map/ppermute | solution.py:166
  31.3 13.5 %collective-permute-start.12 = (bf16[2,256,256]{2,1,0:T(8,128)(2,1)S(1)}, bf16[2,256,256]{2,1,0:T(8,128)(2,1)S(1)}, u32[]{:S(2)}, u32[]{:S(2)}) collective-permute-start(bf16[2,256,256]{2,1,0:T(8,128)(2,1)S(1)} %get-tuple-element.15), channel_id=1, source_target_pairs={{0,24},{8,16},{16,8},{24,0},{1,25},{9,17},{17,9},{25,1},{2,26},{10... | collective-permute-start | bytes 786440 | tf_op jit(solution)/shard_map/ppermute | solution.py:166
  32.9 12.8 %collective-permute-start.14 = (bf16[2,256,128]{2,1,0:T(8,128)(2,1)S(1)}, bf16[2,256,128]{2,1,0:T(8,128)(2,1)S(1)}, u32[]{:S(2)}, u32[]{:S(2)}) collective-permute-start(bf16[2,256,128]{2,1,0:T(8,128)(2,1)S(1)} %get-tuple-element.19), channel_id=1, source_target_pairs={{0,2},{1,3},{2,0},{3,1},{4,6},{5,7},{6,4},{7,5},{8,10},{9,11},{10,... | collective-permute-start | bytes 393224 | tf_op jit(solution)/shard_map/ppermute | solution.py:169
  33.0 12.7 %collective-permute-start.15 = (bf16[2,256,128]{2,1,0:T(8,128)(2,1)S(1)}, bf16[2,256,128]{2,1,0:T(8,128)(2,1)S(1)}, u32[]{:S(2)}, u32[]{:S(2)}) collective-permute-start(bf16[2,256,128]{2,1,0:T(8,128)(2,1)S(1)} %get-tuple-element.20), channel_id=1, source_target_pairs={{0,4},{1,5},{2,6},{3,7},{4,0},{5,1},{6,2},{7,3},{8,12},{9,13},{10,... | collective-permute-start | bytes 393224 | tf_op jit(solution)/shard_map/ppermute | solution.py:169
  38.4 7.3 %collective-permute-start.16 = (bf16[2,256,128]{2,1,0:T(8,128)(2,1)S(1)}, bf16[2,256,128]{2,1,0:T(8,128)(2,1)S(1)}, u32[]{:S(2)}, u32[]{:S(2)}) collective-permute-start(bf16[2,256,128]{2,1,0:T(8,128)(2,1)S(1)} %get-tuple-element.21), channel_id=1, source_target_pairs={{0,6},{1,7},{2,4},{3,5},{4,2},{5,3},{6,0},{7,1},{8,14},{9,15},{10,... | collective-permute-start | bytes 393224 | tf_op jit(solution)/shard_map/ppermute | solution.py:169

commit v2 on v1

--- a/solution.py
+++ b/solution.py
@@ -116,21 +116,22 @@
             triples = jnp.dot(amp_full[pair], ints_full[slot], preferred_element_type=jnp.float32)
             scaled.append((triples / (occ + base)).astype(jnp.bfloat16))
 
+    low = core_pos == 0
     for step in range(n_chip):
-        base_d = (chip_pos ^ step) * (CORES * sub_d)
-        for core, out in ((core_pos, grad_mine), (1 - core_pos, grad_other)):
-            at = pl.multiple_of(base_d + core * sub_d, sub_d)
-            for pair in range(n_pair):
-                total = None
-                for slot in range(n_i):
-                    part = lax.dot_general(
-                        scaled[slot * n_pair + pair],
-                        ints_full[slot, pl.ds(at, sub_d), :],
-                        (((1,), (1,)), ((), ())),
-                        preferred_element_type=jnp.float32,
-                    )
-                    total = part if total is None else total + part
-                out[step, pair] = total.astype(out.dtype)
+        at = pl.multiple_of((chip_pos ^ step) * (CORES * sub_d), CORES * sub_d)
+        for pair in range(n_pair):
+            total = None
+            for slot in range(n_i):
+                part = lax.dot_general(
+                    scaled[slot * n_pair + pair],
+                    ints_full[slot, pl.ds(at, CORES * sub_d), :],
+                    (((1,), (1,)), ((), ())),
+                    preferred_element_type=jnp.float32,
+                )
+                total = part if total is None else total + part
+            first, second = total[:, :sub_d], total[:, sub_d:]
+            grad_mine[step, pair] = jnp.where(low, first, second).astype(grad_mine.dtype)
+            grad_other[step, pair] = jnp.where(low, second, first).astype(grad_other.dtype)
 
     for step in range(n_row):
         at = pl.multiple_of((row_pos ^ step) * block_d, block_d)
@@ -171,9 +172,11 @@
     def over_cores(value):
         return lax.ppermute(value, "col", [(k, k ^ 1) for k in range(n_col)])
 
-    ints_own = integrals.reshape(n_i, block_d, tile)
     mine = [amplitudes] + [over_chips(amplitudes, step) for step in range(1, n_chip)]
-    ints = [ints_own] + [over_row(ints_own, step) for step in range(1, n_row)]
+    near = [over_row(integrals, 1), over_row(integrals, 2)]
+    half = n_i // 2
+    far = jnp.concatenate([over_row(near[0][:half], 2), over_row(near[1][half:], 1)])
+    ints = [value.reshape(n_i, block_d, tile) for value in [integrals] + near + [far]]
     other = [over_cores(value) for value in mine]
 
     vmem = pl.BlockSpec(memory_space=pltpu.VMEM)
@@ -248,8 +251,9 @@
             and sub_d % LANES == 0
             and block_c % LANES == 0
             and block_d % LANES == 0
-            and n_row & (n_row - 1) == 0
+            and n_row == 4
             and n_col & (n_col - 1) == 0
+            and args[6].shape[0] % 2 == 0
         )
         if whole_tiles:
             return exchanged(n_row, n_col, *args)

time: 46.5 us -> 42.2 us (0.908)
  waiting for transfers between devices: 18.5 us -> 12.4 us
  starting transfers between devices: 20.8 us -> 22.4 us
  Pallas kernels: 3.52 us -> 2.95 us
    ppermute x6 -> x7, waiting for transfers between devices: 10.7 us -> 5.64 us  [over_row(): return lax.ppermute(value, 'row', [(k, k ^ mask) for k in range(n_row)])]
    ppermute x6 -> x7, starting transfers between devices: 9.22 us -> 11.4 us  [over_row(): return lax.ppermute(value, 'row', [(k, k ^ mask) for k in range(n_row)])]
    ppermute x6, starting transfers between devices: 11 us -> 9.96 us  [over_chips(): lax.ppermute(value, 'col', [(k, k ^ CORES * mask) for k in range(n_col)])]
    ppermute x5, waiting for transfers between devices: 1.03 us -> 0.1 us  [over_cores(): return lax.ppermute(value, 'col', [(k, k ^ 1) for k in range(n_col)])]
    pallas_call x1, Pallas kernels: 3.43 us -> 2.86 us  [exchanged(): pl.pallas_call(functools.partial(products, n_row, n_chip), out_shape=[jax...]
    unnamed x12 -> x14, local copies, waits for them, and re-layouts: 0.03 us -> 0.56 us
    reshape x1 -> x4, local copies, waits for them, and re-layouts: 1.15 us -> 0.68 us  [exchanged(): value.reshape(n_i, block_d, tile)]
  transfers between devices with their start and end apart: 17 -> 18, of which waited for: 8 -> 6; matrix products, arithmetic and copies ran while one was open for 4% -> 5% of each run, Pallas kernels for 0% -> 0%
where the time goes in v2:
time: 42.2 us; the launch traced here: 42 us
  starting transfers between devices  22.4 us (53%)
  waiting for transfers between devices  12.4 us (29%)
  Pallas kernels  2.95 us (7%)
  local copies, waits for them, and re-layouts  2.19 us (5%)
  other arithmetic  1.21 us (3%)
  between operations  0.8 us (2%)
    ppermute x7, starting transfers between devices, over_row(): return lax.ppermute(value, 'row', [(k, k ^ mask) for k in range(n_row)])  11.4 us
    ppermute x6, starting transfers between devices, over_chips(): lax.ppermute(value, 'col', [(k, k ^ CORES * mask) for k in range(n_col)])  9.96 us
    ppermute x6, waiting for transfers between devices, over_chips(): lax.ppermute(value, 'col', [(k, k ^ CORES * mask) for k in range(n_col)])  6.7 us
    ppermute x7, waiting for transfers between devices, over_row(): return lax.ppermute(value, 'row', [(k, k ^ mask) for k in range(n_row)])  5.64 us
    pallas_call x1, Pallas kernels, exchanged(): pl.pallas_call(functools.partial(products, n_row, n_chip), out_shape=[jax...  2.86 us
    ppermute x5, starting transfers between devices, over_cores(): return lax.ppermute(value, 'col', [(k, k ^ 1) for k in range(n_col)])  1.09 us
  transfers between devices with their start and end apart: 18, of which 6 were waited for; matrix products, arithmetic and copies ran while one was open for 5% of the time, Pallas kernels for 0%

profile of v2, /device:TPU:0, one launch (start us, length us, event | category | flops | bytes accessed | tf_op | source)
XLA Modules:
  0.0 42.0 jit_solution(3943267775748484957)
XLA Ops:
  0.6 3.0 %collective-permute-start.8 = (bf16[2,256,2,128]{3,2,1,0:T(2,128)(2,1)}, bf16[2,256,2,128]{3,2,1,0:T(2,128)(2,1)S(1)}, u32[]{:S(2)}, u32[]{:S(2)}) collective-permute-start(bf16[2,256,2,128]{3,2,1,0:T(2,128)(2,1)} %param.13), channel_id=1, source_target_pairs={{0,16},{8,24},{16,0},{24,8},{1,17},{9,25},{17,1},{25,9},{2,18},{10... | collective-permute-start | bytes 786440 | tf_op jit(solution)/shard_map/ppermute | solution.py:167
  3.7 1.5 %collective-permute-start.7 = (bf16[2,256,2,128]{3,2,1,0:T(2,128)(2,1)}, bf16[2,256,2,128]{3,2,1,0:T(2,128)(2,1)S(1)}, u32[]{:S(2)}, u32[]{:S(2)}) collective-permute-start(bf16[2,256,2,128]{3,2,1,0:T(2,128)(2,1)} %param.13), channel_id=1, source_target_pairs={{0,8},{8,0},{16,24},{24,16},{1,9},{9,1},{17,25},{25,17},{2,10},{10... | collective-permute-start | bytes 786440 | tf_op jit(solution)/shard_map/ppermute | solution.py:167
  5.2 3.6 %collective-permute-start.2 = (bf16[2,256,128]{2,1,0:T(8,128)(2,1)}, bf16[2,256,128]{2,1,0:T(8,128)(2,1)S(1)}, u32[]{:S(2)}, u32[]{:S(2)}) collective-permute-start(bf16[2,256,128]{2,1,0:T(8,128)(2,1)} %refs_6_.1), channel_id=1, source_target_pairs={{0,6},{1,7},{2,4},{3,5},{4,2},{5,3},{6,0},{7,1},{8,14},{9,15},{10,... | collective-permute-start | bytes 393224 | tf_op jit(solution)/shard_map/ppermute | solution.py:170
  8.8 0.0 collective-permute-start.1
  8.8 0.8 %collective-permute-start = (bf16[2,256,128]{2,1,0:T(8,128)(2,1)}, bf16[2,256,128]{2,1,0:T(8,128)(2,1)S(1)}, u32[]{:S(2)}, u32[]{:S(2)}) collective-permute-start(bf16[2,256,128]{2,1,0:T(8,128)(2,1)} %refs_6_.1), channel_id=1, source_target_pairs={{0,2},{1,3},{2,0},{3,1},{4,6},{5,7},{6,4},{7,5},{8,10},{9,11},{10,... | collective-permute-start | bytes 393224 | tf_op jit(solution)/shard_map/ppermute | solution.py:170
  9.6 0.6 %collective-permute-done.8 = bf16[2,256,2,128]{3,2,1,0:T(2,128)(2,1)S(1)} collective-permute-done((bf16[2,256,2,128]{3,2,1,0:T(2,128)(2,1)}, bf16[2,256,2,128]{3,2,1,0:T(2,128)(2,1)S(1)}, u32[]{:S(2)}, u32[]{:S(2)}) %collective-permute-start.8) | collective-permute-done | bytes 262176 | tf_op jit(solution)/shard_map/ppermute | solution.py:167
  10.2 0.1 slice.9
  10.3 0.0 copy-start
  10.3 1.8 %collective-permute-start.10 = (bf16[1,256,2,128]{3,2,1,0:T(2,128)(2,1)S(1)}, bf16[1,256,2,128]{3,2,1,0:T(2,128)(2,1)S(1)}, u32[]{:S(2)}, u32[]{:S(2)}) collective-permute-start(bf16[1,256,2,128]{3,2,1,0:T(2,128)(2,1)S(1)} %slice.9), channel_id=1, source_target_pairs={{0,8},{8,0},{16,24},{24,16},{1,9},{9,1},{17,25},{25,17},{2,10},{10... | collective-permute-start | bytes 393224 | tf_op jit(solution)/shard_map/ppermute | solution.py:167
  12.1 0.0 collective-permute-done.7
  12.1 0.1 slice.8
  12.2 1.6 %collective-permute-start.9 = (bf16[1,256,2,128]{3,2,1,0:T(2,128)(2,1)S(1)}, bf16[1,256,2,128]{3,2,1,0:T(2,128)(2,1)S(1)}, u32[]{:S(2)}, u32[]{:S(2)}) collective-permute-start(bf16[1,256,2,128]{3,2,1,0:T(2,128)(2,1)S(1)} %slice.8), channel_id=1, source_target_pairs={{0,16},{8,24},{16,0},{24,8},{1,17},{9,25},{17,1},{25,9},{2,18},{10... | collective-permute-start | bytes 393224 | tf_op jit(solution)/shard_map/ppermute | solution.py:167
  13.8 0.0 collective-permute-done.2.refs_9_
  13.8 0.0 collective-permute-start.3
  13.8 5.7 %collective-permute-done.1.refs_8_ = bf16[2,256,128]{2,1,0:T(8,128)(2,1)S(1)} collective-permute-done((bf16[2,256,128]{2,1,0:T(8,128)(2,1)}, bf16[2,256,128]{2,1,0:T(8,128)(2,1)S(1)}, u32[]{:S(2)}, u32[]{:S(2)}) %collective-permute-start.1) | collective-permute-done | bytes 131104 | tf_op jit(solution)/shard_map/ppermute | solution.py:170
  19.5 0.0 collective-permute-done.refs_7_
  19.5 0.5 %collective-permute-start.5 = (bf16[2,256,128]{2,1,0:T(8,128)(2,1)S(1)}, bf16[2,256,128]{2,1,0:T(8,128)(2,1)S(1)}, u32[]{:S(2)}, u32[]{:S(2)}) collective-permute-start(bf16[2,256,128]{2,1,0:T(8,128)(2,1)S(1)} %collective-permute-done.1.refs_8_), channel_id=1, source_target_pairs={{0,1},{1,0},{2,3},{3,2},{4,5},{5,4},{6,7},{7,6},{8,9},{9,8},{10,11... | collective-permute-start | bytes 393224 | tf_op jit(solution)/shard_map/ppermute | solution.py:173
  20.0 0.0 collective-permute-done.10
  20.0 0.1 collective-permute-start.4
  20.1 0.2 reshape.23.refs_14_
  20.3 0.2 reshape.25.refs_16_
  20.4 0.2 reshape.24.refs_15_
  20.6 0.0 collective-permute-done.9
  20.6 0.4 pad_maximum_fusion
  21.0 0.0 copy-start.1
  21.0 0.0 copy-start.4
  21.0 0.0 copy-start.5
  21.0 0.2 reshape.26.refs_17_
  21.2 0.0 copy-start.2
  21.2 0.0 copy-start.3
  21.3 0.1 collective-permute-done.4.refs_11_
  21.4 0.3 copy-done.1
  21.7 0.2 copy-done.2
  21.9 2.9 %products.1 = (f32[2,256,256]{2,1,0:T(8,128)S(1)}, bf16[2,256,256]{2,1,0:T(8,128)(2,1)S(1)}, bf16[2,256,256]{2,1,0:T(8,128)(2,1)S(1)}, bf16[2,256,256]{2,1,0:T(8...) custom-call(s32[2]{0:T(128)S(1)} %copy-done.3, s32[2,2]{1,0:T(2,128)S(1)} %copy-done.2, ...), custom_call_target="tpu_custom_call" | custom-call | flops 1610612736 | bytes 8388608 | tf_op jit(solution)/shard_map/products/pallas_call | solution.py:186
  24.8 0.5 %collective-permute-start.14 = (bf16[4,2,256,128]{3,2,1,0:T(8,128)(2,1)S(1)}, bf16[4,2,256,128]{3,2,1,0:T(8,128)(2,1)S(1)}, u32[]{:S(2)}, u32[]{:S(2)}) collective-permute-start(bf16[4,2,256,128]{3,2,1,0:T(8,128)(2,1)S(1)} %get-tuple-element.17), channel_id=1, source_target_pairs={{0,1},{1,0},{2,3},{3,2},{4,5},{5,4},{6,7},{7,6},{8,9},{9,8},{10,11... | collective-permute-start | bytes 1572872 | tf_op jit(solution)/shard_map/ppermute | solution.py:173
  25.3 0.5 %collective-permute-start.11 = (bf16[2,256,256]{2,1,0:T(8,128)(2,1)S(1)}, bf16[2,256,256]{2,1,0:T(8,128)(2,1)S(1)}, u32[]{:S(2)}, u32[]{:S(2)}) collective-permute-start(bf16[2,256,256]{2,1,0:T(8,128)(2,1)S(1)} %get-tuple-element.13), channel_id=1, source_target_pairs={{0,8},{8,0},{16,24},{24,16},{1,9},{9,1},{17,25},{25,17},{2,10},{10... | collective-permute-start | bytes 786440 | tf_op jit(solution)/shard_map/ppermute | solution.py:167
  25.8 0.5 %collective-permute-start.12 = (bf16[2,256,256]{2,1,0:T(8,128)(2,1)S(1)}, bf16[2,256,256]{2,1,0:T(8,128)(2,1)S(1)}, u32[]{:S(2)}, u32[]{:S(2)}) collective-permute-start(bf16[2,256,256]{2,1,0:T(8,128)(2,1)S(1)} %get-tuple-element.14), channel_id=1, source_target_pairs={{0,16},{8,24},{16,0},{24,8},{1,17},{9,25},{17,1},{25,9},{2,18},{10... | collective-permute-start | bytes 786440 | tf_op jit(solution)/shard_map/ppermute | solution.py:167
  26.3 2.4 %collective-permute-start.13 = (bf16[2,256,256]{2,1,0:T(8,128)(2,1)S(1)}, bf16[2,256,256]{2,1,0:T(8,128)(2,1)S(1)}, u32[]{:S(2)}, u32[]{:S(2)}) collective-permute-start(bf16[2,256,256]{2,1,0:T(8,128)(2,1)S(1)} %get-tuple-element.15), channel_id=1, source_target_pairs={{0,24},{8,16},{16,8},{24,0},{1,25},{9,17},{17,9},{25,1},{2,26},{10... | collective-permute-start | bytes 786440 | tf_op jit(solution)/shard_map/ppermute | solution.py:167
  28.8 0.1 core_sums.1
  28.9 0.1 collective-permute-start.15
  28.9 3.0 %collective-permute-start.16 = (bf16[2,256,128]{2,1,0:T(8,128)(2,1)S(1)}, bf16[2,256,128]{2,1,0:T(8,128)(2,1)S(1)}, u32[]{:S(2)}, u32[]{:S(2)}) collective-permute-start(bf16[2,256,128]{2,1,0:T(8,128)(2,1)S(1)} %get-tuple-element.20), channel_id=1, source_target_pairs={{0,4},{1,5},{2,6},{3,7},{4,0},{5,1},{6,2},{7,3},{8,12},{9,13},{10,... | collective-permute-start | bytes 393224 | tf_op jit(solution)/shard_map/ppermute | solution.py:170
  32.0 2.5 %collective-permute-done.11 = bf16[2,256,256]{2,1,0:T(8,128)(2,1)S(1)} collective-permute-done((bf16[2,256,256]{2,1,0:T(8,128)(2,1)S(1)}, bf16[2,256,256]{2,1,0:T(8,128)(2,1)S(1)}, u32[]{:S(2)}, u32[]{:S(2)}) %collective-permute-start.11) | collective-permute-done | bytes 262176 | tf_op jit(solution)/shard_map/ppermute | solution.py:167
  34.4 2.5 %collective-permute-start.17 = (bf16[2,256,128]{2,1,0:T(8,128)(2,1)S(1)}, bf16[2,256,128]{2,1,0:T(8,128)(2,1)S(1)}, u32[]{:S(2)}, u32[]{:S(2)}) collective-permute-start(bf16[2,256,128]{2,1,0:T(8,128)(2,1)S(1)} %get-tuple-element.21), channel_id=1, source_target_pairs={{0,6},{1,7},{2,4},{3,5},{4,2},{5,3},{6,0},{7,1},{8,14},{9,15},{10,... | collective-permute-start | bytes 393224 | tf_op jit(solution)/shard_map/ppermute | solution.py:170
  36.9 2.5 %collective-permute-done.12 = bf16[2,256,256]{2,1,0:T(8,128)(2,1)S(1)} collective-permute-done((bf16[2,256,256]{2,1,0:T(8,128)(2,1)S(1)}, bf16[2,256,256]{2,1,0:T(8,128)(2,1)S(1)}, u32[]{:S(2)}, u32[]{:S(2)}) %collective-permute-start.12) | collective-permute-done | bytes 262176 | tf_op jit(solution)/shard_map/ppermute | solution.py:167
  39.4 0.1 add_convert_fusion
  39.6 0.8 %reshape.27 = bf16[2,256,2,128]{3,2,1,0:T(2,128)(2,1)} reshape(bf16[2,256,256]{2,1,0:T(8,128)(2,1)S(1)} %add_convert_fusion) | data formatting | bytes 524288 | tf_op jit(solution)/shard_map/reshape | solution.py:238
  40.3 1.0 %collective-permute-done.17 = bf16[2,256,128]{2,1,0:T(8,128)(2,1)S(1)} collective-permute-done((bf16[2,256,128]{2,1,0:T(8,128)(2,1)S(1)}, bf16[2,256,128]{2,1,0:T(8,128)(2,1)S(1)}, u32[]{:S(2)}, u32[]{:S(2)}) %collective-permute-start.17) | collective-permute-done | bytes 131104 | tf_op jit(solution)/shard_map/ppermute | solution.py:170
  41.3 0.7 %add_convert_fusion.1 = bf16[2,256,128]{2,1,0:T(8,128)(2,1)} fusion(bf16[2,256,128]{2,1,0:T(8,128)(2,1)S(1)} %collective-permute-done.17, bf16[2,256,128]{2,1,0:T(8,128)(2,1)S(1)} %collective-permute-done.16, f32[2,256,128]{2,1,0:T(8,128)S(1)} %get-tuple-element.18, bf16[2,256,128]{2,1,0:T(8,128)(2,1)S(1)} %collective-permute-done.15), kind=kLoop, calls=%fused_computation.2 | loop fusion | flops 458752 | bytes 786432 | tf_op jit(solution)/shard_map/convert_element_type | solution.py:239
  (14 shorter events, 0.0 us)
Async XLA Ops:
  0.6 19.5 %copy-start.6 = (bf16[2,256,2,128]{3,2,1,0:T(2,128)(2,1)S(1)}, bf16[2,256,2,128]{3,2,1,0:T(2,128)(2,1)}, u32[]{:S(2)}) copy-start(bf16[2,256,2,128]{3,2,1,0:T(2,128)(2,1)} %param.13) | copy-start | bytes 786436
  0.6 9.5 %collective-permute-start.8 = (bf16[2,256,2,128]{3,2,1,0:T(2,128)(2,1)}, bf16[2,256,2,128]{3,2,1,0:T(2,128)(2,1)S(1)}, u32[]{:S(2)}, u32[]{:S(2)}) collective-permute-start(bf16[2,256,2,128]{3,2,1,0:T(2,128)(2,1)} %param.13), channel_id=1, source_target_pairs={{0,16},{8,24},{16,0},{24,8},{1,17},{9,25},{17,1},{25,9},{2,18},{10... | collective-permute-start | bytes 786440 | tf_op jit(solution)/shard_map/ppermute | solution.py:167
  3.7 8.4 %collective-permute-start.7 = (bf16[2,256,2,128]{3,2,1,0:T(2,128)(2,1)}, bf16[2,256,2,128]{3,2,1,0:T(2,128)(2,1)S(1)}, u32[]{:S(2)}, u32[]{:S(2)}) collective-permute-start(bf16[2,256,2,128]{3,2,1,0:T(2,128)(2,1)} %param.13), channel_id=1, source_target_pairs={{0,8},{8,0},{16,24},{24,16},{1,9},{9,1},{17,25},{25,17},{2,10},{10... | collective-permute-start | bytes 786440 | tf_op jit(solution)/shard_map/ppermute | solution.py:167
  5.2 8.6 %collective-permute-start.2 = (bf16[2,256,128]{2,1,0:T(8,128)(2,1)}, bf16[2,256,128]{2,1,0:T(8,128)(2,1)S(1)}, u32[]{:S(2)}, u32[]{:S(2)}) collective-permute-start(bf16[2,256,128]{2,1,0:T(8,128)(2,1)} %refs_6_.1), channel_id=1, source_target_pairs={{0,6},{1,7},{2,4},{3,5},{4,2},{5,3},{6,0},{7,1},{8,14},{9,15},{10,... | collective-permute-start | bytes 393224 | tf_op jit(solution)/shard_map/ppermute | solution.py:170
  8.8 10.7 %collective-permute-start.1 = (bf16[2,256,128]{2,1,0:T(8,128)(2,1)}, bf16[2,256,128]{2,1,0:T(8,128)(2,1)S(1)}, u32[]{:S(2)}, u32[]{:S(2)}) collective-permute-start(bf16[2,256,128]{2,1,0:T(8,128)(2,1)} %refs_6_.1), channel_id=1, source_target_pairs={{0,4},{1,5},{2,6},{3,7},{4,0},{5,1},{6,2},{7,3},{8,12},{9,13},{10,... | collective-permute-start | bytes 393224 | tf_op jit(solution)/shard_map/ppermute | solution.py:170
  8.8 10.7 %collective-permute-start = (bf16[2,256,128]{2,1,0:T(8,128)(2,1)}, bf16[2,256,128]{2,1,0:T(8,128)(2,1)S(1)}, u32[]{:S(2)}, u32[]{:S(2)}) collective-permute-start(bf16[2,256,128]{2,1,0:T(8,128)(2,1)} %refs_6_.1), channel_id=1, source_target_pairs={{0,2},{1,3},{2,0},{3,1},{4,6},{5,7},{6,4},{7,5},{8,10},{9,11},{10,... | collective-permute-start | bytes 393224 | tf_op jit(solution)/shard_map/ppermute | solution.py:170
  10.3 3.5 %copy-start = (bf16[2,256,128]{2,1,0:T(8,128)(2,1)S(1)}, bf16[2,256,128]{2,1,0:T(8,128)(2,1)}, u32[]{:S(2)}) copy-start(bf16[2,256,128]{2,1,0:T(8,128)(2,1)} %refs_6_.1) | copy-start | bytes 393220
  10.3 9.7 %collective-permute-start.10 = (bf16[1,256,2,128]{3,2,1,0:T(2,128)(2,1)S(1)}, bf16[1,256,2,128]{3,2,1,0:T(2,128)(2,1)S(1)}, u32[]{:S(2)}, u32[]{:S(2)}) collective-permute-start(bf16[1,256,2,128]{3,2,1,0:T(2,128)(2,1)S(1)} %slice.9), channel_id=1, source_target_pairs={{0,8},{8,0},{16,24},{24,16},{1,9},{9,1},{17,25},{25,17},{2,10},{10... | collective-permute-start | bytes 393224 | tf_op jit(solution)/shard_map/ppermute | solution.py:167
  12.2 8.4 %collective-permute-start.9 = (bf16[1,256,2,128]{3,2,1,0:T(2,128)(2,1)S(1)}, bf16[1,256,2,128]{3,2,1,0:T(2,128)(2,1)S(1)}, u32[]{:S(2)}, u32[]{:S(2)}) collective-permute-start(bf16[1,256,2,128]{3,2,1,0:T(2,128)(2,1)S(1)} %slice.8), channel_id=1, source_target_pairs={{0,16},{8,24},{16,0},{24,8},{1,17},{9,25},{17,1},{25,9},{2,18},{10... | collective-permute-start | bytes 393224 | tf_op jit(solution)/shard_map/ppermute | solution.py:167
  13.8 7.5 %collective-permute-start.3 = (bf16[2,256,128]{2,1,0:T(8,128)(2,1)S(1)}, bf16[2,256,128]{2,1,0:T(8,128)(2,1)S(1)}, u32[]{:S(2)}, u32[]{:S(2)}) collective-permute-start(bf16[2,256,128]{2,1,0:T(8,128)(2,1)S(1)} %copy-done), channel_id=1, source_target_pairs={{0,1},{1,0},{2,3},{3,2},{4,5},{5,4},{6,7},{7,6},{8,9},{9,8},{10,11... | collective-permute-start | bytes 393224 | tf_op jit(solution)/shard_map/ppermute | solution.py:173
  19.5 1.8 %collective-permute-start.6 = (bf16[2,256,128]{2,1,0:T(8,128)(2,1)S(1)}, bf16[2,256,128]{2,1,0:T(8,128)(2,1)S(1)}, u32[]{:S(2)}, u32[]{:S(2)}) collective-permute-start(bf16[2,256,128]{2,1,0:T(8,128)(2,1)S(1)} %collective-permute-done.2.refs_9_), channel_id=1, source_target_pairs={{0,1},{1,0},{2,3},{3,2},{4,5},{5,4},{6,7},{7,6},{8,9},{9,8},{10,11... | collective-permute-start | bytes 393224 | tf_op jit(solution)/shard_map/ppermute | solution.py:173
  19.5 1.8 %collective-permute-start.5 = (bf16[2,256,128]{2,1,0:T(8,128)(2,1)S(1)}, bf16[2,256,128]{2,1,0:T(8,128)(2,1)S(1)}, u32[]{:S(2)}, u32[]{:S(2)}) collective-permute-start(bf16[2,256,128]{2,1,0:T(8,128)(2,1)S(1)} %collective-permute-done.1.refs_8_), channel_id=1, source_target_pairs={{0,1},{1,0},{2,3},{3,2},{4,5},{5,4},{6,7},{7,6},{8,9},{9,8},{10,11... | collective-permute-start | bytes 393224 | tf_op jit(solution)/shard_map/ppermute | solution.py:173
  20.0 1.3 %collective-permute-start.4 = (bf16[2,256,128]{2,1,0:T(8,128)(2,1)S(1)}, bf16[2,256,128]{2,1,0:T(8,128)(2,1)S(1)}, u32[]{:S(2)}, u32[]{:S(2)}) collective-permute-start(bf16[2,256,128]{2,1,0:T(8,128)(2,1)S(1)} %collective-permute-done.refs_7_), channel_id=1, source_target_pairs={{0,1},{1,0},{2,3},{3,2},{4,5},{5,4},{6,7},{7,6},{8,9},{9,8},{10,11... | collective-permute-start | bytes 393224 | tf_op jit(solution)/shard_map/ppermute | solution.py:173
  21.0 0.7 %copy-start.1 = (f32[1024]{0:T(1024)S(1)}, f32[1024]{0:T(1024)}, u32[]{:S(2)}) copy-start(f32[1024]{0:T(1024)} %refs_4_.1) | copy-start | bytes 12292
  21.0 0.7 %copy-start.4 = (s32[2]{0:T(128)S(1)}, s32[2]{0:T(128)}, u32[]{:S(2)}) copy-start(s32[2]{0:T(128)} %refs_2_.1) | copy-start | bytes 28
  21.0 0.7 %copy-start.5 = (f32[128]{0:T(128)S(1)}, f32[128]{0:T(128)}, u32[]{:S(2)}) copy-start(f32[128]{0:T(128)} %refs_3_.1) | copy-start | bytes 1540
  21.2 0.7 %copy-start.2 = (s32[2,2]{1,0:T(2,128)S(1)}, s32[2,2]{1,0:T(2,128)}, u32[]{:S(2)}) copy-start(s32[2,2]{1,0:T(2,128)} %refs_1_.1) | copy-start | bytes 52
  21.2 0.7 %copy-start.3 = (s32[2]{0:T(128)S(1)}, s32[2]{0:T(128)}, u32[]{:S(2)}) copy-start(s32[2]{0:T(128)} %refs_0_.1) | copy-start | bytes 28
  24.8 4.0 %collective-permute-start.14 = (bf16[4,2,256,128]{3,2,1,0:T(8,128)(2,1)S(1)}, bf16[4,2,256,128]{3,2,1,0:T(8,128)(2,1)S(1)}, u32[]{:S(2)}, u32[]{:S(2)}) collective-permute-start(bf16[4,2,256,128]{3,2,1,0:T(8,128)(2,1)S(1)} %get-tuple-element.17), channel_id=1, source_target_pairs={{0,1},{1,0},{2,3},{3,2},{4,5},{5,4},{6,7},{7,6},{8,9},{9,8},{10,11... | collective-permute-start | bytes 1572872 | tf_op jit(solution)/shard_map/ppermute | solution.py:173
  25.3 9.2 %collective-permute-start.11 = (bf16[2,256,256]{2,1,0:T(8,128)(2,1)S(1)}, bf16[2,256,256]{2,1,0:T(8,128)(2,1)S(1)}, u32[]{:S(2)}, u32[]{:S(2)}) collective-permute-start(bf16[2,256,256]{2,1,0:T(8,128)(2,1)S(1)} %get-tuple-element.13), channel_id=1, source_target_pairs={{0,8},{8,0},{16,24},{24,16},{1,9},{9,1},{17,25},{25,17},{2,10},{10... | collective-permute-start | bytes 786440 | tf_op jit(solution)/shard_map/ppermute | solution.py:167
  25.8 13.6 %collective-permute-start.12 = (bf16[2,256,256]{2,1,0:T(8,128)(2,1)S(1)}, bf16[2,256,256]{2,1,0:T(8,128)(2,1)S(1)}, u32[]{:S(2)}, u32[]{:S(2)}) collective-permute-start(bf16[2,256,256]{2,1,0:T(8,128)(2,1)S(1)} %get-tuple-element.14), channel_id=1, source_target_pairs={{0,16},{8,24},{16,0},{24,8},{1,17},{9,25},{17,1},{25,9},{2,18},{10... | collective-permute-start | bytes 786440 | tf_op jit(solution)/shard_map/ppermute | solution.py:167
  26.3 13.1 %collective-permute-start.13 = (bf16[2,256,256]{2,1,0:T(8,128)(2,1)S(1)}, bf16[2,256,256]{2,1,0:T(8,128)(2,1)S(1)}, u32[]{:S(2)}, u32[]{:S(2)}) collective-permute-start(bf16[2,256,256]{2,1,0:T(8,128)(2,1)S(1)} %get-tuple-element.15), channel_id=1, source_target_pairs={{0,24},{8,16},{16,8},{24,0},{1,25},{9,17},{17,9},{25,1},{2,26},{10... | collective-permute-start | bytes 786440 | tf_op jit(solution)/shard_map/ppermute | solution.py:167
  28.9 11.5 %collective-permute-start.15 = (bf16[2,256,128]{2,1,0:T(8,128)(2,1)S(1)}, bf16[2,256,128]{2,1,0:T(8,128)(2,1)S(1)}, u32[]{:S(2)}, u32[]{:S(2)}) collective-permute-start(bf16[2,256,128]{2,1,0:T(8,128)(2,1)S(1)} %get-tuple-element.19), channel_id=1, source_target_pairs={{0,2},{1,3},{2,0},{3,1},{4,6},{5,7},{6,4},{7,5},{8,10},{9,11},{10,... | collective-permute-start | bytes 393224 | tf_op jit(solution)/shard_map/ppermute | solution.py:170
  28.9 11.4 %collective-permute-start.16 = (bf16[2,256,128]{2,1,0:T(8,128)(2,1)S(1)}, bf16[2,256,128]{2,1,0:T(8,128)(2,1)S(1)}, u32[]{:S(2)}, u32[]{:S(2)}) collective-permute-start(bf16[2,256,128]{2,1,0:T(8,128)(2,1)S(1)} %get-tuple-element.20), channel_id=1, source_target_pairs={{0,4},{1,5},{2,6},{3,7},{4,0},{5,1},{6,2},{7,3},{8,12},{9,13},{10,... | collective-permute-start | bytes 393224 | tf_op jit(solution)/shard_map/ppermute | solution.py:170
  34.4 6.9 %collective-permute-start.17 = (bf16[2,256,128]{2,1,0:T(8,128)(2,1)S(1)}, bf16[2,256,128]{2,1,0:T(8,128)(2,1)S(1)}, u32[]{:S(2)}, u32[]{:S(2)}) collective-permute-start(bf16[2,256,128]{2,1,0:T(8,128)(2,1)S(1)} %get-tuple-element.21), channel_id=1, source_target_pairs={{0,6},{1,7},{2,4},{3,5},{4,2},{5,3},{6,0},{7,1},{8,14},{9,15},{10,... | collective-permute-start | bytes 393224 | tf_op jit(solution)/shard_map/ppermute | solution.py:170

commit v3 on v2

--- a/solution.py
+++ b/solution.py
@@ -9,6 +9,7 @@
 
 CORES = 2
 LANES = 128
+X_MASK, Y_MASK = 1, 2
 
 
 def pick_energy(index_values, energies):
@@ -65,34 +66,13 @@
     return (density, amp_grad)
 
 
-def products(n_row, n_chip, *refs):
-    refs = list(refs)
-    i_list, pairs, vir_offsets, occ_energy, vir_smem, vir_rows = refs[:6]
-    mine = refs[6 : 6 + n_chip]
-    other = refs[6 + n_chip : 6 + 2 * n_chip]
-    ints = refs[6 + 2 * n_chip : 6 + 2 * n_chip + n_row]
-    outs = refs[6 + 2 * n_chip + n_row :]
-    dens_out = outs[:n_row]
-    grad_mine, grad_other, amp_full, ints_full = outs[n_row:]
-    n_pair, block_c, width = amp_full.shape
-    n_i, _, tile = ints_full.shape
-    sub_d = mine[0].shape[2]
-    block_d = ints[0].shape[1]
+def denominators(
+    i_list, pairs, vir_offsets, occ_energy, vir_smem, vir_rows, denom
+):
+    n_i, n_pair, block_c, tile = denom.shape
     width_b = tile // LANES
     row_pos = lax.axis_index("row")
     col_pos = lax.axis_index("col")
-    chip_pos = col_pos // CORES
-    core_pos = col_pos % CORES
-    for step in range(n_chip):
-        base_d = (chip_pos ^ step) * (CORES * sub_d)
-        at_mine = pl.multiple_of(base_d + core_pos * sub_d, sub_d)
-        at_other = pl.multiple_of(base_d + (1 - core_pos) * sub_d, sub_d)
-        amp_full[:, :, pl.ds(at_mine, sub_d)] = mine[step][...]
-        amp_full[:, :, pl.ds(at_other, sub_d)] = other[step][...]
-    for step in range(n_row):
-        at = pl.multiple_of((row_pos ^ step) * block_d, block_d)
-        ints_full[:, pl.ds(at, block_d), :] = ints[step][...]
-
     rows_c = block_c // LANES
     e_c = vir_rows[pl.ds(row_pos * rows_c, rows_c), :]
     e_c = jnp.concatenate(
@@ -104,8 +84,6 @@
         e_b = vir_smem[vir_offsets[1] + col_pos * width_b + b]
         base.append(-((e_c + e_b) + e_a))
     base = jnp.concatenate(base, axis=1)
-
-    scaled = []
     for slot in range(n_i):
         for pair in range(n_pair):
             occ = (
@@ -113,8 +91,43 @@
                 + occ_energy[pairs[pair, 0]]
                 + occ_energy[pairs[pair, 1]]
             )
+            denom[slot, pair] = occ + base
+
+
+def products(n_chip, *refs):
+    denom, ints_own, ints_x, ints_y, ints_xy, ints_yx = refs[:6]
+    mine = refs[6 : 6 + n_chip]
+    other = refs[6 + n_chip : 6 + 2 * n_chip]
+    keep_x, send_x, keep_y, send_y, grad_mine, grad_other = refs[6 + 2 * n_chip : 12 + 2 * n_chip]
+    amp_full, ints_full = refs[12 + 2 * n_chip :]
+    n_pair, block_c, width = amp_full.shape
+    n_i, _, tile = ints_full.shape
+    half = n_i // 2
+    sub_d = mine[0].shape[2]
+    block_d = ints_own.shape[1]
+    row_pos = lax.axis_index("row")
+    col_pos = lax.axis_index("col")
+    chip_pos = col_pos // CORES
+    core_pos = col_pos % CORES
+    both = X_MASK ^ Y_MASK
+    for mask, block in ((0, ints_own), (X_MASK, ints_x), (Y_MASK, ints_y)):
+        at = pl.multiple_of((row_pos ^ mask) * block_d, block_d)
+        ints_full[:, pl.ds(at, block_d), :] = block[...]
+    at = pl.multiple_of((row_pos ^ both) * block_d, block_d)
+    ints_full[:half, pl.ds(at, block_d), :] = ints_xy[...]
+    ints_full[half:, pl.ds(at, block_d), :] = ints_yx[...]
+    for step in range(n_chip):
+        base_d = (chip_pos ^ step) * (CORES * sub_d)
+        at_mine = pl.multiple_of(base_d + core_pos * sub_d, sub_d)
+        at_other = pl.multiple_of(base_d + (1 - core_pos) * sub_d, sub_d)
+        amp_full[:, :, pl.ds(at_mine, sub_d)] = mine[step][...]
+        amp_full[:, :, pl.ds(at_other, sub_d)] = other[step][...]
+
+    scaled = []
+    for slot in range(n_i):
+        for pair in range(n_pair):
             triples = jnp.dot(amp_full[pair], ints_full[slot], preferred_element_type=jnp.float32)
-            scaled.append((triples / (occ + base)).astype(jnp.bfloat16))
+            scaled.append((triples / denom[slot, pair]).astype(jnp.bfloat16))
 
     low = core_pos == 0
     for step in range(n_chip):
@@ -133,9 +146,12 @@
             grad_mine[step, pair] = jnp.where(low, first, second).astype(grad_mine.dtype)
             grad_other[step, pair] = jnp.where(low, second, first).astype(grad_other.dtype)
 
-    for step in range(n_row):
-        at = pl.multiple_of((row_pos ^ step) * block_d, block_d)
-        for slot in range(n_i):
+    plan = ((0, 0, keep_x, 0), (0, Y_MASK, keep_x, 1), (0, X_MASK, send_x, 0), (0, both, send_x, 1))
+    plan += ((1, 0, keep_y, 0), (1, X_MASK, keep_y, 1), (1, Y_MASK, send_y, 0), (1, both, send_y, 1))
+    for part_of, mask, out, place in plan:
+        at = pl.multiple_of((row_pos ^ mask) * block_d, block_d)
+        for k in range(half):
+            slot = part_of * half + k
             total = None
             for pair in range(n_pair):
                 part = lax.dot_general(
@@ -145,7 +161,25 @@
                     preferred_element_type=jnp.float32,
                 )
                 total = part if total is None else total + part
-            dens_out[step][slot] = total.astype(dens_out[step].dtype)
+            out[place, k] = total.astype(out.dtype)
+
+
+def results(own_x, last_x, own_y, last_y, own, *refs):
+    density, amp_grad = refs[-2:]
+    total = own[...]
+    for value in refs[:-2]:
+        total = total + value[...].astype(jnp.float32)
+    amp_grad[...] = total.astype(amp_grad.dtype)
+    half = own_x.shape[0]
+    for part_of, (kept, last) in enumerate(((own_x, last_x), (own_y, last_y))):
+        for k in range(half):
+            total = (kept[k] + last[k].astype(jnp.float32)).astype(density.dtype)
+            density[part_of * half + k] = total.reshape(density.shape[1:])
+
+
+def row_sums(keep, received, own, onward):
+    own[...] = keep[0] + received[0].astype(jnp.float32)
+    onward[...] = (keep[1] + received[1].astype(jnp.float32)).astype(onward.dtype)
 
 
 def core_sums(n_chip, own, received, kept, *outs):
@@ -172,72 +206,83 @@
     def over_cores(value):
         return lax.ppermute(value, "col", [(k, k ^ 1) for k in range(n_col)])
 
-    mine = [amplitudes] + [over_chips(amplitudes, step) for step in range(1, n_chip)]
-    near = [over_row(integrals, 1), over_row(integrals, 2)]
-    half = n_i // 2
-    far = jnp.concatenate([over_row(near[0][:half], 2), over_row(near[1][half:], 1)])
-    ints = [value.reshape(n_i, block_d, tile) for value in [integrals] + near + [far]]
-    other = [over_cores(value) for value in mine]
-
     vmem = pl.BlockSpec(memory_space=pltpu.VMEM)
     smem = pl.BlockSpec(memory_space=pltpu.SMEM)
+    shape = jax.ShapeDtypeStruct
     f32, bf16 = jnp.float32, jnp.bfloat16
-    flops = 6 * n_i * n_pair * block_c * width * tile
-    results = pl.pallas_call(
-        functools.partial(products, n_row, n_chip),
-        out_shape=[
-            jax.ShapeDtypeStruct((n_i, block_d, tile), f32 if step == 0 else bf16)
-            for step in range(n_row)
-        ]
-        + [
-            jax.ShapeDtypeStruct((n_chip, n_pair, block_c, sub_d), f32),
-            jax.ShapeDtypeStruct((n_chip, n_pair, block_c, sub_d), bf16),
-        ],
-        in_specs=[smem] * 5 + [vmem] * (1 + 2 * n_chip + n_row),
-        out_specs=[vmem] * (n_row + 2),
+
+    def room(mib):
+        return pltpu.CompilerParams(vmem_limit_bytes=mib * 2**20)
+
+    def flat(value):
+        return value.reshape(value.shape[:2] + (tile,))
+
+    half = n_i // 2
+    denom = pl.pallas_call(
+        denominators,
+        out_shape=shape((n_i, n_pair, block_c, tile), f32),
+        in_specs=[smem] * 5 + [vmem],
+        out_specs=vmem,
+        compiler_params=room(8),
+        name="denominators",
+    )(i_list, pairs, vir_offsets, occ_energy, vir_energy, vir_energy.reshape(-1, LANES))
+    mine = [amplitudes] + [over_chips(amplitudes, step) for step in range(1, n_chip)]
+    ints_x, ints_y = over_row(integrals, X_MASK), over_row(integrals, Y_MASK)
+    ints_own = flat(integrals)
+    ints_y, denom = lax.optimization_barrier((ints_y, denom))
+    ints_xy, ints_yx = over_row(ints_x[:half], Y_MASK), over_row(ints_y[half:], X_MASK)
+    flat_x, flat_y = flat(ints_x), flat(ints_y)
+    other = [over_cores(value) for value in mine]
+    dens_shape = (2, half, block_d, tile)
+    grad_shape = (n_chip, n_pair, block_c, sub_d)
+    keep_x, send_x, keep_y, send_y, grad_mine, grad_other = pl.pallas_call(
+        functools.partial(products, n_chip),
+        out_shape=[shape(dens_shape, f32), shape(dens_shape, bf16)] * 2
+        + [shape(grad_shape, f32), shape(grad_shape, bf16)],
+        in_specs=[vmem] * (6 + 2 * n_chip),
+        out_specs=[vmem] * 6,
         scratch_shapes=[
             pltpu.VMEM((n_pair, block_c, width), bf16),
             pltpu.VMEM((n_i, width, tile), bf16),
         ],
-        compiler_params=pltpu.CompilerParams(vmem_limit_bytes=40 * 2**20),
-        cost_estimate=pl.CostEstimate(flops=flops, bytes_accessed=8 * 2**20, transcendentals=0),
+        compiler_params=room(36),
         name="products",
-    )(
-        i_list,
-        pairs,
-        vir_offsets,
-        occ_energy,
-        vir_energy,
-        vir_energy.reshape(width // LANES, LANES),
-        *mine,
-        *other,
-        *ints,
-    )
-    dens = results[:n_row]
-    grad_mine, grad_other = results[n_row:]
+    )(denom, ints_own, flat_x, flat_y, flat(ints_xy), flat(ints_yx), *mine, *other)
     block = (n_pair, block_c, sub_d)
     grads = pl.pallas_call(
         functools.partial(core_sums, n_chip),
-        out_shape=[
-            jax.ShapeDtypeStruct(block, f32 if step == 0 else bf16) for step in range(n_chip)
-        ],
+        out_shape=[shape(block, f32 if step == 0 else bf16) for step in range(n_chip)],
         in_specs=[vmem] * 2,
         out_specs=[vmem] * n_chip,
-        compiler_params=pltpu.CompilerParams(vmem_limit_bytes=24 * 2**20),
+        compiler_params=room(16),
         name="core_sums",
     )(grad_mine, over_cores(grad_other))
-    dens_in = [over_row(dens[step], step) for step in range(1, n_row)]
-    grad_in = [over_chips(grads[step], step) for step in range(1, n_chip)]
-    density = dens[0]
-    for value in dens_in:
-        density = density + value.astype(f32)
-    amp_grad = grads[0]
-    for value in grad_in:
-        amp_grad = amp_grad + value.astype(f32)
-    return (
-        density.astype(bf16).reshape(n_i, block_d, width_b, width_a),
-        amp_grad.astype(bf16),
-    )
+
+    def summed(keep, received):
+        return pl.pallas_call(
+            row_sums,
+            out_shape=[shape(dens_shape[1:], f32), shape(dens_shape[1:], bf16)],
+            in_specs=[vmem] * 2,
+            out_specs=[vmem] * 2,
+            compiler_params=room(8),
+            name="row_sums",
+        )(keep, received)
+
+    from_x, from_y = over_row(send_x, X_MASK), over_row(send_y, Y_MASK)
+    grad_parts = [over_chips(grads[step], step) for step in range(1, n_chip)]
+    from_x, from_y, grad_parts[0] = lax.optimization_barrier((from_x, from_y, grad_parts[0]))
+    own_x, onward_x = summed(keep_x, from_x)
+    own_y, onward_y = summed(keep_y, from_y)
+    last_x, last_y = over_row(onward_x, Y_MASK), over_row(onward_y, X_MASK)
+    density, amp_grad = pl.pallas_call(
+        results,
+        out_shape=[shape((n_i, block_d, width_b, width_a), bf16), shape(block, bf16)],
+        in_specs=[vmem] * (4 + n_chip),
+        out_specs=[vmem] * 2,
+        compiler_params=room(16),
+        name="results",
+    )(own_x, last_x, own_y, last_y, grads[0], *grad_parts)
+    return density, amp_grad
 
 
 def solution(mesh):

time: 42.2 us -> 41.6 us (0.986)
  waiting for transfers between devices: 12.4 us -> 15 us
  starting transfers between devices: 22.4 us -> 20.6 us
  other arithmetic: 1.21 us -> 0 us
  local copies, waits for them, and re-layouts: 2.19 us -> 0.99 us
  Pallas kernels: 2.95 us -> 4.03 us
    ppermute x6, waiting for transfers between devices: 6.7 us -> 11.2 us  [over_chips(): lax.ppermute(value, 'col', [(k, k ^ CORES * mask) for k in range(n_col)])]
    ppermute x7 -> x8, waiting for transfers between devices: 5.64 us -> 2.64 us  [over_row(): return lax.ppermute(value, 'row', [(k, k ^ mask) for k in range(n_row)])]
    ppermute x5, waiting for transfers between devices: 0.1 us -> 1.23 us  [over_cores(): return lax.ppermute(value, 'col', [(k, k ^ 1) for k in range(n_col)])]
    pallas_call x2 -> x6, Pallas kernels: 2.95 us -> 4.03 us  [the longest x1 2.25 us: exchanged(): pl.pallas_call(functools.partial(products, n_chip), out_shape=[shape(dens...]
    ppermute x7 -> x8, starting transfers between devices: 11.4 us -> 10.5 us  [over_row(): return lax.ppermute(value, 'row', [(k, k ^ mask) for k in range(n_row)])]
    convert_element_type x2 -> x0, other arithmetic: 0.84 us -> none  [the longest x1 0.72 us: exchanged(): amp_grad.astype(bf16)]
    reshape x5, local copies, waits for them, and re-layouts: 1.44 us -> 0.69 us  [flat(): return value.reshape(value.shape[:2] + (tile,))]
    ppermute x6, starting transfers between devices: 9.96 us -> 9.34 us  [over_chips(): lax.ppermute(value, 'col', [(k, k ^ CORES * mask) for k in range(n_col)])]
  transfers between devices with their start and end apart: 18 -> 19, of which waited for: 6 -> 10; matrix products, arithmetic and copies ran while one was open for 5% -> 2% of each run, Pallas kernels for 0% -> 2%
where the time goes in v3:
time: 41.6 us; the launch traced here: 41.5 us
  starting transfers between devices  20.6 us (50%)
  waiting for transfers between devices  15 us (36%)
  Pallas kernels  4.03 us (10%)
  local copies, waits for them, and re-layouts  0.99 us (2%)
  between operations  0.8 us (2%)
    ppermute x6, waiting for transfers between devices, over_chips(): lax.ppermute(value, 'col', [(k, k ^ CORES * mask) for k in range(n_col)])  11.2 us
    ppermute x8, starting transfers between devices, over_row(): return lax.ppermute(value, 'row', [(k, k ^ mask) for k in range(n_row)])  10.5 us
    ppermute x6, starting transfers between devices, over_chips(): lax.ppermute(value, 'col', [(k, k ^ CORES * mask) for k in range(n_col)])  9.34 us
    ppermute x8, waiting for transfers between devices, over_row(): return lax.ppermute(value, 'row', [(k, k ^ mask) for k in range(n_row)])  2.64 us
    pallas_call x1, Pallas kernels, exchanged(): pl.pallas_call(functools.partial(products, n_chip), out_shape=[shape(dens...  2.25 us
    ppermute x5, waiting for transfers between devices, over_cores(): return lax.ppermute(value, 'col', [(k, k ^ 1) for k in range(n_col)])  1.23 us
  transfers between devices with their start and end apart: 19, of which 10 were waited for; matrix products, arithmetic and copies ran while one was open for 2% of the time, Pallas kernels for 2%

profile of v3, /device:TPU:0, one launch (start us, length us, event | category | flops | bytes accessed | tf_op | source)
XLA Modules:
  0.0 41.5 jit_solution(2482181306662654474)
XLA Ops:
  0.6 3.0 %collective-permute-start.1 = (bf16[2,256,2,128]{3,2,1,0:T(2,128)(2,1)}, bf16[2,256,2,128]{3,2,1,0:T(2,128)(2,1)S(1)}, u32[]{:S(2)}, u32[]{:S(2)}) collective-permute-start(bf16[2,256,2,128]{3,2,1,0:T(2,128)(2,1)} %param.13), channel_id=1, source_target_pairs={{0,8},{8,0},{16,24},{24,16},{1,9},{9,1},{17,25},{25,17},{2,10},{10... | collective-permute-start | bytes 786440 | tf_op jit(solution)/shard_map/ppermute | solution.py:201
  3.6 1.5 %collective-permute-start = (bf16[2,256,2,128]{3,2,1,0:T(2,128)(2,1)}, bf16[2,256,2,128]{3,2,1,0:T(2,128)(2,1)S(1)}, u32[]{:S(2)}, u32[]{:S(2)}) collective-permute-start(bf16[2,256,2,128]{3,2,1,0:T(2,128)(2,1)} %param.13), channel_id=1, source_target_pairs={{0,16},{8,24},{16,0},{24,8},{1,17},{9,25},{17,1},{25,9},{2,18},{10... | collective-permute-start | bytes 786440 | tf_op jit(solution)/shard_map/ppermute | solution.py:201
  5.2 3.6 %collective-permute-start.6 = (bf16[2,256,128]{2,1,0:T(8,128)(2,1)}, bf16[2,256,128]{2,1,0:T(8,128)(2,1)S(1)}, u32[]{:S(2)}, u32[]{:S(2)}) collective-permute-start(bf16[2,256,128]{2,1,0:T(8,128)(2,1)} %refs_6_.1), channel_id=1, source_target_pairs={{0,6},{1,7},{2,4},{3,5},{4,2},{5,3},{6,0},{7,1},{8,14},{9,15},{10,... | collective-permute-start | bytes 393224 | tf_op jit(solution)/shard_map/ppermute | solution.py:204
  8.8 0.8 %collective-permute-start.4 = (bf16[2,256,128]{2,1,0:T(8,128)(2,1)}, bf16[2,256,128]{2,1,0:T(8,128)(2,1)S(1)}, u32[]{:S(2)}, u32[]{:S(2)}) collective-permute-start(bf16[2,256,128]{2,1,0:T(8,128)(2,1)} %refs_6_.1), channel_id=1, source_target_pairs={{0,2},{1,3},{2,0},{3,1},{4,6},{5,7},{6,4},{7,5},{8,10},{9,11},{10,... | collective-permute-start | bytes 393224 | tf_op jit(solution)/shard_map/ppermute | solution.py:204
  9.5 0.6 %collective-permute-done.1 = bf16[2,256,2,128]{3,2,1,0:T(2,128)(2,1)S(1)} collective-permute-done((bf16[2,256,2,128]{3,2,1,0:T(2,128)(2,1)}, bf16[2,256,2,128]{3,2,1,0:T(2,128)(2,1)S(1)}, u32[]{:S(2)}, u32[]{:S(2)}) %collective-permute-start.1) | collective-permute-done | bytes 262176 | tf_op jit(solution)/shard_map/ppermute | solution.py:201
  10.2 0.1 slice.8
  10.3 0.0 copy-start.2
  10.3 0.0 copy-start.3
  10.3 1.8 %collective-permute-start.2 = (bf16[1,256,2,128]{3,2,1,0:T(2,128)(2,1)S(1)}, bf16[1,256,2,128]{3,2,1,0:T(2,128)(2,1)S(1)}, u32[]{:S(2)}, u32[]{:S(2)}) collective-permute-start(bf16[1,256,2,128]{3,2,1,0:T(2,128)(2,1)S(1)} %slice.8), channel_id=1, source_target_pairs={{0,16},{8,24},{16,0},{24,8},{1,17},{9,25},{17,1},{25,9},{2,18},{10... | collective-permute-start | bytes 393224 | tf_op jit(solution)/shard_map/ppermute | solution.py:201
  12.1 0.0 copy-start
  12.1 0.8 %denominators.1.refs_0_ = f32[2,2,256,256]{3,2,1,0:T(8,128)S(1)} custom-call(s32[2]{0:T(128)S(1)} %copy-done.3, s32[2,2]{1,0:T(2,128)S(1)} %copy-done.2, s32[2]{0:T(128)S(1)} %copy-done.4, f32[128]{0:T(128)S(1)} %copy-done.5, f32[1024]{0:T(1024)S(1)} %copy-done.1, f32[8,128]{1,0:T(8,128)S(1)} %bitcast.1), custom_call_target="tpu_custom_call" | custom-call | tf_op jit(solution)/shard_map/denominators/pallas_call | solution.py:221
  12.9 0.0 copy-start.6
  13.0 0.0 collective-permute-done
  13.0 0.1 copy-done
  13.0 0.0 collective-permute-start.7
  13.1 0.1 slice.7
  13.2 0.4 %collective-permute-done.6.refs_9_ = bf16[2,256,128]{2,1,0:T(8,128)(2,1)S(1)} collective-permute-done((bf16[2,256,128]{2,1,0:T(8,128)(2,1)}, bf16[2,256,128]{2,1,0:T(8,128)(2,1)S(1)}, u32[]{:S(2)}, u32[]{:S(2)}) %collective-permute-start.6) | collective-permute-done | bytes 131104 | tf_op jit(solution)/shard_map/ppermute | solution.py:204
  13.6 1.1 %collective-permute-start.3 = (bf16[1,256,2,128]{3,2,1,0:T(2,128)(2,1)S(1)}, bf16[1,256,2,128]{3,2,1,0:T(2,128)(2,1)S(1)}, u32[]{:S(2)}, u32[]{:S(2)}) collective-permute-start(bf16[1,256,2,128]{3,2,1,0:T(2,128)(2,1)S(1)} %slice.7), channel_id=1, source_target_pairs={{0,8},{8,0},{16,24},{24,16},{1,9},{9,1},{17,25},{25,17},{2,10},{10... | collective-permute-start | bytes 393224 | tf_op jit(solution)/shard_map/ppermute | solution.py:201
  14.7 4.8 %collective-permute-done.5.refs_8_ = bf16[2,256,128]{2,1,0:T(8,128)(2,1)S(1)} collective-permute-done((bf16[2,256,128]{2,1,0:T(8,128)(2,1)}, bf16[2,256,128]{2,1,0:T(8,128)(2,1)S(1)}, u32[]{:S(2)}, u32[]{:S(2)}) %collective-permute-start.5) | collective-permute-done | bytes 131104 | tf_op jit(solution)/shard_map/ppermute | solution.py:204
  19.5 0.5 %collective-permute-start.9 = (bf16[2,256,128]{2,1,0:T(8,128)(2,1)S(1)}, bf16[2,256,128]{2,1,0:T(8,128)(2,1)S(1)}, u32[]{:S(2)}, u32[]{:S(2)}) collective-permute-start(bf16[2,256,128]{2,1,0:T(8,128)(2,1)S(1)} %collective-permute-done.5.refs_8_), channel_id=1, source_target_pairs={{0,1},{1,0},{2,3},{3,2},{4,5},{5,4},{6,7},{7,6},{8,9},{9,8},{10,11... | collective-permute-start | bytes 393224 | tf_op jit(solution)/shard_map/ppermute | solution.py:207
  20.0 0.1 collective-permute-start.8
  20.1 0.2 reshape.23.refs_1_
  20.2 0.2 reshape.25.refs_3_
  20.4 0.2 reshape.24.refs_2_
  20.6 0.1 reshape.26.refs_4_
  20.7 0.0 collective-permute-done.3
  20.7 0.1 reshape.27.refs_5_
  20.8 0.0 collective-permute-done.7.refs_10_
  20.8 0.0 collective-permute-done.10.refs_13_
  20.8 0.2 collective-permute-done.9.refs_12_
  21.0 0.3 collective-permute-done.8.refs_11_
  21.3 2.2 %products.1 = (f32[2,1,256,256]{3,2,1,0:T(8,128)S(1)}, bf16[2,1,256,256]{3,2,1,0:T(8,128)(2,1)S(1)}, f32[2,1,256,256]{3,2,1,0:T(8,128)S(1)}, bf16[2,1,256,256]{3...) custom-call(f32[2,2,256,256]{3,2,1,0:T(8,128)S(1)} %denominators.1.refs_0_, ...), custom_call_target="tpu_custom_call" | custom-call | tf_op jit(solution)/shard_map/products/pallas_call | solution.py:238
  23.6 0.2 collective-permute-start.13
  23.9 0.5 %collective-permute-start.11 = (bf16[2,1,256,256]{3,2,1,0:T(8,128)(2,1)S(1)}, bf16[2,1,256,256]{3,2,1,0:T(8,128)(2,1)S(1)}, u32[]{:S(2)}, u32[]{:S(2)}) collective-permute-start(bf16[2,1,256,256]{3,2,1,0:T(8,128)(2,1)S(1)} %get-tuple-element.24), channel_id=1, source_target_pairs={{0,8},{8,0},{16,24},{24,16},{1,9},{9,1},{17,25},{25,17},{2,10},{10... | collective-permute-start | bytes 786440 | tf_op jit(solution)/shard_map/ppermute | solution.py:201
  24.4 0.5 %collective-permute-start.12 = (bf16[2,1,256,256]{3,2,1,0:T(8,128)(2,1)S(1)}, bf16[2,1,256,256]{3,2,1,0:T(8,128)(2,1)S(1)}, u32[]{:S(2)}, u32[]{:S(2)}) collective-permute-start(bf16[2,1,256,256]{3,2,1,0:T(8,128)(2,1)S(1)} %get-tuple-element.25), channel_id=1, source_target_pairs={{0,16},{8,24},{16,0},{24,8},{1,17},{9,25},{17,1},{25,9},{2,18},{10... | collective-permute-start | bytes 786440 | tf_op jit(solution)/shard_map/ppermute | solution.py:201
  24.9 0.7 %collective-permute-done.13.received = bf16[4,2,256,128]{3,2,1,0:T(8,128)(2,1)S(1)} collective-permute-done((bf16[4,2,256,128]{3,2,1,0:T(8,128)(2,1)S(1)}, bf16[4,2,256,128]{3,2,1,0:T(8,128)(2,1)S(1)}, u32[]{:S(2)}, u32[]{:S(2)}) %collective-permute-start.13) | collective-permute-done | bytes 524320 | tf_op jit(solution)/shard_map/ppermute | solution.py:207
  25.6 0.1 core_sums.1
  25.7 2.1 %collective-permute-start.14 = (bf16[2,256,128]{2,1,0:T(8,128)(2,1)S(1)}, bf16[2,256,128]{2,1,0:T(8,128)(2,1)S(1)}, u32[]{:S(2)}, u32[]{:S(2)}) collective-permute-start(bf16[2,256,128]{2,1,0:T(8,128)(2,1)S(1)} %get-tuple-element.28), channel_id=1, source_target_pairs={{0,2},{1,3},{2,0},{3,1},{4,6},{5,7},{6,4},{7,5},{8,10},{9,11},{10,... | collective-permute-start | bytes 393224 | tf_op jit(solution)/shard_map/ppermute | solution.py:204
  27.7 1.5 %collective-permute-start.17 = (bf16[2,256,128]{2,1,0:T(8,128)(2,1)S(1)}, bf16[2,256,128]{2,1,0:T(8,128)(2,1)S(1)}, u32[]{:S(2)}, u32[]{:S(2)}) collective-permute-start(bf16[2,256,128]{2,1,0:T(8,128)(2,1)S(1)} %get-tuple-element.38), channel_id=1, source_target_pairs={{0,4},{1,5},{2,6},{3,7},{4,0},{5,1},{6,2},{7,3},{8,12},{9,13},{10,... | collective-permute-start | bytes 393224 | tf_op jit(solution)/shard_map/ppermute | solution.py:204
  29.2 1.4 %collective-permute-start.18 = (bf16[2,256,128]{2,1,0:T(8,128)(2,1)S(1)}, bf16[2,256,128]{2,1,0:T(8,128)(2,1)S(1)}, u32[]{:S(2)}, u32[]{:S(2)}) collective-permute-start(bf16[2,256,128]{2,1,0:T(8,128)(2,1)S(1)} %get-tuple-element.39), channel_id=1, source_target_pairs={{0,6},{1,7},{2,4},{3,5},{4,2},{5,3},{6,0},{7,1},{8,14},{9,15},{10,... | collective-permute-start | bytes 393224 | tf_op jit(solution)/shard_map/ppermute | solution.py:204
  30.6 1.8 %collective-permute-done.11.received = bf16[2,1,256,256]{3,2,1,0:T(8,128)(2,1)S(1)} collective-permute-done((bf16[2,1,256,256]{3,2,1,0:T(8,128)(2,1)S(1)}, bf16[2,1,256,256]{3,2,1,0:T(8,128)(2,1)S(1)}, u32[]{:S(2)}, u32[]{:S(2)}) %collective-permute-start.11) | collective-permute-done | bytes 262176 | tf_op jit(solution)/shard_map/ppermute | solution.py:201
  32.4 0.2 collective-permute-done.12.received
  32.6 0.9 %collective-permute-done.14.refs_0_ = bf16[2,256,128]{2,1,0:T(8,128)(2,1)S(1)} collective-permute-done((bf16[2,256,128]{2,1,0:T(8,128)(2,1)S(1)}, bf16[2,256,128]{2,1,0:T(8,128)(2,1)S(1)}, u32[]{:S(2)}, u32[]{:S(2)}) %collective-permute-start.14) | collective-permute-done | bytes 131104 | tf_op jit(solution)/shard_map/ppermute | solution.py:204
  33.6 0.6 %collective-permute-start.16 = (bf16[1,256,256]{2,1,0:T(8,128)(2,1)S(1)}, bf16[1,256,256]{2,1,0:T(8,128)(2,1)S(1)}, u32[]{:S(2)}, u32[]{:S(2)}) collective-permute-start(bf16[1,256,256]{2,1,0:T(8,128)(2,1)S(1)} %get-tuple-element.35), channel_id=1, source_target_pairs={{0,8},{8,0},{16,24},{24,16},{1,9},{9,1},{17,25},{25,17},{2,10},{10... | collective-permute-start | bytes 393224 | tf_op jit(solution)/shard_map/ppermute | solution.py:201
  34.3 1.3 %collective-permute-start.15 = (bf16[1,256,256]{2,1,0:T(8,128)(2,1)S(1)}, bf16[1,256,256]{2,1,0:T(8,128)(2,1)S(1)}, u32[]{:S(2)}, u32[]{:S(2)}) collective-permute-start(bf16[1,256,256]{2,1,0:T(8,128)(2,1)S(1)} %get-tuple-element.31), channel_id=1, source_target_pairs={{0,16},{8,24},{16,0},{24,8},{1,17},{9,25},{17,1},{25,9},{2,18},{10... | collective-permute-start | bytes 393224 | tf_op jit(solution)/shard_map/ppermute | solution.py:201
  35.6 5.0 %collective-permute-done.17.refs_1_ = bf16[2,256,128]{2,1,0:T(8,128)(2,1)S(1)} collective-permute-done((bf16[2,256,128]{2,1,0:T(8,128)(2,1)S(1)}, bf16[2,256,128]{2,1,0:T(8,128)(2,1)S(1)}, u32[]{:S(2)}, u32[]{:S(2)}) %collective-permute-start.17) | collective-permute-done | bytes 131104 | tf_op jit(solution)/shard_map/ppermute | solution.py:204
  40.7 0.0 collective-permute-done.15.last_x
  40.7 0.8 %results.1 = (bf16[2,256,2,128]{3,2,1,0:T(2,128)(2,1)}, bf16[2,256,128]{2,1,0:T(8,128)(2,1)}) custom-call(f32[1,256,256]{2,1,0:T(8,128)S(1)} %get-tuple-element.30.own_x, bf16[1,256,256]{2,1,0:T(8,128)(2,1)S(1)} %collective-permute-done.15.last_x, f32[1,256,256]{2,1,0:T(8,128)S(1)} %get-tuple-element.34.own_y, ...), custom_call_target="tpu_custom_call" | custom-call | tf_op jit(solution)/shard_map/results/pallas_call | solution.py:277
  (17 shorter events, 0.1 us)
Async XLA Ops:
  0.6 9.5 %collective-permute-start.1 = (bf16[2,256,2,128]{3,2,1,0:T(2,128)(2,1)}, bf16[2,256,2,128]{3,2,1,0:T(2,128)(2,1)S(1)}, u32[]{:S(2)}, u32[]{:S(2)}) collective-permute-start(bf16[2,256,2,128]{3,2,1,0:T(2,128)(2,1)} %param.13), channel_id=1, source_target_pairs={{0,8},{8,0},{16,24},{24,16},{1,9},{9,1},{17,25},{25,17},{2,10},{10... | collective-permute-start | bytes 786440 | tf_op jit(solution)/shard_map/ppermute | solution.py:201
  3.6 9.3 %collective-permute-start = (bf16[2,256,2,128]{3,2,1,0:T(2,128)(2,1)}, bf16[2,256,2,128]{3,2,1,0:T(2,128)(2,1)S(1)}, u32[]{:S(2)}, u32[]{:S(2)}) collective-permute-start(bf16[2,256,2,128]{3,2,1,0:T(2,128)(2,1)} %param.13), channel_id=1, source_target_pairs={{0,16},{8,24},{16,0},{24,8},{1,17},{9,25},{17,1},{25,9},{2,18},{10... | collective-permute-start | bytes 786440 | tf_op jit(solution)/shard_map/ppermute | solution.py:201
  5.2 8.4 %collective-permute-start.6 = (bf16[2,256,128]{2,1,0:T(8,128)(2,1)}, bf16[2,256,128]{2,1,0:T(8,128)(2,1)S(1)}, u32[]{:S(2)}, u32[]{:S(2)}) collective-permute-start(bf16[2,256,128]{2,1,0:T(8,128)(2,1)} %refs_6_.1), channel_id=1, source_target_pairs={{0,6},{1,7},{2,4},{3,5},{4,2},{5,3},{6,0},{7,1},{8,14},{9,15},{10,... | collective-permute-start | bytes 393224 | tf_op jit(solution)/shard_map/ppermute | solution.py:204
  8.8 10.7 %collective-permute-start.5 = (bf16[2,256,128]{2,1,0:T(8,128)(2,1)}, bf16[2,256,128]{2,1,0:T(8,128)(2,1)S(1)}, u32[]{:S(2)}, u32[]{:S(2)}) collective-permute-start(bf16[2,256,128]{2,1,0:T(8,128)(2,1)} %refs_6_.1), channel_id=1, source_target_pairs={{0,4},{1,5},{2,6},{3,7},{4,0},{5,1},{6,2},{7,3},{8,12},{9,13},{10,... | collective-permute-start | bytes 393224 | tf_op jit(solution)/shard_map/ppermute | solution.py:204
  8.8 10.7 %collective-permute-start.4 = (bf16[2,256,128]{2,1,0:T(8,128)(2,1)}, bf16[2,256,128]{2,1,0:T(8,128)(2,1)S(1)}, u32[]{:S(2)}, u32[]{:S(2)}) collective-permute-start(bf16[2,256,128]{2,1,0:T(8,128)(2,1)} %refs_6_.1), channel_id=1, source_target_pairs={{0,2},{1,3},{2,0},{3,1},{4,6},{5,7},{6,4},{7,5},{8,10},{9,11},{10,... | collective-permute-start | bytes 393224 | tf_op jit(solution)/shard_map/ppermute | solution.py:204
  10.2 2.0 %copy-start.1 = (f32[1024]{0:T(1024)S(1)}, f32[1024]{0:T(1024)}, u32[]{:S(2)}) copy-start(f32[1024]{0:T(1024)} %vir_smem.1) | copy-start | bytes 12292
  10.2 2.0 %copy-start.4 = (s32[2]{0:T(128)S(1)}, s32[2]{0:T(128)}, u32[]{:S(2)}) copy-start(s32[2]{0:T(128)} %vir_offsets.1) | copy-start | bytes 28
  10.2 2.0 %copy-start.5 = (f32[128]{0:T(128)S(1)}, f32[128]{0:T(128)}, u32[]{:S(2)}) copy-start(f32[128]{0:T(128)} %occ_energy.1) | copy-start | bytes 1540
  10.3 1.9 %copy-start.2 = (s32[2,2]{1,0:T(2,128)S(1)}, s32[2,2]{1,0:T(2,128)}, u32[]{:S(2)}) copy-start(s32[2,2]{1,0:T(2,128)} %pairs.1) | copy-start | bytes 52
  10.3 1.9 %copy-start.3 = (s32[2]{0:T(128)S(1)}, s32[2]{0:T(128)}, u32[]{:S(2)}) copy-start(s32[2]{0:T(128)} %i_list.1) | copy-start | bytes 28
  10.3 9.7 %collective-permute-start.2 = (bf16[1,256,2,128]{3,2,1,0:T(2,128)(2,1)S(1)}, bf16[1,256,2,128]{3,2,1,0:T(2,128)(2,1)S(1)}, u32[]{:S(2)}, u32[]{:S(2)}) collective-permute-start(bf16[1,256,2,128]{3,2,1,0:T(2,128)(2,1)S(1)} %slice.8), channel_id=1, source_target_pairs={{0,16},{8,24},{16,0},{24,8},{1,17},{9,25},{17,1},{25,9},{2,18},{10... | collective-permute-start | bytes 393224 | tf_op jit(solution)/shard_map/ppermute | solution.py:201
  12.1 0.9 %copy-start = (bf16[2,256,128]{2,1,0:T(8,128)(2,1)S(1)}, bf16[2,256,128]{2,1,0:T(8,128)(2,1)}, u32[]{:S(2)}) copy-start(bf16[2,256,128]{2,1,0:T(8,128)(2,1)} %refs_6_.1) | copy-start | bytes 393220
  12.9 7.1 %copy-start.6 = (bf16[2,256,2,128]{3,2,1,0:T(2,128)(2,1)S(1)}, bf16[2,256,2,128]{3,2,1,0:T(2,128)(2,1)}, u32[]{:S(2)}) copy-start(bf16[2,256,2,128]{3,2,1,0:T(2,128)(2,1)} %param.13) | copy-start | bytes 786436
  13.0 7.8 %collective-permute-start.7 = (bf16[2,256,128]{2,1,0:T(8,128)(2,1)S(1)}, bf16[2,256,128]{2,1,0:T(8,128)(2,1)S(1)}, u32[]{:S(2)}, u32[]{:S(2)}) collective-permute-start(bf16[2,256,128]{2,1,0:T(8,128)(2,1)S(1)} %copy-done), channel_id=1, source_target_pairs={{0,1},{1,0},{2,3},{3,2},{4,5},{5,4},{6,7},{7,6},{8,9},{9,8},{10,11... | collective-permute-start | bytes 393224 | tf_op jit(solution)/shard_map/ppermute | solution.py:207
  13.6 7.1 %collective-permute-start.3 = (bf16[1,256,2,128]{3,2,1,0:T(2,128)(2,1)S(1)}, bf16[1,256,2,128]{3,2,1,0:T(2,128)(2,1)S(1)}, u32[]{:S(2)}, u32[]{:S(2)}) collective-permute-start(bf16[1,256,2,128]{3,2,1,0:T(2,128)(2,1)S(1)} %slice.7), channel_id=1, source_target_pairs={{0,8},{8,0},{16,24},{24,16},{1,9},{9,1},{17,25},{25,17},{2,10},{10... | collective-permute-start | bytes 393224 | tf_op jit(solution)/shard_map/ppermute | solution.py:201
  19.5 1.3 %collective-permute-start.10 = (bf16[2,256,128]{2,1,0:T(8,128)(2,1)S(1)}, bf16[2,256,128]{2,1,0:T(8,128)(2,1)S(1)}, u32[]{:S(2)}, u32[]{:S(2)}) collective-permute-start(bf16[2,256,128]{2,1,0:T(8,128)(2,1)S(1)} %collective-permute-done.6.refs_9_), channel_id=1, source_target_pairs={{0,1},{1,0},{2,3},{3,2},{4,5},{5,4},{6,7},{7,6},{8,9},{9,8},{10,11... | collective-permute-start | bytes 393224 | tf_op jit(solution)/shard_map/ppermute | solution.py:207
  19.5 1.5 %collective-permute-start.9 = (bf16[2,256,128]{2,1,0:T(8,128)(2,1)S(1)}, bf16[2,256,128]{2,1,0:T(8,128)(2,1)S(1)}, u32[]{:S(2)}, u32[]{:S(2)}) collective-permute-start(bf16[2,256,128]{2,1,0:T(8,128)(2,1)S(1)} %collective-permute-done.5.refs_8_), channel_id=1, source_target_pairs={{0,1},{1,0},{2,3},{3,2},{4,5},{5,4},{6,7},{7,6},{8,9},{9,8},{10,11... | collective-permute-start | bytes 393224 | tf_op jit(solution)/shard_map/ppermute | solution.py:207
  20.0 1.3 %collective-permute-start.8 = (bf16[2,256,128]{2,1,0:T(8,128)(2,1)S(1)}, bf16[2,256,128]{2,1,0:T(8,128)(2,1)S(1)}, u32[]{:S(2)}, u32[]{:S(2)}) collective-permute-start(bf16[2,256,128]{2,1,0:T(8,128)(2,1)S(1)} %collective-permute-done.4.refs_7_), channel_id=1, source_target_pairs={{0,1},{1,0},{2,3},{3,2},{4,5},{5,4},{6,7},{7,6},{8,9},{9,8},{10,11... | collective-permute-start | bytes 393224 | tf_op jit(solution)/shard_map/ppermute | solution.py:207
  23.6 2.0 %collective-permute-start.13 = (bf16[4,2,256,128]{3,2,1,0:T(8,128)(2,1)S(1)}, bf16[4,2,256,128]{3,2,1,0:T(8,128)(2,1)S(1)}, u32[]{:S(2)}, u32[]{:S(2)}) collective-permute-start(bf16[4,2,256,128]{3,2,1,0:T(8,128)(2,1)S(1)} %get-tuple-element.27), channel_id=1, source_target_pairs={{0,1},{1,0},{2,3},{3,2},{4,5},{5,4},{6,7},{7,6},{8,9},{9,8},{10,11... | collective-permute-start | bytes 1572872 | tf_op jit(solution)/shard_map/ppermute | solution.py:207
  23.9 8.5 %collective-permute-start.11 = (bf16[2,1,256,256]{3,2,1,0:T(8,128)(2,1)S(1)}, bf16[2,1,256,256]{3,2,1,0:T(8,128)(2,1)S(1)}, u32[]{:S(2)}, u32[]{:S(2)}) collective-permute-start(bf16[2,1,256,256]{3,2,1,0:T(8,128)(2,1)S(1)} %get-tuple-element.24), channel_id=1, source_target_pairs={{0,8},{8,0},{16,24},{24,16},{1,9},{9,1},{17,25},{25,17},{2,10},{10... | collective-permute-start | bytes 786440 | tf_op jit(solution)/shard_map/ppermute | solution.py:201
  24.4 8.3 %collective-permute-start.12 = (bf16[2,1,256,256]{3,2,1,0:T(8,128)(2,1)S(1)}, bf16[2,1,256,256]{3,2,1,0:T(8,128)(2,1)S(1)}, u32[]{:S(2)}, u32[]{:S(2)}) collective-permute-start(bf16[2,1,256,256]{3,2,1,0:T(8,128)(2,1)S(1)} %get-tuple-element.25), channel_id=1, source_target_pairs={{0,16},{8,24},{16,0},{24,8},{1,17},{9,25},{17,1},{25,9},{2,18},{10... | collective-permute-start | bytes 786440 | tf_op jit(solution)/shard_map/ppermute | solution.py:201
  25.7 7.9 %collective-permute-start.14 = (bf16[2,256,128]{2,1,0:T(8,128)(2,1)S(1)}, bf16[2,256,128]{2,1,0:T(8,128)(2,1)S(1)}, u32[]{:S(2)}, u32[]{:S(2)}) collective-permute-start(bf16[2,256,128]{2,1,0:T(8,128)(2,1)S(1)} %get-tuple-element.28), channel_id=1, source_target_pairs={{0,2},{1,3},{2,0},{3,1},{4,6},{5,7},{6,4},{7,5},{8,10},{9,11},{10,... | collective-permute-start | bytes 393224 | tf_op jit(solution)/shard_map/ppermute | solution.py:204
  27.7 12.9 %collective-permute-start.17 = (bf16[2,256,128]{2,1,0:T(8,128)(2,1)S(1)}, bf16[2,256,128]{2,1,0:T(8,128)(2,1)S(1)}, u32[]{:S(2)}, u32[]{:S(2)}) collective-permute-start(bf16[2,256,128]{2,1,0:T(8,128)(2,1)S(1)} %get-tuple-element.38), channel_id=1, source_target_pairs={{0,4},{1,5},{2,6},{3,7},{4,0},{5,1},{6,2},{7,3},{8,12},{9,13},{10,... | collective-permute-start | bytes 393224 | tf_op jit(solution)/shard_map/ppermute | solution.py:204
  29.2 11.4 %collective-permute-start.18 = (bf16[2,256,128]{2,1,0:T(8,128)(2,1)S(1)}, bf16[2,256,128]{2,1,0:T(8,128)(2,1)S(1)}, u32[]{:S(2)}, u32[]{:S(2)}) collective-permute-start(bf16[2,256,128]{2,1,0:T(8,128)(2,1)S(1)} %get-tuple-element.39), channel_id=1, source_target_pairs={{0,6},{1,7},{2,4},{3,5},{4,2},{5,3},{6,0},{7,1},{8,14},{9,15},{10,... | collective-permute-start | bytes 393224 | tf_op jit(solution)/shard_map/ppermute | solution.py:204
  33.6 7.0 %collective-permute-start.16 = (bf16[1,256,256]{2,1,0:T(8,128)(2,1)S(1)}, bf16[1,256,256]{2,1,0:T(8,128)(2,1)S(1)}, u32[]{:S(2)}, u32[]{:S(2)}) collective-permute-start(bf16[1,256,256]{2,1,0:T(8,128)(2,1)S(1)} %get-tuple-element.35), channel_id=1, source_target_pairs={{0,8},{8,0},{16,24},{24,16},{1,9},{9,1},{17,25},{25,17},{2,10},{10... | collective-permute-start | bytes 393224 | tf_op jit(solution)/shard_map/ppermute | solution.py:201
  34.3 6.3 %collective-permute-start.15 = (bf16[1,256,256]{2,1,0:T(8,128)(2,1)S(1)}, bf16[1,256,256]{2,1,0:T(8,128)(2,1)S(1)}, u32[]{:S(2)}, u32[]{:S(2)}) collective-permute-start(bf16[1,256,256]{2,1,0:T(8,128)(2,1)S(1)} %get-tuple-element.31), channel_id=1, source_target_pairs={{0,16},{8,24},{16,0},{24,8},{1,17},{9,25},{17,1},{25,9},{2,18},{10... | collective-permute-start | bytes 393224 | tf_op jit(solution)/shard_map/ppermute | solution.py:201

commit v4 on v3

--- a/solution.py
+++ b/solution.py
@@ -94,34 +94,57 @@
             denom[slot, pair] = occ + base
 
 
-def products(n_chip, *refs):
-    denom, ints_own, ints_x, ints_y, ints_xy, ints_yx = refs[:6]
-    mine = refs[6 : 6 + n_chip]
-    other = refs[6 + n_chip : 6 + 2 * n_chip]
-    keep_x, send_x, keep_y, send_y, grad_mine, grad_other = refs[6 + 2 * n_chip : 12 + 2 * n_chip]
-    amp_full, ints_full = refs[12 + 2 * n_chip :]
+def all_rows(own, near_x, near_y, far_xy, far_yx, full):
+    half = own.shape[0] // 2
+    block_d = own.shape[1]
+    row_pos = lax.axis_index("row")
+    for mask, block in ((0, own), (X_MASK, near_x), (Y_MASK, near_y)):
+        at = pl.multiple_of((row_pos ^ mask) * block_d, block_d)
+        full[:, pl.ds(at, block_d), :] = block[...]
+    at = pl.multiple_of((row_pos ^ (X_MASK ^ Y_MASK)) * block_d, block_d)
+    full[:half, pl.ds(at, block_d), :] = far_xy[...]
+    full[half:, pl.ds(at, block_d), :] = far_yx[...]
+
+
+def products(
+    denom,
+    ints_full,
+    near,
+    across,
+    far,
+    other_near,
+    other_across,
+    other_far,
+    keep_x,
+    send_x,
+    keep_y,
+    send_y,
+    grad_mine,
+    grad_other,
+    amp_full,
+):
     n_pair, block_c, width = amp_full.shape
     n_i, _, tile = ints_full.shape
     half = n_i // 2
-    sub_d = mine[0].shape[2]
-    block_d = ints_own.shape[1]
+    n_chip, _, _, sub_d = grad_mine.shape
+    block_d = keep_x.shape[2]
     row_pos = lax.axis_index("row")
     col_pos = lax.axis_index("col")
     chip_pos = col_pos // CORES
     core_pos = col_pos % CORES
     both = X_MASK ^ Y_MASK
-    for mask, block in ((0, ints_own), (X_MASK, ints_x), (Y_MASK, ints_y)):
-        at = pl.multiple_of((row_pos ^ mask) * block_d, block_d)
-        ints_full[:, pl.ds(at, block_d), :] = block[...]
-    at = pl.multiple_of((row_pos ^ both) * block_d, block_d)
-    ints_full[:half, pl.ds(at, block_d), :] = ints_xy[...]
-    ints_full[half:, pl.ds(at, block_d), :] = ints_yx[...]
-    for step in range(n_chip):
+    blocks = (
+        (0, near.at[0], other_near.at[0]),
+        (1, near.at[1], other_near.at[1]),
+        (2, far, other_far),
+        (3, across, other_across),
+    )
+    for step, mine, other in blocks:
         base_d = (chip_pos ^ step) * (CORES * sub_d)
         at_mine = pl.multiple_of(base_d + core_pos * sub_d, sub_d)
         at_other = pl.multiple_of(base_d + (1 - core_pos) * sub_d, sub_d)
-        amp_full[:, :, pl.ds(at_mine, sub_d)] = mine[step][...]
-        amp_full[:, :, pl.ds(at_other, sub_d)] = other[step][...]
+        amp_full[:, :, pl.ds(at_mine, sub_d)] = mine[...]
+        amp_full[:, :, pl.ds(at_other, sub_d)] = other[...]
 
     scaled = []
     for slot in range(n_i):
@@ -223,38 +246,44 @@
         out_shape=shape((n_i, n_pair, block_c, tile), f32),
         in_specs=[smem] * 5 + [vmem],
         out_specs=vmem,
-        compiler_params=room(8),
+        compiler_params=room(4),
         name="denominators",
     )(i_list, pairs, vir_offsets, occ_energy, vir_energy, vir_energy.reshape(-1, LANES))
-    mine = [amplitudes] + [over_chips(amplitudes, step) for step in range(1, n_chip)]
+    across, beside, far = [over_chips(amplitudes, step) for step in (3, 1, 2)]
     ints_x, ints_y = over_row(integrals, X_MASK), over_row(integrals, Y_MASK)
     ints_own = flat(integrals)
     ints_y, denom = lax.optimization_barrier((ints_y, denom))
     ints_xy, ints_yx = over_row(ints_x[:half], Y_MASK), over_row(ints_y[half:], X_MASK)
     flat_x, flat_y = flat(ints_x), flat(ints_y)
-    other = [over_cores(value) for value in mine]
+    near = jnp.stack([amplitudes, beside])
+    other_near, other_across, other_far = over_cores(near), over_cores(across), over_cores(far)
+    ints_full = pl.pallas_call(
+        all_rows,
+        out_shape=shape((n_i, width, tile), bf16),
+        in_specs=[vmem] * 5,
+        out_specs=vmem,
+        compiler_params=room(6),
+        name="all_rows",
+    )(ints_own, flat_x, flat_y, flat(ints_xy), flat(ints_yx))
     dens_shape = (2, half, block_d, tile)
     grad_shape = (n_chip, n_pair, block_c, sub_d)
     keep_x, send_x, keep_y, send_y, grad_mine, grad_other = pl.pallas_call(
-        functools.partial(products, n_chip),
+        products,
         out_shape=[shape(dens_shape, f32), shape(dens_shape, bf16)] * 2
         + [shape(grad_shape, f32), shape(grad_shape, bf16)],
-        in_specs=[vmem] * (6 + 2 * n_chip),
+        in_specs=[vmem] * 8,
         out_specs=[vmem] * 6,
-        scratch_shapes=[
-            pltpu.VMEM((n_pair, block_c, width), bf16),
-            pltpu.VMEM((n_i, width, tile), bf16),
-        ],
-        compiler_params=room(36),
+        scratch_shapes=[pltpu.VMEM((n_pair, block_c, width), bf16)],
+        compiler_params=room(14),
         name="products",
-    )(denom, ints_own, flat_x, flat_y, flat(ints_xy), flat(ints_yx), *mine, *other)
+    )(denom, ints_full, near, across, far, other_near, other_across, other_far)
     block = (n_pair, block_c, sub_d)
     grads = pl.pallas_call(
         functools.partial(core_sums, n_chip),
         out_shape=[shape(block, f32 if step == 0 else bf16) for step in range(n_chip)],
         in_specs=[vmem] * 2,
         out_specs=[vmem] * n_chip,
-        compiler_params=room(16),
+        compiler_params=room(6),
         name="core_sums",
     )(grad_mine, over_cores(grad_other))
 
@@ -264,7 +293,7 @@
             out_shape=[shape(dens_shape[1:], f32), shape(dens_shape[1:], bf16)],
             in_specs=[vmem] * 2,
             out_specs=[vmem] * 2,
-            compiler_params=room(8),
+            compiler_params=room(4),
             name="row_sums",
         )(keep, received)
 
@@ -279,7 +308,7 @@
         out_shape=[shape((n_i, block_d, width_b, width_a), bf16), shape(block, bf16)],
         in_specs=[vmem] * (4 + n_chip),
         out_specs=[vmem] * 2,
-        compiler_params=room(16),
+        compiler_params=room(6),
         name="results",
     )(own_x, last_x, own_y, last_y, grads[0], *grad_parts)
     return density, amp_grad
@@ -296,8 +325,7 @@
             and sub_d % LANES == 0
             and block_c % LANES == 0
             and block_d % LANES == 0
-            and n_row == 4
-            and n_col & (n_col - 1) == 0
+            and (n_row, n_col) == (4, 4 * CORES)
             and args[6].shape[0] % 2 == 0
         )
         if whole_tiles:

time: 41.6 us -> 40.8 us (0.981)
  waiting for transfers between devices: 15 us -> 11.6 us
  local copies, waits for them, and re-layouts: 0.99 us -> 2.1 us
  other arithmetic: 0 us -> 0.99 us
  starting transfers between devices: 20.6 us -> 21.1 us
    ppermute x6, waiting for transfers between devices: 11.2 us -> 9.05 us  [over_chips(): lax.ppermute(value, 'col', [(k, k ^ CORES * mask) for k in range(n_col)])]
    ppermute x6, starting transfers between devices: 9.34 us -> 10.7 us  [over_chips(): lax.ppermute(value, 'col', [(k, k ^ CORES * mask) for k in range(n_col)])]
    ppermute x8, starting transfers between devices: 10.5 us -> 9.38 us  [over_row(): return lax.ppermute(value, 'row', [(k, k ^ mask) for k in range(n_row)])]
    ppermute x5 -> x4, waiting for transfers between devices: 1.23 us -> 0.19 us  [over_cores(): return lax.ppermute(value, 'col', [(k, k ^ 1) for k in range(n_col)])]
    another operation x0 -> x1, other arithmetic: none -> 0.99 us  [exchanged(): near = jnp.stack([amplitudes, beside])]
    slice x1, local copies, waits for them, and re-layouts: 0.09 us -> 0.75 us  [exchanged(): ints_y[half:]]
    unnamed x14 -> x12, local copies, waits for them, and re-layouts: 0.11 us -> 0.58 us
    ppermute x5 -> x4, starting transfers between devices: 0.83 us -> 0.97 us  [over_cores(): return lax.ppermute(value, 'col', [(k, k ^ 1) for k in range(n_col)])]
  transfers between devices with their start and end apart: 19 -> 18, of which waited for: 10 -> 6; matrix products, arithmetic and copies ran while one was open for 2% -> 6% of each run, Pallas kernels for 2% -> 3%
where the time goes in v4:
time: 40.8 us; the launch traced here: 40.6 us
  starting transfers between devices  21.1 us (52%)
  waiting for transfers between devices  11.6 us (28%)
  Pallas kernels  4.06 us (10%)
  local copies, waits for them, and re-layouts  2.1 us (5%)
  other arithmetic  0.99 us (2%)
  between operations  0.82 us (2%)
    ppermute x6, starting transfers between devices, over_chips(): lax.ppermute(value, 'col', [(k, k ^ CORES * mask) for k in range(n_col)])  10.7 us
    ppermute x8, starting transfers between devices, over_row(): return lax.ppermute(value, 'row', [(k, k ^ mask) for k in range(n_row)])  9.38 us
    ppermute x6, waiting for transfers between devices, over_chips(): lax.ppermute(value, 'col', [(k, k ^ CORES * mask) for k in range(n_col)])  9.05 us
    ppermute x8, waiting for transfers between devices, over_row(): return lax.ppermute(value, 'row', [(k, k ^ mask) for k in range(n_row)])  2.34 us
    pallas_call x1, Pallas kernels, exchanged(): pl.pallas_call(products, out_shape=[shape(dens_shape, f32), shape(dens_sh...  2.2 us
    another operation x1, other arithmetic, exchanged(): near = jnp.stack([amplitudes, beside])  0.99 us
    ppermute x4, starting transfers between devices, over_cores(): return lax.ppermute(value, 'col', [(k, k ^ 1) for k in range(n_col)])  0.97 us
  transfers between devices with their start and end apart: 18, of which 6 were waited for; matrix products, arithmetic and copies ran while one was open for 6% of the time, Pallas kernels for 3%

profile of v4, /device:TPU:0, one launch (start us, length us, event | category | flops | bytes accessed | tf_op | source)
XLA Modules:
  0.0 40.6 jit_solution(9931357417126469623)
XLA Ops:
  0.6 3.1 %collective-permute-start.4 = (bf16[2,256,128]{2,1,0:T(8,128)(2,1)}, bf16[2,256,128]{2,1,0:T(8,128)(2,1)S(1)}, u32[]{:S(2)}, u32[]{:S(2)}) collective-permute-start(bf16[2,256,128]{2,1,0:T(8,128)(2,1)} %param.12), channel_id=1, source_target_pairs={{0,2},{1,3},{2,0},{3,1},{4,6},{5,7},{6,4},{7,5},{8,10},{9,11},{10,... | collective-permute-start | bytes 393224 | tf_op jit(solution)/shard_map/ppermute | solution.py:227
  3.7 1.5 %collective-permute-start.1 = (bf16[2,256,2,128]{3,2,1,0:T(2,128)(2,1)}, bf16[2,256,2,128]{3,2,1,0:T(2,128)(2,1)S(1)}, u32[]{:S(2)}, u32[]{:S(2)}) collective-permute-start(bf16[2,256,2,128]{3,2,1,0:T(2,128)(2,1)} %param.13), channel_id=1, source_target_pairs={{0,8},{8,0},{16,24},{24,16},{1,9},{9,1},{17,25},{25,17},{2,10},{10... | collective-permute-start | bytes 786440 | tf_op jit(solution)/shard_map/ppermute | solution.py:224
  5.2 1.5 %collective-permute-start = (bf16[2,256,2,128]{3,2,1,0:T(2,128)(2,1)}, bf16[2,256,2,128]{3,2,1,0:T(2,128)(2,1)S(1)}, u32[]{:S(2)}, u32[]{:S(2)}) collective-permute-start(bf16[2,256,2,128]{3,2,1,0:T(2,128)(2,1)} %param.13), channel_id=1, source_target_pairs={{0,16},{8,24},{16,0},{24,8},{1,17},{9,25},{17,1},{25,9},{2,18},{10... | collective-permute-start | bytes 786440 | tf_op jit(solution)/shard_map/ppermute | solution.py:224
  6.7 2.6 %collective-permute-start.6 = (bf16[2,256,128]{2,1,0:T(8,128)(2,1)}, bf16[2,256,128]{2,1,0:T(8,128)(2,1)S(1)}, u32[]{:S(2)}, u32[]{:S(2)}) collective-permute-start(bf16[2,256,128]{2,1,0:T(8,128)(2,1)} %param.12), channel_id=1, source_target_pairs={{0,4},{1,5},{2,6},{3,7},{4,0},{5,1},{6,2},{7,3},{8,12},{9,13},{10,... | collective-permute-start | bytes 393224 | tf_op jit(solution)/shard_map/ppermute | solution.py:227
  9.3 0.2 collective-permute-start.5
  9.5 0.0 collective-permute-done.4
  9.6 1.0 %pad_maximum_fusion.near = bf16[2,2,256,128]{3,2,1,0:T(8,128)(2,1)S(1)} fusion(bf16[1,2,256,128]{3,2,1,0:T(8,128)(2,1)S(1)} %bitcast.5, bf16[1,2,256,128]{3,2,1,0:T(8,128)(2,1)} %bitcast.4), kind=kLoop, calls=%fused_computation | loop fusion | flops 131072 | bytes 524288 | tf_op jit(solution)/shard_map/stack | solution.py:258
  10.5 0.0 copy-start.1
  10.6 0.0 copy-start.2
  10.6 0.1 collective-permute-start.7
  10.7 0.5 %copy-done.1 = s32[2,2]{1,0:T(2,128)S(1)} copy-done((s32[2,2]{1,0:T(2,128)S(1)}, s32[2,2]{1,0:T(2,128)}, u32[]{:S(2)}) %copy-start.1) | copy-done | bytes 40
  11.2 0.8 %denominators.1.denom = f32[2,2,256,256]{3,2,1,0:T(8,128)S(1)} custom-call(s32[2]{0:T(128)S(1)} %copy-done.2, s32[2,2]{1,0:T(2,128)S(1)} %copy-done.1, s32[2]{0:T(128)S(1)} %copy-done.3, f32[128]{0:T(128)S(1)} %copy-done.4, f32[1024]{0:T(1024)S(1)} %copy-done, f32[8,128]{1,0:T(8,128)S(1)} %bitcast.3), custom_call_target="tpu_custom_call" | custom-call | tf_op jit(solution)/shard_map/denominators/pallas_call | solution.py:244
  12.0 0.0 copy-start.5
  12.0 0.1 slice.8
  12.1 1.2 %collective-permute-start.2 = (bf16[1,256,2,128]{3,2,1,0:T(2,128)(2,1)S(1)}, bf16[1,256,2,128]{3,2,1,0:T(2,128)(2,1)S(1)}, u32[]{:S(2)}, u32[]{:S(2)}) collective-permute-start(bf16[1,256,2,128]{3,2,1,0:T(2,128)(2,1)S(1)} %slice.8), channel_id=1, source_target_pairs={{0,16},{8,24},{16,0},{24,8},{1,17},{9,25},{17,1},{25,9},{2,18},{10... | collective-permute-start | bytes 393224 | tf_op jit(solution)/shard_map/ppermute | solution.py:224
  13.4 0.7 %slice.7 = bf16[1,256,2,128]{3,2,1,0:T(2,128)(2,1)} slice(bf16[2,256,2,128]{3,2,1,0:T(2,128)(2,1)S(1)} %collective-permute-done), slice={[1:2], [0:256], [0:2], [0:128]} | slice | bytes 262144 | tf_op jit(solution)/shard_map/slice | solution.py:256
  14.1 1.5 %collective-permute-start.3 = (bf16[1,256,2,128]{3,2,1,0:T(2,128)(2,1)}, bf16[1,256,2,128]{3,2,1,0:T(2,128)(2,1)S(1)}, u32[]{:S(2)}, u32[]{:S(2)}) collective-permute-start(bf16[1,256,2,128]{3,2,1,0:T(2,128)(2,1)} %slice.7), channel_id=1, source_target_pairs={{0,8},{8,0},{16,24},{24,16},{1,9},{9,1},{17,25},{25,17},{2,10},{10... | collective-permute-start | bytes 393224 | tf_op jit(solution)/shard_map/ppermute | solution.py:224
  15.6 2.8 %collective-permute-done.6.far = bf16[2,256,128]{2,1,0:T(8,128)(2,1)S(1)} collective-permute-done((bf16[2,256,128]{2,1,0:T(8,128)(2,1)}, bf16[2,256,128]{2,1,0:T(8,128)(2,1)S(1)}, u32[]{:S(2)}, u32[]{:S(2)}) %collective-permute-start.6) | collective-permute-done | bytes 131104 | tf_op jit(solution)/shard_map/ppermute | solution.py:227
  18.4 0.5 %collective-permute-start.8 = (bf16[2,256,128]{2,1,0:T(8,128)(2,1)S(1)}, bf16[2,256,128]{2,1,0:T(8,128)(2,1)S(1)}, u32[]{:S(2)}, u32[]{:S(2)}) collective-permute-start(bf16[2,256,128]{2,1,0:T(8,128)(2,1)S(1)} %collective-permute-done.5.across), channel_id=1, source_target_pairs={{0,1},{1,0},{2,3},{3,2},{4,5},{5,4},{6,7},{7,6},{8,9},{9,8},{10,11... | collective-permute-start | bytes 393224 | tf_op jit(solution)/shard_map/ppermute | solution.py:230
  18.9 0.2 reshape.23.own
  19.1 0.2 reshape.25.near_y
  19.2 0.2 reshape.24.near_x
  19.4 0.1 reshape.26.far_xy
  19.5 0.0 collective-permute-done.3
  19.5 0.1 reshape.27.far_yx
  19.6 0.1 all_rows.1.ints_full
  19.7 0.0 collective-permute-done.9.other_far
  19.7 0.2 collective-permute-done.8.other_across
  19.9 0.0 collective-permute-done.7.other_near
  19.9 2.2 %products.1 = (f32[2,1,256,256]{3,2,1,0:T(8,128)S(1)}, bf16[2,1,256,256]{3,2,1,0:T(8,128)(2,1)S(1)}, f32[2,1,256,256]{3,2,1,0:T(8,128)S(1)}, bf16[2,1,256,256]{3...) custom-call(f32[2,2,256,256]{3,2,1,0:T(8,128)S(1)} %denominators.1.denom, ...), custom_call_target="tpu_custom_call" | custom-call | tf_op jit(solution)/shard_map/products/pallas_call | solution.py:270
  22.1 0.4 collective-permute-start.12
  22.5 1.1 %collective-permute-start.10 = (bf16[2,1,256,256]{3,2,1,0:T(8,128)(2,1)S(1)}, bf16[2,1,256,256]{3,2,1,0:T(8,128)(2,1)S(1)}, u32[]{:S(2)}, u32[]{:S(2)}) collective-permute-start(bf16[2,1,256,256]{3,2,1,0:T(8,128)(2,1)S(1)} %get-tuple-element.24), channel_id=1, source_target_pairs={{0,8},{8,0},{16,24},{24,16},{1,9},{9,1},{17,25},{25,17},{2,10},{10... | collective-permute-start | bytes 786440 | tf_op jit(solution)/shard_map/ppermute | solution.py:224
  23.6 0.9 %collective-permute-start.11 = (bf16[2,1,256,256]{3,2,1,0:T(8,128)(2,1)S(1)}, bf16[2,1,256,256]{3,2,1,0:T(8,128)(2,1)S(1)}, u32[]{:S(2)}, u32[]{:S(2)}) collective-permute-start(bf16[2,1,256,256]{3,2,1,0:T(8,128)(2,1)S(1)} %get-tuple-element.25), channel_id=1, source_target_pairs={{0,16},{8,24},{16,0},{24,8},{1,17},{9,25},{17,1},{25,9},{2,18},{10... | collective-permute-start | bytes 786440 | tf_op jit(solution)/shard_map/ppermute | solution.py:224
  24.5 0.0 collective-permute-done.12.received
  24.5 0.1 core_sums.1
  24.6 2.3 %collective-permute-start.13 = (bf16[2,256,128]{2,1,0:T(8,128)(2,1)S(1)}, bf16[2,256,128]{2,1,0:T(8,128)(2,1)S(1)}, u32[]{:S(2)}, u32[]{:S(2)}) collective-permute-start(bf16[2,256,128]{2,1,0:T(8,128)(2,1)S(1)} %get-tuple-element.28), channel_id=1, source_target_pairs={{0,2},{1,3},{2,0},{3,1},{4,6},{5,7},{6,4},{7,5},{8,10},{9,11},{10,... | collective-permute-start | bytes 393224 | tf_op jit(solution)/shard_map/ppermute | solution.py:227
  26.9 1.1 %collective-permute-start.16 = (bf16[2,256,128]{2,1,0:T(8,128)(2,1)S(1)}, bf16[2,256,128]{2,1,0:T(8,128)(2,1)S(1)}, u32[]{:S(2)}, u32[]{:S(2)}) collective-permute-start(bf16[2,256,128]{2,1,0:T(8,128)(2,1)S(1)} %get-tuple-element.38), channel_id=1, source_target_pairs={{0,4},{1,5},{2,6},{3,7},{4,0},{5,1},{6,2},{7,3},{8,12},{9,13},{10,... | collective-permute-start | bytes 393224 | tf_op jit(solution)/shard_map/ppermute | solution.py:227
  28.0 1.4 %collective-permute-start.17 = (bf16[2,256,128]{2,1,0:T(8,128)(2,1)S(1)}, bf16[2,256,128]{2,1,0:T(8,128)(2,1)S(1)}, u32[]{:S(2)}, u32[]{:S(2)}) collective-permute-start(bf16[2,256,128]{2,1,0:T(8,128)(2,1)S(1)} %get-tuple-element.39), channel_id=1, source_target_pairs={{0,6},{1,7},{2,4},{3,5},{4,2},{5,3},{6,0},{7,1},{8,14},{9,15},{10,... | collective-permute-start | bytes 393224 | tf_op jit(solution)/shard_map/ppermute | solution.py:227
  29.4 1.5 %collective-permute-done.10.received = bf16[2,1,256,256]{3,2,1,0:T(8,128)(2,1)S(1)} collective-permute-done((bf16[2,1,256,256]{3,2,1,0:T(8,128)(2,1)S(1)}, bf16[2,1,256,256]{3,2,1,0:T(8,128)(2,1)S(1)}, u32[]{:S(2)}, u32[]{:S(2)}) %collective-permute-start.10) | collective-permute-done | bytes 262176 | tf_op jit(solution)/shard_map/ppermute | solution.py:224
  30.9 0.8 %collective-permute-done.11.received = bf16[2,1,256,256]{3,2,1,0:T(8,128)(2,1)S(1)} collective-permute-done((bf16[2,1,256,256]{3,2,1,0:T(8,128)(2,1)S(1)}, bf16[2,1,256,256]{3,2,1,0:T(8,128)(2,1)S(1)}, u32[]{:S(2)}, u32[]{:S(2)}) %collective-permute-start.11) | collective-permute-done | bytes 262176 | tf_op jit(solution)/shard_map/ppermute | solution.py:224
  31.7 0.9 %collective-permute-done.13.refs_0_ = bf16[2,256,128]{2,1,0:T(8,128)(2,1)S(1)} collective-permute-done((bf16[2,256,128]{2,1,0:T(8,128)(2,1)S(1)}, bf16[2,256,128]{2,1,0:T(8,128)(2,1)S(1)}, u32[]{:S(2)}, u32[]{:S(2)}) %collective-permute-start.13) | collective-permute-done | bytes 131104 | tf_op jit(solution)/shard_map/ppermute | solution.py:227
  32.6 0.3 collective-permute-start.15
  33.0 1.3 %collective-permute-start.14 = (bf16[1,256,256]{2,1,0:T(8,128)(2,1)S(1)}, bf16[1,256,256]{2,1,0:T(8,128)(2,1)S(1)}, u32[]{:S(2)}, u32[]{:S(2)}) collective-permute-start(bf16[1,256,256]{2,1,0:T(8,128)(2,1)S(1)} %get-tuple-element.31), channel_id=1, source_target_pairs={{0,16},{8,24},{16,0},{24,8},{1,17},{9,25},{17,1},{25,9},{2,18},{10... | collective-permute-start | bytes 393224 | tf_op jit(solution)/shard_map/ppermute | solution.py:224
  34.4 5.4 %collective-permute-done.16.refs_1_ = bf16[2,256,128]{2,1,0:T(8,128)(2,1)S(1)} collective-permute-done((bf16[2,256,128]{2,1,0:T(8,128)(2,1)S(1)}, bf16[2,256,128]{2,1,0:T(8,128)(2,1)S(1)}, u32[]{:S(2)}, u32[]{:S(2)}) %collective-permute-start.16) | collective-permute-done | bytes 131104 | tf_op jit(solution)/shard_map/ppermute | solution.py:227
  39.8 0.0 collective-permute-done.17.refs_2_
  39.8 0.0 collective-permute-done.15.last_y
  39.8 0.0 collective-permute-done.14.last_x
  39.8 0.8 %results.1 = (bf16[2,256,2,128]{3,2,1,0:T(2,128)(2,1)}, bf16[2,256,128]{2,1,0:T(8,128)(2,1)}) custom-call(f32[1,256,256]{2,1,0:T(8,128)S(1)} %get-tuple-element.30.own_x, bf16[1,256,256]{2,1,0:T(8,128)(2,1)S(1)} %collective-permute-done.14.last_x, f32[1,256,256]{2,1,0:T(8,128)S(1)} %get-tuple-element.34.own_y, ...), custom_call_target="tpu_custom_call" | custom-call | tf_op jit(solution)/shard_map/results/pallas_call | solution.py:306
  (15 shorter events, 0.1 us)
Async XLA Ops:
  0.6 8.9 %collective-permute-start.4 = (bf16[2,256,128]{2,1,0:T(8,128)(2,1)}, bf16[2,256,128]{2,1,0:T(8,128)(2,1)S(1)}, u32[]{:S(2)}, u32[]{:S(2)}) collective-permute-start(bf16[2,256,128]{2,1,0:T(8,128)(2,1)} %param.12), channel_id=1, source_target_pairs={{0,2},{1,3},{2,0},{3,1},{4,6},{5,7},{6,4},{7,5},{8,10},{9,11},{10,... | collective-permute-start | bytes 393224 | tf_op jit(solution)/shard_map/ppermute | solution.py:227
  3.7 8.3 %collective-permute-start.1 = (bf16[2,256,2,128]{3,2,1,0:T(2,128)(2,1)}, bf16[2,256,2,128]{3,2,1,0:T(2,128)(2,1)S(1)}, u32[]{:S(2)}, u32[]{:S(2)}) collective-permute-start(bf16[2,256,2,128]{3,2,1,0:T(2,128)(2,1)} %param.13), channel_id=1, source_target_pairs={{0,8},{8,0},{16,24},{24,16},{1,9},{9,1},{17,25},{25,17},{2,10},{10... | collective-permute-start | bytes 786440 | tf_op jit(solution)/shard_map/ppermute | solution.py:224
  5.2 8.2 %collective-permute-start = (bf16[2,256,2,128]{3,2,1,0:T(2,128)(2,1)}, bf16[2,256,2,128]{3,2,1,0:T(2,128)(2,1)S(1)}, u32[]{:S(2)}, u32[]{:S(2)}) collective-permute-start(bf16[2,256,2,128]{3,2,1,0:T(2,128)(2,1)} %param.13), channel_id=1, source_target_pairs={{0,16},{8,24},{16,0},{24,8},{1,17},{9,25},{17,1},{25,9},{2,18},{10... | collective-permute-start | bytes 786440 | tf_op jit(solution)/shard_map/ppermute | solution.py:224
  6.7 11.6 %collective-permute-start.6 = (bf16[2,256,128]{2,1,0:T(8,128)(2,1)}, bf16[2,256,128]{2,1,0:T(8,128)(2,1)S(1)}, u32[]{:S(2)}, u32[]{:S(2)}) collective-permute-start(bf16[2,256,128]{2,1,0:T(8,128)(2,1)} %param.12), channel_id=1, source_target_pairs={{0,4},{1,5},{2,6},{3,7},{4,0},{5,1},{6,2},{7,3},{8,12},{9,13},{10,... | collective-permute-start | bytes 393224 | tf_op jit(solution)/shard_map/ppermute | solution.py:227
  9.3 9.1 %collective-permute-start.5 = (bf16[2,256,128]{2,1,0:T(8,128)(2,1)}, bf16[2,256,128]{2,1,0:T(8,128)(2,1)S(1)}, u32[]{:S(2)}, u32[]{:S(2)}) collective-permute-start(bf16[2,256,128]{2,1,0:T(8,128)(2,1)} %param.12), channel_id=1, source_target_pairs={{0,6},{1,7},{2,4},{3,5},{4,2},{5,3},{6,0},{7,1},{8,14},{9,15},{10,... | collective-permute-start | bytes 393224 | tf_op jit(solution)/shard_map/ppermute | solution.py:227
  9.5 1.1 %copy-start = (f32[1024]{0:T(1024)S(1)}, f32[1024]{0:T(1024)}, u32[]{:S(2)}) copy-start(f32[1024]{0:T(1024)} %vir_smem.1) | copy-start | bytes 12292
  9.5 1.1 %copy-start.3 = (s32[2]{0:T(128)S(1)}, s32[2]{0:T(128)}, u32[]{:S(2)}) copy-start(s32[2]{0:T(128)} %vir_offsets.1) | copy-start | bytes 28
  9.6 1.1 %copy-start.4 = (f32[128]{0:T(128)S(1)}, f32[128]{0:T(128)}, u32[]{:S(2)}) copy-start(f32[128]{0:T(128)} %occ_energy.1) | copy-start | bytes 1540
  10.5 0.7 %copy-start.1 = (s32[2,2]{1,0:T(2,128)S(1)}, s32[2,2]{1,0:T(2,128)}, u32[]{:S(2)}) copy-start(s32[2,2]{1,0:T(2,128)} %pairs.1) | copy-start | bytes 52
  10.6 0.7 %copy-start.2 = (s32[2]{0:T(128)S(1)}, s32[2]{0:T(128)}, u32[]{:S(2)}) copy-start(s32[2]{0:T(128)} %i_list.1) | copy-start | bytes 28
  10.6 9.3 %collective-permute-start.7 = (bf16[2,2,256,128]{3,2,1,0:T(8,128)(2,1)S(1)}, bf16[2,2,256,128]{3,2,1,0:T(8,128)(2,1)S(1)}, u32[]{:S(2)}, u32[]{:S(2)}) collective-permute-start(bf16[2,2,256,128]{3,2,1,0:T(8,128)(2,1)S(1)} %pad_maximum_fusion.near), channel_id=1, source_target_pairs={{0,1},{1,0},{2,3},{3,2},{4,5},{5,4},{6,7},{7,6},{8,9},{9,8},{10,11... | collective-permute-start | bytes 786440 | tf_op jit(solution)/shard_map/ppermute | solution.py:230
  12.0 6.9 %copy-start.5 = (bf16[2,256,2,128]{3,2,1,0:T(2,128)(2,1)S(1)}, bf16[2,256,2,128]{3,2,1,0:T(2,128)(2,1)}, u32[]{:S(2)}) copy-start(bf16[2,256,2,128]{3,2,1,0:T(2,128)(2,1)} %param.13) | copy-start | bytes 786436
  12.1 7.3 %collective-permute-start.2 = (bf16[1,256,2,128]{3,2,1,0:T(2,128)(2,1)S(1)}, bf16[1,256,2,128]{3,2,1,0:T(2,128)(2,1)S(1)}, u32[]{:S(2)}, u32[]{:S(2)}) collective-permute-start(bf16[1,256,2,128]{3,2,1,0:T(2,128)(2,1)S(1)} %slice.8), channel_id=1, source_target_pairs={{0,16},{8,24},{16,0},{24,8},{1,17},{9,25},{17,1},{25,9},{2,18},{10... | collective-permute-start | bytes 393224 | tf_op jit(solution)/shard_map/ppermute | solution.py:224
  14.1 5.4 %collective-permute-start.3 = (bf16[1,256,2,128]{3,2,1,0:T(2,128)(2,1)}, bf16[1,256,2,128]{3,2,1,0:T(2,128)(2,1)S(1)}, u32[]{:S(2)}, u32[]{:S(2)}) collective-permute-start(bf16[1,256,2,128]{3,2,1,0:T(2,128)(2,1)} %slice.7), channel_id=1, source_target_pairs={{0,8},{8,0},{16,24},{24,16},{1,9},{9,1},{17,25},{25,17},{2,10},{10... | collective-permute-start | bytes 393224 | tf_op jit(solution)/shard_map/ppermute | solution.py:224
  18.4 1.3 %collective-permute-start.9 = (bf16[2,256,128]{2,1,0:T(8,128)(2,1)S(1)}, bf16[2,256,128]{2,1,0:T(8,128)(2,1)S(1)}, u32[]{:S(2)}, u32[]{:S(2)}) collective-permute-start(bf16[2,256,128]{2,1,0:T(8,128)(2,1)S(1)} %collective-permute-done.6.far), channel_id=1, source_target_pairs={{0,1},{1,0},{2,3},{3,2},{4,5},{5,4},{6,7},{7,6},{8,9},{9,8},{10,11... | collective-permute-start | bytes 393224 | tf_op jit(solution)/shard_map/ppermute | solution.py:230
  18.4 1.5 %collective-permute-start.8 = (bf16[2,256,128]{2,1,0:T(8,128)(2,1)S(1)}, bf16[2,256,128]{2,1,0:T(8,128)(2,1)S(1)}, u32[]{:S(2)}, u32[]{:S(2)}) collective-permute-start(bf16[2,256,128]{2,1,0:T(8,128)(2,1)S(1)} %collective-permute-done.5.across), channel_id=1, source_target_pairs={{0,1},{1,0},{2,3},{3,2},{4,5},{5,4},{6,7},{7,6},{8,9},{9,8},{10,11... | collective-permute-start | bytes 393224 | tf_op jit(solution)/shard_map/ppermute | solution.py:230
  22.1 2.4 %collective-permute-start.12 = (bf16[4,2,256,128]{3,2,1,0:T(8,128)(2,1)S(1)}, bf16[4,2,256,128]{3,2,1,0:T(8,128)(2,1)S(1)}, u32[]{:S(2)}, u32[]{:S(2)}) collective-permute-start(bf16[4,2,256,128]{3,2,1,0:T(8,128)(2,1)S(1)} %get-tuple-element.27), channel_id=1, source_target_pairs={{0,1},{1,0},{2,3},{3,2},{4,5},{5,4},{6,7},{7,6},{8,9},{9,8},{10,11... | collective-permute-start | bytes 1572872 | tf_op jit(solution)/shard_map/ppermute | solution.py:230
  22.5 8.4 %collective-permute-start.10 = (bf16[2,1,256,256]{3,2,1,0:T(8,128)(2,1)S(1)}, bf16[2,1,256,256]{3,2,1,0:T(8,128)(2,1)S(1)}, u32[]{:S(2)}, u32[]{:S(2)}) collective-permute-start(bf16[2,1,256,256]{3,2,1,0:T(8,128)(2,1)S(1)} %get-tuple-element.24), channel_id=1, source_target_pairs={{0,8},{8,0},{16,24},{24,16},{1,9},{9,1},{17,25},{25,17},{2,10},{10... | collective-permute-start | bytes 786440 | tf_op jit(solution)/shard_map/ppermute | solution.py:224
  23.6 8.2 %collective-permute-start.11 = (bf16[2,1,256,256]{3,2,1,0:T(8,128)(2,1)S(1)}, bf16[2,1,256,256]{3,2,1,0:T(8,128)(2,1)S(1)}, u32[]{:S(2)}, u32[]{:S(2)}) collective-permute-start(bf16[2,1,256,256]{3,2,1,0:T(8,128)(2,1)S(1)} %get-tuple-element.25), channel_id=1, source_target_pairs={{0,16},{8,24},{16,0},{24,8},{1,17},{9,25},{17,1},{25,9},{2,18},{10... | collective-permute-start | bytes 786440 | tf_op jit(solution)/shard_map/ppermute | solution.py:224
  24.6 8.0 %collective-permute-start.13 = (bf16[2,256,128]{2,1,0:T(8,128)(2,1)S(1)}, bf16[2,256,128]{2,1,0:T(8,128)(2,1)S(1)}, u32[]{:S(2)}, u32[]{:S(2)}) collective-permute-start(bf16[2,256,128]{2,1,0:T(8,128)(2,1)S(1)} %get-tuple-element.28), channel_id=1, source_target_pairs={{0,2},{1,3},{2,0},{3,1},{4,6},{5,7},{6,4},{7,5},{8,10},{9,11},{10,... | collective-permute-start | bytes 393224 | tf_op jit(solution)/shard_map/ppermute | solution.py:227
  26.9 12.9 %collective-permute-start.16 = (bf16[2,256,128]{2,1,0:T(8,128)(2,1)S(1)}, bf16[2,256,128]{2,1,0:T(8,128)(2,1)S(1)}, u32[]{:S(2)}, u32[]{:S(2)}) collective-permute-start(bf16[2,256,128]{2,1,0:T(8,128)(2,1)S(1)} %get-tuple-element.38), channel_id=1, source_target_pairs={{0,4},{1,5},{2,6},{3,7},{4,0},{5,1},{6,2},{7,3},{8,12},{9,13},{10,... | collective-permute-start | bytes 393224 | tf_op jit(solution)/shard_map/ppermute | solution.py:227
  28.0 11.8 %collective-permute-start.17 = (bf16[2,256,128]{2,1,0:T(8,128)(2,1)S(1)}, bf16[2,256,128]{2,1,0:T(8,128)(2,1)S(1)}, u32[]{:S(2)}, u32[]{:S(2)}) collective-permute-start(bf16[2,256,128]{2,1,0:T(8,128)(2,1)S(1)} %get-tuple-element.39), channel_id=1, source_target_pairs={{0,6},{1,7},{2,4},{3,5},{4,2},{5,3},{6,0},{7,1},{8,14},{9,15},{10,... | collective-permute-start | bytes 393224 | tf_op jit(solution)/shard_map/ppermute | solution.py:227
  32.6 7.1 %collective-permute-start.15 = (bf16[1,256,256]{2,1,0:T(8,128)(2,1)S(1)}, bf16[1,256,256]{2,1,0:T(8,128)(2,1)S(1)}, u32[]{:S(2)}, u32[]{:S(2)}) collective-permute-start(bf16[1,256,256]{2,1,0:T(8,128)(2,1)S(1)} %get-tuple-element.35), channel_id=1, source_target_pairs={{0,8},{8,0},{16,24},{24,16},{1,9},{9,1},{17,25},{25,17},{2,10},{10... | collective-permute-start | bytes 393224 | tf_op jit(solution)/shard_map/ppermute | solution.py:224
  33.0 6.8 %collective-permute-start.14 = (bf16[1,256,256]{2,1,0:T(8,128)(2,1)S(1)}, bf16[1,256,256]{2,1,0:T(8,128)(2,1)S(1)}, u32[]{:S(2)}, u32[]{:S(2)}) collective-permute-start(bf16[1,256,256]{2,1,0:T(8,128)(2,1)S(1)} %get-tuple-element.31), channel_id=1, source_target_pairs={{0,16},{8,24},{16,0},{24,8},{1,17},{9,25},{17,1},{25,9},{2,18},{10... | collective-permute-start | bytes 393224 | tf_op jit(solution)/shard_map/ppermute | solution.py:224

commit v5 on v4

--- a/solution.py
+++ b/solution.py
@@ -69,7 +69,9 @@
 def denominators(
     i_list, pairs, vir_offsets, occ_energy, vir_smem, vir_rows, denom
 ):
-    n_i, n_pair, block_c, tile = denom.shape
+    n_i, n_pair = i_list.shape[0], pairs.shape[0]
+    block_c = denom.shape[0] // n_pair
+    tile = denom.shape[1] // n_i
     width_b = tile // LANES
     row_pos = lax.axis_index("row")
     col_pos = lax.axis_index("col")
@@ -91,30 +93,44 @@
                 + occ_energy[pairs[pair, 0]]
                 + occ_energy[pairs[pair, 1]]
             )
-            denom[slot, pair] = occ + base
+            rows = slice(pair * block_c, (pair + 1) * block_c)
+            denom[rows, slot * tile : (slot + 1) * tile] = occ + base
+
+
+def first_slots(whole, part):
+    part[...] = whole[: part.shape[0]]
+
+
+def last_slots(whole, part):
+    part[...] = whole[part.shape[0] :]
 
 
 def all_rows(own, near_x, near_y, far_xy, far_yx, full):
-    half = own.shape[0] // 2
-    block_d = own.shape[1]
+    n_i, block_d, tile = own.shape
+    half = n_i // 2
     row_pos = lax.axis_index("row")
-    for mask, block in ((0, own), (X_MASK, near_x), (Y_MASK, near_y)):
+    for mask, blocks in (
+        (0, (own,)),
+        (X_MASK, (near_x,)),
+        (Y_MASK, (near_y,)),
+        (X_MASK ^ Y_MASK, (far_xy, far_yx)),
+    ):
         at = pl.multiple_of((row_pos ^ mask) * block_d, block_d)
-        full[:, pl.ds(at, block_d), :] = block[...]
-    at = pl.multiple_of((row_pos ^ (X_MASK ^ Y_MASK)) * block_d, block_d)
-    full[:half, pl.ds(at, block_d), :] = far_xy[...]
-    full[half:, pl.ds(at, block_d), :] = far_yx[...]
+        for slot in range(n_i):
+            block = blocks[0] if slot < half else blocks[-1]
+            place = slot - half if len(blocks) > 1 and slot >= half else slot
+            full[pl.ds(at, block_d), slot * tile : (slot + 1) * tile] = block[place]
 
 
 def products(
     denom,
     ints_full,
-    near,
-    across,
+    ends,
     far,
-    other_near,
-    other_across,
+    beside,
+    other_ends,
     other_far,
+    other_beside,
     keep_x,
     send_x,
     keep_y,
@@ -123,68 +139,62 @@
     grad_other,
     amp_full,
 ):
-    n_pair, block_c, width = amp_full.shape
-    n_i, _, tile = ints_full.shape
-    half = n_i // 2
-    n_chip, _, _, sub_d = grad_mine.shape
-    block_d = keep_x.shape[2]
+    n_chip, n_pair, block_c, sub_d = grad_mine.shape
+    _, half, block_d, tile = keep_x.shape
     row_pos = lax.axis_index("row")
     col_pos = lax.axis_index("col")
     chip_pos = col_pos // CORES
     core_pos = col_pos % CORES
-    both = X_MASK ^ Y_MASK
     blocks = (
-        (0, near.at[0], other_near.at[0]),
-        (1, near.at[1], other_near.at[1]),
+        (0, ends.at[0], other_ends.at[0]),
+        (1, beside, other_beside),
         (2, far, other_far),
-        (3, across, other_across),
+        (3, ends.at[1], other_ends.at[1]),
     )
     for step, mine, other in blocks:
         base_d = (chip_pos ^ step) * (CORES * sub_d)
         at_mine = pl.multiple_of(base_d + core_pos * sub_d, sub_d)
         at_other = pl.multiple_of(base_d + (1 - core_pos) * sub_d, sub_d)
-        amp_full[:, :, pl.ds(at_mine, sub_d)] = mine[...]
-        amp_full[:, :, pl.ds(at_other, sub_d)] = other[...]
-
-    scaled = []
-    for slot in range(n_i):
         for pair in range(n_pair):
-            triples = jnp.dot(amp_full[pair], ints_full[slot], preferred_element_type=jnp.float32)
-            scaled.append((triples / denom[slot, pair]).astype(jnp.bfloat16))
+            rows = slice(pair * block_c, (pair + 1) * block_c)
+            amp_full[rows, pl.ds(at_mine, sub_d)] = mine[pair]
+            amp_full[rows, pl.ds(at_other, sub_d)] = other[pair]
+
+    triples = jnp.dot(amp_full[...], ints_full[...], preferred_element_type=jnp.float32)
+    scaled = (triples / denom[...]).astype(jnp.bfloat16)
 
     low = core_pos == 0
     for step in range(n_chip):
         at = pl.multiple_of((chip_pos ^ step) * (CORES * sub_d), CORES * sub_d)
-        for pair in range(n_pair):
-            total = None
-            for slot in range(n_i):
-                part = lax.dot_general(
-                    scaled[slot * n_pair + pair],
-                    ints_full[slot, pl.ds(at, CORES * sub_d), :],
-                    (((1,), (1,)), ((), ())),
-                    preferred_element_type=jnp.float32,
-                )
-                total = part if total is None else total + part
-            first, second = total[:, :sub_d], total[:, sub_d:]
-            grad_mine[step, pair] = jnp.where(low, first, second).astype(grad_mine.dtype)
-            grad_other[step, pair] = jnp.where(low, second, first).astype(grad_other.dtype)
-
-    plan = ((0, 0, keep_x, 0), (0, Y_MASK, keep_x, 1), (0, X_MASK, send_x, 0), (0, both, send_x, 1))
-    plan += ((1, 0, keep_y, 0), (1, X_MASK, keep_y, 1), (1, Y_MASK, send_y, 0), (1, both, send_y, 1))
-    for part_of, mask, out, place in plan:
+        total = lax.dot_general(
+            scaled,
+            ints_full[pl.ds(at, CORES * sub_d), :],
+            (((1,), (1,)), ((), ())),
+            preferred_element_type=jnp.float32,
+        ).reshape(n_pair, block_c, CORES * sub_d)
+        first, second = total[:, :, :sub_d], total[:, :, sub_d:]
+        grad_mine[step] = jnp.where(low, first, second).astype(grad_mine.dtype)
+        grad_other[step] = jnp.where(low, second, first).astype(grad_other.dtype)
+
+    both = X_MASK ^ Y_MASK
+    plan = (
+        (0, (keep_x, 0), (keep_y, 0)),
+        (X_MASK, (send_x, 0), (keep_y, 1)),
+        (Y_MASK, (keep_x, 1), (send_y, 0)),
+        (both, (send_x, 1), (send_y, 1)),
+    )
+    for mask, first, second in plan:
         at = pl.multiple_of((row_pos ^ mask) * block_d, block_d)
-        for k in range(half):
-            slot = part_of * half + k
-            total = None
-            for pair in range(n_pair):
-                part = lax.dot_general(
-                    amp_full[pair, :, pl.ds(at, block_d)],
-                    scaled[slot * n_pair + pair],
-                    (((0,), (0,)), ((), ())),
-                    preferred_element_type=jnp.float32,
-                )
-                total = part if total is None else total + part
-            out[place, k] = total.astype(out.dtype)
+        total = lax.dot_general(
+            amp_full[:, pl.ds(at, block_d)],
+            scaled,
+            (((0,), (0,)), ((), ())),
+            preferred_element_type=jnp.float32,
+        )
+        for part_of, (out, place) in enumerate((first, second)):
+            for k in range(half):
+                slot = part_of * half + k
+                out[place, k] = total[:, slot * tile : (slot + 1) * tile].astype(out.dtype)
 
 
 def results(own_x, last_x, own_y, last_y, own, *refs):
@@ -241,9 +251,20 @@
         return value.reshape(value.shape[:2] + (tile,))
 
     half = n_i // 2
+
+    def part_of(kernel, whole):
+        return pl.pallas_call(
+            kernel,
+            out_shape=shape((half, block_d, tile), bf16),
+            in_specs=[vmem],
+            out_specs=vmem,
+            compiler_params=room(4),
+            name=kernel.__name__,
+        )(whole)
+
     denom = pl.pallas_call(
         denominators,
-        out_shape=shape((n_i, n_pair, block_c, tile), f32),
+        out_shape=shape((n_pair * block_c, n_i * tile), f32),
         in_specs=[smem] * 5 + [vmem],
         out_specs=vmem,
         compiler_params=room(4),
@@ -252,19 +273,20 @@
     across, beside, far = [over_chips(amplitudes, step) for step in (3, 1, 2)]
     ints_x, ints_y = over_row(integrals, X_MASK), over_row(integrals, Y_MASK)
     ints_own = flat(integrals)
-    ints_y, denom = lax.optimization_barrier((ints_y, denom))
-    ints_xy, ints_yx = over_row(ints_x[:half], Y_MASK), over_row(ints_y[half:], X_MASK)
     flat_x, flat_y = flat(ints_x), flat(ints_y)
-    near = jnp.stack([amplitudes, beside])
-    other_near, other_across, other_far = over_cores(near), over_cores(across), over_cores(far)
+    ints_xy = over_row(part_of(first_slots, flat_x), Y_MASK)
+    ints_yx = over_row(part_of(last_slots, flat_y), X_MASK)
+    across, ints_own, denom = lax.optimization_barrier((across, ints_own, denom))
+    ends = jnp.stack([amplitudes, across])
+    other_ends, other_far, other_beside = over_cores(ends), over_cores(far), over_cores(beside)
     ints_full = pl.pallas_call(
         all_rows,
-        out_shape=shape((n_i, width, tile), bf16),
+        out_shape=shape((width, n_i * tile), bf16),
         in_specs=[vmem] * 5,
         out_specs=vmem,
         compiler_params=room(6),
         name="all_rows",
-    )(ints_own, flat_x, flat_y, flat(ints_xy), flat(ints_yx))
+    )(ints_own, flat_x, flat_y, ints_xy, ints_yx)
     dens_shape = (2, half, block_d, tile)
     grad_shape = (n_chip, n_pair, block_c, sub_d)
     keep_x, send_x, keep_y, send_y, grad_mine, grad_other = pl.pallas_call(
@@ -273,10 +295,10 @@
         + [shape(grad_shape, f32), shape(grad_shape, bf16)],
         in_specs=[vmem] * 8,
         out_specs=[vmem] * 6,
-        scratch_shapes=[pltpu.VMEM((n_pair, block_c, width), bf16)],
+        scratch_shapes=[pltpu.VMEM((n_pair * block_c, width), bf16)],
         compiler_params=room(14),
         name="products",
-    )(denom, ints_full, near, across, far, other_near, other_across, other_far)
+    )(denom, ints_full, ends, far, beside, other_ends, other_far, other_beside)
     block = (n_pair, block_c, sub_d)
     grads = pl.pallas_call(
         functools.partial(core_sums, n_chip),

time: 40.8 us -> 39.7 us (0.973)
  waiting for transfers between devices: 11.6 us -> 10.5 us
  other arithmetic: 0.99 us -> 0.03 us
  starting transfers between devices: 21.1 us -> 22 us
    ppermute x6, waiting for transfers between devices: 9.05 us -> 3.44 us  [over_chips(): lax.ppermute(value, 'col', [(k, k ^ CORES * mask) for k in range(n_col)])]
    ppermute x8, waiting for transfers between devices: 2.34 us -> 7.03 us  [over_row(): return lax.ppermute(value, 'row', [(k, k ^ mask) for k in range(n_row)])]
    ppermute x8, starting transfers between devices: 9.38 us -> 11 us  [over_row(): return lax.ppermute(value, 'row', [(k, k ^ mask) for k in range(n_row)])]
    another operation x1, other arithmetic: 0.99 us -> 0.03 us  [exchanged(): ends = jnp.stack([amplitudes, across])]
    slice x2 -> x0, local copies, waits for them, and re-layouts: 0.84 us -> none  [the longest x1 0.75 us: exchanged(): ints_y[half:]]
    reshape x5 -> x3, local copies, waits for them, and re-layouts: 0.69 us -> 1.5 us  [flat(): return value.reshape(value.shape[:2] + (tile,))]
    pallas_call x2 -> x4, Pallas kernels: 0.86 us -> 0.89 us  [the longest x1 0.78 us: exchanged(): pl.pallas_call(denominators, out_shape=shape((n_pair * block_c, n_i * til...]
  transfers between devices with their start and end apart: 18 -> 18, of which waited for: 6 -> 6; matrix products, arithmetic and copies ran while one was open for 6% -> 4% of each run, Pallas kernels for 3% -> 3%
where the time goes in v5:
time: 39.7 us; the launch traced here: 39.5 us
  starting transfers between devices  22 us (55%)
  waiting for transfers between devices  10.5 us (26%)
  Pallas kernels  3.96 us (10%)
  local copies, waits for them, and re-layouts  2.25 us (6%)
  between operations  0.8 us (2%)
    ppermute x8, starting transfers between devices, over_row(): return lax.ppermute(value, 'row', [(k, k ^ mask) for k in range(n_row)])  11 us
    ppermute x6, starting transfers between devices, over_chips(): lax.ppermute(value, 'col', [(k, k ^ CORES * mask) for k in range(n_col)])  10.4 us
    ppermute x8, waiting for transfers between devices, over_row(): return lax.ppermute(value, 'row', [(k, k ^ mask) for k in range(n_row)])  7.03 us
    ppermute x6, waiting for transfers between devices, over_chips(): lax.ppermute(value, 'col', [(k, k ^ CORES * mask) for k in range(n_col)])  3.44 us
    pallas_call x1, Pallas kernels, exchanged(): pl.pallas_call(products, out_shape=[shape(dens_shape, f32), shape(dens_sh...  2.09 us
    reshape x3, local copies, waits for them, and re-layouts, flat(): return value.reshape(value.shape[:2] + (tile,))  1.5 us
    pallas_call x1, Pallas kernels, exchanged(): pl.pallas_call(results, out_shape=[shape((n_i, block_d, width_b, width_a)...  0.81 us
  transfers between devices with their start and end apart: 18, of which 6 were waited for; matrix products, arithmetic and copies ran while one was open for 4% of the time, Pallas kernels for 3%

profile of v5, /device:TPU:0, one launch (start us, length us, event | category | flops | bytes accessed | tf_op | source)
XLA Modules:
  0.0 39.5 jit_solution(9665193561930136983)
XLA Ops:
  0.6 5.1 %collective-permute-start = (bf16[2,256,128]{2,1,0:T(8,128)(2,1)}, bf16[2,256,128]{2,1,0:T(8,128)(2,1)S(1)}, u32[]{:S(2)}, u32[]{:S(2)}) collective-permute-start(bf16[2,256,128]{2,1,0:T(8,128)(2,1)} %param.12), channel_id=1, source_target_pairs={{0,6},{1,7},{2,4},{3,5},{4,2},{5,3},{6,0},{7,1},{8,14},{9,15},{10,... | collective-permute-start | bytes 393224 | tf_op jit(solution)/shard_map/ppermute | solution.py:237
  5.7 1.5 %collective-permute-start.2 = (bf16[2,256,2,128]{3,2,1,0:T(2,128)(2,1)}, bf16[2,256,2,128]{3,2,1,0:T(2,128)(2,1)S(1)}, u32[]{:S(2)}, u32[]{:S(2)}) collective-permute-start(bf16[2,256,2,128]{3,2,1,0:T(2,128)(2,1)} %param.13), channel_id=1, source_target_pairs={{0,16},{8,24},{16,0},{24,8},{1,17},{9,25},{17,1},{25,9},{2,18},{10... | collective-permute-start | bytes 786440 | tf_op jit(solution)/shard_map/ppermute | solution.py:234
  7.3 1.5 %collective-permute-start.1 = (bf16[2,256,2,128]{3,2,1,0:T(2,128)(2,1)}, bf16[2,256,2,128]{3,2,1,0:T(2,128)(2,1)S(1)}, u32[]{:S(2)}, u32[]{:S(2)}) collective-permute-start(bf16[2,256,2,128]{3,2,1,0:T(2,128)(2,1)} %param.13), channel_id=1, source_target_pairs={{0,8},{8,0},{16,24},{24,16},{1,9},{9,1},{17,25},{25,17},{2,10},{10... | collective-permute-start | bytes 786440 | tf_op jit(solution)/shard_map/ppermute | solution.py:234
  8.8 0.0 collective-permute-start.6
  8.8 0.8 %collective-permute-start.5 = (bf16[2,256,128]{2,1,0:T(8,128)(2,1)}, bf16[2,256,128]{2,1,0:T(8,128)(2,1)S(1)}, u32[]{:S(2)}, u32[]{:S(2)}) collective-permute-start(bf16[2,256,128]{2,1,0:T(8,128)(2,1)} %param.12), channel_id=1, source_target_pairs={{0,4},{1,5},{2,6},{3,7},{4,0},{5,1},{6,2},{7,3},{8,12},{9,13},{10,... | collective-permute-start | bytes 393224 | tf_op jit(solution)/shard_map/ppermute | solution.py:237
  9.6 1.2 %reshape.16.own = bf16[2,256,256]{2,1,0:T(8,128)(2,1)S(1)} reshape(bf16[2,256,2,128]{3,2,1,0:T(2,128)(2,1)} %param.13) | data formatting | bytes 524288 | tf_op jit(solution)/shard_map/reshape | solution.py:251
  10.7 0.0 copy-start.1
  10.7 0.0 copy-start.2
  10.8 0.6 %copy-done.1 = s32[2,2]{1,0:T(2,128)S(1)} copy-done((s32[2,2]{1,0:T(2,128)S(1)}, s32[2,2]{1,0:T(2,128)}, u32[]{:S(2)}) %copy-start.1) | copy-done | bytes 40
  11.4 0.8 %denominators.1.denom = f32[512,512]{1,0:T(8,128)S(1)} custom-call(s32[2]{0:T(128)S(1)} %copy-done.2, s32[2,2]{1,0:T(2,128)S(1)} %copy-done.1, s32[2]{0:T(128)S(1)} %copy-done.3, f32[128]{0:T(128)S(1)} %copy-done.4, f32[1024]{0:T(1024)S(1)} %copy-done, f32[8,128]{1,0:T(8,128)S(1)} %bitcast.3), custom_call_target="tpu_custom_call" | custom-call | tf_op jit(solution)/shard_map/denominators/pallas_call | solution.py:265
  12.2 0.0 collective-permute-done
  12.2 0.1 copy-done.5
  12.3 0.1 collective-permute-start.7
  12.4 1.3 %collective-permute-done.2 = bf16[2,256,2,128]{3,2,1,0:T(2,128)(2,1)S(1)} collective-permute-done((bf16[2,256,2,128]{3,2,1,0:T(2,128)(2,1)}, bf16[2,256,2,128]{3,2,1,0:T(2,128)(2,1)S(1)}, u32[]{:S(2)}, u32[]{:S(2)}) %collective-permute-start.2) | collective-permute-done | bytes 262176 | tf_op jit(solution)/shard_map/ppermute | solution.py:234
  13.7 0.2 reshape.19.whole.near_y
  13.9 1.6 %collective-permute-start.4 = (bf16[1,256,256]{2,1,0:T(8,128)(2,1)S(1)}, bf16[1,256,256]{2,1,0:T(8,128)(2,1)S(1)}, u32[]{:S(2)}, u32[]{:S(2)}) collective-permute-start(bf16[1,256,256]{2,1,0:T(8,128)(2,1)S(1)} %last_slots.1), channel_id=1, source_target_pairs={{0,8},{8,0},{16,24},{24,16},{1,9},{9,1},{17,25},{25,17},{2,10},{10... | collective-permute-start | bytes 393224 | tf_op jit(solution)/shard_map/ppermute | solution.py:234
  15.5 0.0 collective-permute-done.1
  15.5 0.2 reshape.18.whole.near_x
  15.7 1.6 %collective-permute-start.3 = (bf16[1,256,256]{2,1,0:T(8,128)(2,1)S(1)}, bf16[1,256,256]{2,1,0:T(8,128)(2,1)S(1)}, u32[]{:S(2)}, u32[]{:S(2)}) collective-permute-start(bf16[1,256,256]{2,1,0:T(8,128)(2,1)S(1)} %first_slots.1), channel_id=1, source_target_pairs={{0,16},{8,24},{16,0},{24,8},{1,17},{9,25},{17,1},{25,9},{2,18},{10... | collective-permute-start | bytes 393224 | tf_op jit(solution)/shard_map/ppermute | solution.py:234
  17.2 0.0 collective-permute-done.6.beside
  17.3 0.0 collective-permute-start.9
  17.3 0.0 collective-permute-done.5.far
  17.3 0.5 %collective-permute-start.8 = (bf16[2,256,128]{2,1,0:T(8,128)(2,1)S(1)}, bf16[2,256,128]{2,1,0:T(8,128)(2,1)S(1)}, u32[]{:S(2)}, u32[]{:S(2)}) collective-permute-start(bf16[2,256,128]{2,1,0:T(8,128)(2,1)S(1)} %collective-permute-done.5.far), channel_id=1, source_target_pairs={{0,1},{1,0},{2,3},{3,2},{4,5},{5,4},{6,7},{7,6},{8,9},{9,8},{10,11... | collective-permute-start | bytes 393224 | tf_op jit(solution)/shard_map/ppermute | solution.py:240
  17.8 1.2 %collective-permute-done.4.far_yx = bf16[1,256,256]{2,1,0:T(8,128)(2,1)S(1)} collective-permute-done((bf16[1,256,256]{2,1,0:T(8,128)(2,1)S(1)}, bf16[1,256,256]{2,1,0:T(8,128)(2,1)S(1)}, u32[]{:S(2)}, u32[]{:S(2)}) %collective-permute-start.4) | collective-permute-done | bytes 131104 | tf_op jit(solution)/shard_map/ppermute | solution.py:234
  18.9 1.8 %collective-permute-done.3.far_xy = bf16[1,256,256]{2,1,0:T(8,128)(2,1)S(1)} collective-permute-done((bf16[1,256,256]{2,1,0:T(8,128)(2,1)S(1)}, bf16[1,256,256]{2,1,0:T(8,128)(2,1)S(1)}, u32[]{:S(2)}, u32[]{:S(2)}) %collective-permute-start.3) | collective-permute-done | bytes 131104 | tf_op jit(solution)/shard_map/ppermute | solution.py:234
  20.7 0.1 all_rows.1.ints_full
  20.8 0.0 collective-permute-done.9.other_beside
  20.8 0.0 collective-permute-done.8.other_far
  20.8 0.0 collective-permute-done.7.other_ends
  20.8 2.1 %products.1 = (f32[2,1,256,256]{3,2,1,0:T(8,128)S(1)}, bf16[2,1,256,256]{3,2,1,0:T(8,128)(2,1)S(1)}, f32[2,1,256,256]{3,2,1,0:T(8,128)S(1)}, bf16[2,1,256,256]{3...) custom-call(f32[512,512]{1,0:T(8,128)S(1)} %denominators.1.denom, ...), custom_call_target="tpu_custom_call" | custom-call | tf_op jit(solution)/shard_map/products/pallas_call | solution.py:292
  22.9 0.1 collective-permute-start.12
  23.0 1.0 %collective-permute-start.10 = (bf16[2,1,256,256]{3,2,1,0:T(8,128)(2,1)S(1)}, bf16[2,1,256,256]{3,2,1,0:T(8,128)(2,1)S(1)}, u32[]{:S(2)}, u32[]{:S(2)}) collective-permute-start(bf16[2,1,256,256]{3,2,1,0:T(8,128)(2,1)S(1)} %get-tuple-element.26), channel_id=1, source_target_pairs={{0,8},{8,0},{16,24},{24,16},{1,9},{9,1},{17,25},{25,17},{2,10},{10... | collective-permute-start | bytes 786440 | tf_op jit(solution)/shard_map/ppermute | solution.py:234
  24.0 1.1 %collective-permute-start.11 = (bf16[2,1,256,256]{3,2,1,0:T(8,128)(2,1)S(1)}, bf16[2,1,256,256]{3,2,1,0:T(8,128)(2,1)S(1)}, u32[]{:S(2)}, u32[]{:S(2)}) collective-permute-start(bf16[2,1,256,256]{3,2,1,0:T(8,128)(2,1)S(1)} %get-tuple-element.27), channel_id=1, source_target_pairs={{0,16},{8,24},{16,0},{24,8},{1,17},{9,25},{17,1},{25,9},{2,18},{10... | collective-permute-start | bytes 786440 | tf_op jit(solution)/shard_map/ppermute | solution.py:234
  25.1 0.0 collective-permute-done.12.received
  25.1 0.1 core_sums.1
  25.2 0.9 %collective-permute-start.13 = (bf16[2,256,128]{2,1,0:T(8,128)(2,1)S(1)}, bf16[2,256,128]{2,1,0:T(8,128)(2,1)S(1)}, u32[]{:S(2)}, u32[]{:S(2)}) collective-permute-start(bf16[2,256,128]{2,1,0:T(8,128)(2,1)S(1)} %get-tuple-element.30), channel_id=1, source_target_pairs={{0,2},{1,3},{2,0},{3,1},{4,6},{5,7},{6,4},{7,5},{8,10},{9,11},{10,... | collective-permute-start | bytes 393224 | tf_op jit(solution)/shard_map/ppermute | solution.py:237
  26.1 1.7 %collective-permute-start.16 = (bf16[2,256,128]{2,1,0:T(8,128)(2,1)S(1)}, bf16[2,256,128]{2,1,0:T(8,128)(2,1)S(1)}, u32[]{:S(2)}, u32[]{:S(2)}) collective-permute-start(bf16[2,256,128]{2,1,0:T(8,128)(2,1)S(1)} %get-tuple-element.40), channel_id=1, source_target_pairs={{0,4},{1,5},{2,6},{3,7},{4,0},{5,1},{6,2},{7,3},{8,12},{9,13},{10,... | collective-permute-start | bytes 393224 | tf_op jit(solution)/shard_map/ppermute | solution.py:237
  27.8 1.9 %collective-permute-start.17 = (bf16[2,256,128]{2,1,0:T(8,128)(2,1)S(1)}, bf16[2,256,128]{2,1,0:T(8,128)(2,1)S(1)}, u32[]{:S(2)}, u32[]{:S(2)}) collective-permute-start(bf16[2,256,128]{2,1,0:T(8,128)(2,1)S(1)} %get-tuple-element.41), channel_id=1, source_target_pairs={{0,6},{1,7},{2,4},{3,5},{4,2},{5,3},{6,0},{7,1},{8,14},{9,15},{10,... | collective-permute-start | bytes 393224 | tf_op jit(solution)/shard_map/ppermute | solution.py:237
  29.7 2.1 %collective-permute-done.10.received = bf16[2,1,256,256]{3,2,1,0:T(8,128)(2,1)S(1)} collective-permute-done((bf16[2,1,256,256]{3,2,1,0:T(8,128)(2,1)S(1)}, bf16[2,1,256,256]{3,2,1,0:T(8,128)(2,1)S(1)}, u32[]{:S(2)}, u32[]{:S(2)}) %collective-permute-start.10) | collective-permute-done | bytes 262176 | tf_op jit(solution)/shard_map/ppermute | solution.py:234
  31.7 0.7 %collective-permute-done.11.received = bf16[2,1,256,256]{3,2,1,0:T(8,128)(2,1)S(1)} collective-permute-done((bf16[2,1,256,256]{3,2,1,0:T(8,128)(2,1)S(1)}, bf16[2,1,256,256]{3,2,1,0:T(8,128)(2,1)S(1)}, u32[]{:S(2)}, u32[]{:S(2)}) %collective-permute-start.11) | collective-permute-done | bytes 262176 | tf_op jit(solution)/shard_map/ppermute | solution.py:234
  32.4 0.0 collective-permute-done.13.refs_0_
  32.5 1.1 %collective-permute-start.15 = (bf16[1,256,256]{2,1,0:T(8,128)(2,1)S(1)}, bf16[1,256,256]{2,1,0:T(8,128)(2,1)S(1)}, u32[]{:S(2)}, u32[]{:S(2)}) collective-permute-start(bf16[1,256,256]{2,1,0:T(8,128)(2,1)S(1)} %get-tuple-element.37), channel_id=1, source_target_pairs={{0,8},{8,0},{16,24},{24,16},{1,9},{9,1},{17,25},{25,17},{2,10},{10... | collective-permute-start | bytes 393224 | tf_op jit(solution)/shard_map/ppermute | solution.py:234
  33.7 1.6 %collective-permute-start.14 = (bf16[1,256,256]{2,1,0:T(8,128)(2,1)S(1)}, bf16[1,256,256]{2,1,0:T(8,128)(2,1)S(1)}, u32[]{:S(2)}, u32[]{:S(2)}) collective-permute-start(bf16[1,256,256]{2,1,0:T(8,128)(2,1)S(1)} %get-tuple-element.33), channel_id=1, source_target_pairs={{0,16},{8,24},{16,0},{24,8},{1,17},{9,25},{17,1},{25,9},{2,18},{10... | collective-permute-start | bytes 393224 | tf_op jit(solution)/shard_map/ppermute | solution.py:234
  35.2 3.4 %collective-permute-done.16.refs_1_ = bf16[2,256,128]{2,1,0:T(8,128)(2,1)S(1)} collective-permute-done((bf16[2,256,128]{2,1,0:T(8,128)(2,1)S(1)}, bf16[2,256,128]{2,1,0:T(8,128)(2,1)S(1)}, u32[]{:S(2)}, u32[]{:S(2)}) %collective-permute-start.16) | collective-permute-done | bytes 131104 | tf_op jit(solution)/shard_map/ppermute | solution.py:237
  38.6 0.0 collective-permute-done.17.refs_2_
  38.6 0.0 collective-permute-done.15.last_y
  38.6 0.0 collective-permute-done.14.last_x
  38.7 0.8 %results.1 = (bf16[2,256,2,128]{3,2,1,0:T(2,128)(2,1)}, bf16[2,256,128]{2,1,0:T(8,128)(2,1)}) custom-call(f32[1,256,256]{2,1,0:T(8,128)S(1)} %get-tuple-element.32.own_x, bf16[1,256,256]{2,1,0:T(8,128)(2,1)S(1)} %collective-permute-done.14.last_x, f32[1,256,256]{2,1,0:T(8,128)S(1)} %get-tuple-element.36.own_y, ...), custom_call_target="tpu_custom_call" | custom-call | tf_op jit(solution)/shard_map/results/pallas_call | solution.py:328
  (13 shorter events, 0.2 us)
Async XLA Ops:
  0.6 11.6 %collective-permute-start = (bf16[2,256,128]{2,1,0:T(8,128)(2,1)}, bf16[2,256,128]{2,1,0:T(8,128)(2,1)S(1)}, u32[]{:S(2)}, u32[]{:S(2)}) collective-permute-start(bf16[2,256,128]{2,1,0:T(8,128)(2,1)} %param.12), channel_id=1, source_target_pairs={{0,6},{1,7},{2,4},{3,5},{4,2},{5,3},{6,0},{7,1},{8,14},{9,15},{10,... | collective-permute-start | bytes 393224 | tf_op jit(solution)/shard_map/ppermute | solution.py:237
  5.7 8.0 %collective-permute-start.2 = (bf16[2,256,2,128]{3,2,1,0:T(2,128)(2,1)}, bf16[2,256,2,128]{3,2,1,0:T(2,128)(2,1)S(1)}, u32[]{:S(2)}, u32[]{:S(2)}) collective-permute-start(bf16[2,256,2,128]{3,2,1,0:T(2,128)(2,1)} %param.13), channel_id=1, source_target_pairs={{0,16},{8,24},{16,0},{24,8},{1,17},{9,25},{17,1},{25,9},{2,18},{10... | collective-permute-start | bytes 786440 | tf_op jit(solution)/shard_map/ppermute | solution.py:234
  7.3 8.2 %collective-permute-start.1 = (bf16[2,256,2,128]{3,2,1,0:T(2,128)(2,1)}, bf16[2,256,2,128]{3,2,1,0:T(2,128)(2,1)S(1)}, u32[]{:S(2)}, u32[]{:S(2)}) collective-permute-start(bf16[2,256,2,128]{3,2,1,0:T(2,128)(2,1)} %param.13), channel_id=1, source_target_pairs={{0,8},{8,0},{16,24},{24,16},{1,9},{9,1},{17,25},{25,17},{2,10},{10... | collective-permute-start | bytes 786440 | tf_op jit(solution)/shard_map/ppermute | solution.py:234
  8.8 8.5 %collective-permute-start.6 = (bf16[2,256,128]{2,1,0:T(8,128)(2,1)}, bf16[2,256,128]{2,1,0:T(8,128)(2,1)S(1)}, u32[]{:S(2)}, u32[]{:S(2)}) collective-permute-start(bf16[2,256,128]{2,1,0:T(8,128)(2,1)} %param.12), channel_id=1, source_target_pairs={{0,2},{1,3},{2,0},{3,1},{4,6},{5,7},{6,4},{7,5},{8,10},{9,11},{10,... | collective-permute-start | bytes 393224 | tf_op jit(solution)/shard_map/ppermute | solution.py:237
  8.8 8.5 %collective-permute-start.5 = (bf16[2,256,128]{2,1,0:T(8,128)(2,1)}, bf16[2,256,128]{2,1,0:T(8,128)(2,1)S(1)}, u32[]{:S(2)}, u32[]{:S(2)}) collective-permute-start(bf16[2,256,128]{2,1,0:T(8,128)(2,1)} %param.12), channel_id=1, source_target_pairs={{0,4},{1,5},{2,6},{3,7},{4,0},{5,1},{6,2},{7,3},{8,12},{9,13},{10,... | collective-permute-start | bytes 393224 | tf_op jit(solution)/shard_map/ppermute | solution.py:237
  9.5 1.2 %copy-start = (f32[1024]{0:T(1024)S(1)}, f32[1024]{0:T(1024)}, u32[]{:S(2)}) copy-start(f32[1024]{0:T(1024)} %vir_smem.1) | copy-start | bytes 12292
  9.5 1.2 %copy-start.3 = (s32[2]{0:T(128)S(1)}, s32[2]{0:T(128)}, u32[]{:S(2)}) copy-start(s32[2]{0:T(128)} %vir_offsets.1) | copy-start | bytes 28
  9.5 1.2 %copy-start.4 = (f32[128]{0:T(128)S(1)}, f32[128]{0:T(128)}, u32[]{:S(2)}) copy-start(f32[128]{0:T(128)} %occ_energy.1) | copy-start | bytes 1540
  10.7 0.7 %copy-start.1 = (s32[2,2]{1,0:T(2,128)S(1)}, s32[2,2]{1,0:T(2,128)}, u32[]{:S(2)}) copy-start(s32[2,2]{1,0:T(2,128)} %pairs.1) | copy-start | bytes 52
  10.7 0.7 %copy-start.2 = (s32[2]{0:T(128)S(1)}, s32[2]{0:T(128)}, u32[]{:S(2)}) copy-start(s32[2]{0:T(128)} %i_list.1) | copy-start | bytes 28
  11.4 0.9 %copy-start.5 = (bf16[2,256,128]{2,1,0:T(8,128)(2,1)S(1)}, bf16[2,256,128]{2,1,0:T(8,128)(2,1)}, u32[]{:S(2)}) copy-start(bf16[2,256,128]{2,1,0:T(8,128)(2,1)} %param.12) | copy-start | bytes 393220
  12.3 8.5 %collective-permute-start.7 = (bf16[2,2,256,128]{3,2,1,0:T(8,128)(2,1)S(1)}, bf16[2,2,256,128]{3,2,1,0:T(8,128)(2,1)S(1)}, u32[]{:S(2)}, u32[]{:S(2)}) collective-permute-start(bf16[2,2,256,128]{3,2,1,0:T(8,128)(2,1)S(1)} %pad_maximum_fusion.ends), channel_id=1, source_target_pairs={{0,1},{1,0},{2,3},{3,2},{4,5},{5,4},{6,7},{7,6},{8,9},{9,8},{10,11... | collective-permute-start | bytes 786440 | tf_op jit(solution)/shard_map/ppermute | solution.py:240
  13.9 5.0 %collective-permute-start.4 = (bf16[1,256,256]{2,1,0:T(8,128)(2,1)S(1)}, bf16[1,256,256]{2,1,0:T(8,128)(2,1)S(1)}, u32[]{:S(2)}, u32[]{:S(2)}) collective-permute-start(bf16[1,256,256]{2,1,0:T(8,128)(2,1)S(1)} %last_slots.1), channel_id=1, source_target_pairs={{0,8},{8,0},{16,24},{24,16},{1,9},{9,1},{17,25},{25,17},{2,10},{10... | collective-permute-start | bytes 393224 | tf_op jit(solution)/shard_map/ppermute | solution.py:234
  15.7 5.0 %collective-permute-start.3 = (bf16[1,256,256]{2,1,0:T(8,128)(2,1)S(1)}, bf16[1,256,256]{2,1,0:T(8,128)(2,1)S(1)}, u32[]{:S(2)}, u32[]{:S(2)}) collective-permute-start(bf16[1,256,256]{2,1,0:T(8,128)(2,1)S(1)} %first_slots.1), channel_id=1, source_target_pairs={{0,16},{8,24},{16,0},{24,8},{1,17},{9,25},{17,1},{25,9},{2,18},{10... | collective-permute-start | bytes 393224 | tf_op jit(solution)/shard_map/ppermute | solution.py:234
  17.3 3.5 %collective-permute-start.9 = (bf16[2,256,128]{2,1,0:T(8,128)(2,1)S(1)}, bf16[2,256,128]{2,1,0:T(8,128)(2,1)S(1)}, u32[]{:S(2)}, u32[]{:S(2)}) collective-permute-start(bf16[2,256,128]{2,1,0:T(8,128)(2,1)S(1)} %collective-permute-done.6.beside), channel_id=1, source_target_pairs={{0,1},{1,0},{2,3},{3,2},{4,5},{5,4},{6,7},{7,6},{8,9},{9,8},{10,11... | collective-permute-start | bytes 393224 | tf_op jit(solution)/shard_map/ppermute | solution.py:240
  17.3 3.5 %collective-permute-start.8 = (bf16[2,256,128]{2,1,0:T(8,128)(2,1)S(1)}, bf16[2,256,128]{2,1,0:T(8,128)(2,1)S(1)}, u32[]{:S(2)}, u32[]{:S(2)}) collective-permute-start(bf16[2,256,128]{2,1,0:T(8,128)(2,1)S(1)} %collective-permute-done.5.far), channel_id=1, source_target_pairs={{0,1},{1,0},{2,3},{3,2},{4,5},{5,4},{6,7},{7,6},{8,9},{9,8},{10,11... | collective-permute-start | bytes 393224 | tf_op jit(solution)/shard_map/ppermute | solution.py:240
  22.9 2.2 %collective-permute-start.12 = (bf16[4,2,256,128]{3,2,1,0:T(8,128)(2,1)S(1)}, bf16[4,2,256,128]{3,2,1,0:T(8,128)(2,1)S(1)}, u32[]{:S(2)}, u32[]{:S(2)}) collective-permute-start(bf16[4,2,256,128]{3,2,1,0:T(8,128)(2,1)S(1)} %get-tuple-element.29), channel_id=1, source_target_pairs={{0,1},{1,0},{2,3},{3,2},{4,5},{5,4},{6,7},{7,6},{8,9},{9,8},{10,11... | collective-permute-start | bytes 1572872 | tf_op jit(solution)/shard_map/ppermute | solution.py:240
  23.0 8.7 %collective-permute-start.10 = (bf16[2,1,256,256]{3,2,1,0:T(8,128)(2,1)S(1)}, bf16[2,1,256,256]{3,2,1,0:T(8,128)(2,1)S(1)}, u32[]{:S(2)}, u32[]{:S(2)}) collective-permute-start(bf16[2,1,256,256]{3,2,1,0:T(8,128)(2,1)S(1)} %get-tuple-element.26), channel_id=1, source_target_pairs={{0,8},{8,0},{16,24},{24,16},{1,9},{9,1},{17,25},{25,17},{2,10},{10... | collective-permute-start | bytes 786440 | tf_op jit(solution)/shard_map/ppermute | solution.py:234
  24.0 8.4 %collective-permute-start.11 = (bf16[2,1,256,256]{3,2,1,0:T(8,128)(2,1)S(1)}, bf16[2,1,256,256]{3,2,1,0:T(8,128)(2,1)S(1)}, u32[]{:S(2)}, u32[]{:S(2)}) collective-permute-start(bf16[2,1,256,256]{3,2,1,0:T(8,128)(2,1)S(1)} %get-tuple-element.27), channel_id=1, source_target_pairs={{0,16},{8,24},{16,0},{24,8},{1,17},{9,25},{17,1},{25,9},{2,18},{10... | collective-permute-start | bytes 786440 | tf_op jit(solution)/shard_map/ppermute | solution.py:234
  25.2 7.2 %collective-permute-start.13 = (bf16[2,256,128]{2,1,0:T(8,128)(2,1)S(1)}, bf16[2,256,128]{2,1,0:T(8,128)(2,1)S(1)}, u32[]{:S(2)}, u32[]{:S(2)}) collective-permute-start(bf16[2,256,128]{2,1,0:T(8,128)(2,1)S(1)} %get-tuple-element.30), channel_id=1, source_target_pairs={{0,2},{1,3},{2,0},{3,1},{4,6},{5,7},{6,4},{7,5},{8,10},{9,11},{10,... | collective-permute-start | bytes 393224 | tf_op jit(solution)/shard_map/ppermute | solution.py:237
  26.1 12.6 %collective-permute-start.16 = (bf16[2,256,128]{2,1,0:T(8,128)(2,1)S(1)}, bf16[2,256,128]{2,1,0:T(8,128)(2,1)S(1)}, u32[]{:S(2)}, u32[]{:S(2)}) collective-permute-start(bf16[2,256,128]{2,1,0:T(8,128)(2,1)S(1)} %get-tuple-element.40), channel_id=1, source_target_pairs={{0,4},{1,5},{2,6},{3,7},{4,0},{5,1},{6,2},{7,3},{8,12},{9,13},{10,... | collective-permute-start | bytes 393224 | tf_op jit(solution)/shard_map/ppermute | solution.py:237
  27.8 10.9 %collective-permute-start.17 = (bf16[2,256,128]{2,1,0:T(8,128)(2,1)S(1)}, bf16[2,256,128]{2,1,0:T(8,128)(2,1)S(1)}, u32[]{:S(2)}, u32[]{:S(2)}) collective-permute-start(bf16[2,256,128]{2,1,0:T(8,128)(2,1)S(1)} %get-tuple-element.41), channel_id=1, source_target_pairs={{0,6},{1,7},{2,4},{3,5},{4,2},{5,3},{6,0},{7,1},{8,14},{9,15},{10,... | collective-permute-start | bytes 393224 | tf_op jit(solution)/shard_map/ppermute | solution.py:237
  32.5 6.2 %collective-permute-start.15 = (bf16[1,256,256]{2,1,0:T(8,128)(2,1)S(1)}, bf16[1,256,256]{2,1,0:T(8,128)(2,1)S(1)}, u32[]{:S(2)}, u32[]{:S(2)}) collective-permute-start(bf16[1,256,256]{2,1,0:T(8,128)(2,1)S(1)} %get-tuple-element.37), channel_id=1, source_target_pairs={{0,8},{8,0},{16,24},{24,16},{1,9},{9,1},{17,25},{25,17},{2,10},{10... | collective-permute-start | bytes 393224 | tf_op jit(solution)/shard_map/ppermute | solution.py:234
  33.7 5.0 %collective-permute-start.14 = (bf16[1,256,256]{2,1,0:T(8,128)(2,1)S(1)}, bf16[1,256,256]{2,1,0:T(8,128)(2,1)S(1)}, u32[]{:S(2)}, u32[]{:S(2)}) collective-permute-start(bf16[1,256,256]{2,1,0:T(8,128)(2,1)S(1)} %get-tuple-element.33), channel_id=1, source_target_pairs={{0,16},{8,24},{16,0},{24,8},{1,17},{9,25},{17,1},{25,9},{2,18},{10... | collective-permute-start | bytes 393224 | tf_op jit(solution)/shard_map/ppermute | solution.py:234

commit v6 on v5

--- a/solution.py
+++ b/solution.py
@@ -198,16 +198,25 @@
 
 
 def results(own_x, last_x, own_y, last_y, own, *refs):
-    density, amp_grad = refs[-2:]
-    total = own[...]
-    for value in refs[:-2]:
-        total = total + value[...].astype(jnp.float32)
-    amp_grad[...] = total.astype(amp_grad.dtype)
+    *parts, density, amp_grad, rows, block, sems = refs
+    n_i = rows.shape[0]
     half = own_x.shape[0]
+    copies = []
     for part_of, (kept, last) in enumerate(((own_x, last_x), (own_y, last_y))):
         for k in range(half):
-            total = (kept[k] + last[k].astype(jnp.float32)).astype(density.dtype)
-            density[part_of * half + k] = total.reshape(density.shape[1:])
+            slot = part_of * half + k
+            total = (kept[k] + last[k].astype(jnp.float32)).astype(rows.dtype)
+            rows[slot] = total.reshape(rows.shape[1:])
+            copies.append(pltpu.make_async_copy(rows.at[slot], density.at[slot], sems.at[slot]))
+            copies[-1].start()
+    total = own[...]
+    for value in parts:
+        total = total + value[...].astype(jnp.float32)
+    block[...] = total.astype(block.dtype)
+    copies.append(pltpu.make_async_copy(block, amp_grad, sems.at[n_i]))
+    copies[-1].start()
+    for copy in copies:
+        copy.wait()
 
 
 def row_sums(keep, received, own, onward):
@@ -329,7 +338,12 @@
         results,
         out_shape=[shape((n_i, block_d, width_b, width_a), bf16), shape(block, bf16)],
         in_specs=[vmem] * (4 + n_chip),
-        out_specs=[vmem] * 2,
+        out_specs=[pl.BlockSpec(memory_space=pl.ANY)] * 2,
+        scratch_shapes=[
+            pltpu.VMEM((n_i, block_d, width_b, width_a), bf16),
+            pltpu.VMEM(block, bf16),
+            pltpu.SemaphoreType.DMA((n_i + 1,)),
+        ],
         compiler_params=room(6),
         name="results",
     )(own_x, last_x, own_y, last_y, grads[0], *grad_parts)

time: 39.7 us -> 39.6 us (level)
  no operation moved by 1% of the time
where the time goes in v6:
time: 39.6 us; the launch traced here: 39.5 us
  starting transfers between devices  22 us (56%)
  waiting for transfers between devices  10.5 us (27%)
  Pallas kernels  3.94 us (10%)
  local copies, waits for them, and re-layouts  2.25 us (6%)
  between operations  0.8 us (2%)
    ppermute x8, starting transfers between devices, over_row(): return lax.ppermute(value, 'row', [(k, k ^ mask) for k in range(n_row)])  11 us
    ppermute x6, starting transfers between devices, over_chips(): lax.ppermute(value, 'col', [(k, k ^ CORES * mask) for k in range(n_col)])  10.4 us
    ppermute x8, waiting for transfers between devices, over_row(): return lax.ppermute(value, 'row', [(k, k ^ mask) for k in range(n_row)])  7.03 us
    ppermute x6, waiting for transfers between devices, over_chips(): lax.ppermute(value, 'col', [(k, k ^ CORES * mask) for k in range(n_col)])  3.44 us
    pallas_call x1, Pallas kernels, exchanged(): pl.pallas_call(products, out_shape=[shape(dens_shape, f32), shape(dens_sh...  2.09 us
    reshape x3, local copies, waits for them, and re-layouts, flat(): return value.reshape(value.shape[:2] + (tile,))  1.5 us
  transfers between devices with their start and end apart: 18, of which 6 were waited for; matrix products, arithmetic and copies ran while one was open for 4% of the time, Pallas kernels for 3%

profile of v6, /device:TPU:0, one launch (start us, length us, event | category | flops | bytes accessed | tf_op | source)
XLA Modules:
  0.0 39.5 jit_solution(10076190492235487142)
XLA Ops:
  0.6 5.1 %collective-permute-start = (bf16[2,256,128]{2,1,0:T(8,128)(2,1)}, bf16[2,256,128]{2,1,0:T(8,128)(2,1)S(1)}, u32[]{:S(2)}, u32[]{:S(2)}) collective-permute-start(bf16[2,256,128]{2,1,0:T(8,128)(2,1)} %param.12), channel_id=1, source_target_pairs={{0,6},{1,7},{2,4},{3,5},{4,2},{5,3},{6,0},{7,1},{8,14},{9,15},{10,... | collective-permute-start | bytes 393224 | tf_op jit(solution)/shard_map/ppermute | solution.py:246
  5.7 1.5 %collective-permute-start.2 = (bf16[2,256,2,128]{3,2,1,0:T(2,128)(2,1)}, bf16[2,256,2,128]{3,2,1,0:T(2,128)(2,1)S(1)}, u32[]{:S(2)}, u32[]{:S(2)}) collective-permute-start(bf16[2,256,2,128]{3,2,1,0:T(2,128)(2,1)} %param.13), channel_id=1, source_target_pairs={{0,16},{8,24},{16,0},{24,8},{1,17},{9,25},{17,1},{25,9},{2,18},{10... | collective-permute-start | bytes 786440 | tf_op jit(solution)/shard_map/ppermute | solution.py:243
  7.3 1.5 %collective-permute-start.1 = (bf16[2,256,2,128]{3,2,1,0:T(2,128)(2,1)}, bf16[2,256,2,128]{3,2,1,0:T(2,128)(2,1)S(1)}, u32[]{:S(2)}, u32[]{:S(2)}) collective-permute-start(bf16[2,256,2,128]{3,2,1,0:T(2,128)(2,1)} %param.13), channel_id=1, source_target_pairs={{0,8},{8,0},{16,24},{24,16},{1,9},{9,1},{17,25},{25,17},{2,10},{10... | collective-permute-start | bytes 786440 | tf_op jit(solution)/shard_map/ppermute | solution.py:243
  8.8 0.0 collective-permute-start.6
  8.8 0.8 %collective-permute-start.5 = (bf16[2,256,128]{2,1,0:T(8,128)(2,1)}, bf16[2,256,128]{2,1,0:T(8,128)(2,1)S(1)}, u32[]{:S(2)}, u32[]{:S(2)}) collective-permute-start(bf16[2,256,128]{2,1,0:T(8,128)(2,1)} %param.12), channel_id=1, source_target_pairs={{0,4},{1,5},{2,6},{3,7},{4,0},{5,1},{6,2},{7,3},{8,12},{9,13},{10,... | collective-permute-start | bytes 393224 | tf_op jit(solution)/shard_map/ppermute | solution.py:246
  9.6 1.2 %reshape.16.own = bf16[2,256,256]{2,1,0:T(8,128)(2,1)S(1)} reshape(bf16[2,256,2,128]{3,2,1,0:T(2,128)(2,1)} %param.13) | data formatting | bytes 524288 | tf_op jit(solution)/shard_map/reshape | solution.py:260
  10.7 0.0 copy-start.1
  10.7 0.0 copy-start.2
  10.8 0.6 %copy-done.1 = s32[2,2]{1,0:T(2,128)S(1)} copy-done((s32[2,2]{1,0:T(2,128)S(1)}, s32[2,2]{1,0:T(2,128)}, u32[]{:S(2)}) %copy-start.1) | copy-done | bytes 40
  11.4 0.8 %denominators.1.denom = f32[512,512]{1,0:T(8,128)S(1)} custom-call(s32[2]{0:T(128)S(1)} %copy-done.2, s32[2,2]{1,0:T(2,128)S(1)} %copy-done.1, s32[2]{0:T(128)S(1)} %copy-done.3, f32[128]{0:T(128)S(1)} %copy-done.4, f32[1024]{0:T(1024)S(1)} %copy-done, f32[8,128]{1,0:T(8,128)S(1)} %bitcast.3), custom_call_target="tpu_custom_call" | custom-call | tf_op jit(solution)/shard_map/denominators/pallas_call | solution.py:274
  12.2 0.0 collective-permute-done
  12.2 0.1 copy-done.5
  12.3 0.1 collective-permute-start.7
  12.4 1.3 %collective-permute-done.2 = bf16[2,256,2,128]{3,2,1,0:T(2,128)(2,1)S(1)} collective-permute-done((bf16[2,256,2,128]{3,2,1,0:T(2,128)(2,1)}, bf16[2,256,2,128]{3,2,1,0:T(2,128)(2,1)S(1)}, u32[]{:S(2)}, u32[]{:S(2)}) %collective-permute-start.2) | collective-permute-done | bytes 262176 | tf_op jit(solution)/shard_map/ppermute | solution.py:243
  13.7 0.2 reshape.19.whole.near_y
  13.9 1.6 %collective-permute-start.4 = (bf16[1,256,256]{2,1,0:T(8,128)(2,1)S(1)}, bf16[1,256,256]{2,1,0:T(8,128)(2,1)S(1)}, u32[]{:S(2)}, u32[]{:S(2)}) collective-permute-start(bf16[1,256,256]{2,1,0:T(8,128)(2,1)S(1)} %last_slots.1), channel_id=1, source_target_pairs={{0,8},{8,0},{16,24},{24,16},{1,9},{9,1},{17,25},{25,17},{2,10},{10... | collective-permute-start | bytes 393224 | tf_op jit(solution)/shard_map/ppermute | solution.py:243
  15.5 0.0 collective-permute-done.1
  15.5 0.2 reshape.18.whole.near_x
  15.7 1.6 %collective-permute-start.3 = (bf16[1,256,256]{2,1,0:T(8,128)(2,1)S(1)}, bf16[1,256,256]{2,1,0:T(8,128)(2,1)S(1)}, u32[]{:S(2)}, u32[]{:S(2)}) collective-permute-start(bf16[1,256,256]{2,1,0:T(8,128)(2,1)S(1)} %first_slots.1), channel_id=1, source_target_pairs={{0,16},{8,24},{16,0},{24,8},{1,17},{9,25},{17,1},{25,9},{2,18},{10... | collective-permute-start | bytes 393224 | tf_op jit(solution)/shard_map/ppermute | solution.py:243
  17.2 0.0 collective-permute-done.6.beside
  17.3 0.0 collective-permute-start.9
  17.3 0.0 collective-permute-done.5.far
  17.3 0.5 %collective-permute-start.8 = (bf16[2,256,128]{2,1,0:T(8,128)(2,1)S(1)}, bf16[2,256,128]{2,1,0:T(8,128)(2,1)S(1)}, u32[]{:S(2)}, u32[]{:S(2)}) collective-permute-start(bf16[2,256,128]{2,1,0:T(8,128)(2,1)S(1)} %collective-permute-done.5.far), channel_id=1, source_target_pairs={{0,1},{1,0},{2,3},{3,2},{4,5},{5,4},{6,7},{7,6},{8,9},{9,8},{10,11... | collective-permute-start | bytes 393224 | tf_op jit(solution)/shard_map/ppermute | solution.py:249
  17.8 1.2 %collective-permute-done.4.far_yx = bf16[1,256,256]{2,1,0:T(8,128)(2,1)S(1)} collective-permute-done((bf16[1,256,256]{2,1,0:T(8,128)(2,1)S(1)}, bf16[1,256,256]{2,1,0:T(8,128)(2,1)S(1)}, u32[]{:S(2)}, u32[]{:S(2)}) %collective-permute-start.4) | collective-permute-done | bytes 131104 | tf_op jit(solution)/shard_map/ppermute | solution.py:243
  18.9 1.8 %collective-permute-done.3.far_xy = bf16[1,256,256]{2,1,0:T(8,128)(2,1)S(1)} collective-permute-done((bf16[1,256,256]{2,1,0:T(8,128)(2,1)S(1)}, bf16[1,256,256]{2,1,0:T(8,128)(2,1)S(1)}, u32[]{:S(2)}, u32[]{:S(2)}) %collective-permute-start.3) | collective-permute-done | bytes 131104 | tf_op jit(solution)/shard_map/ppermute | solution.py:243
  20.7 0.1 all_rows.1.ints_full
  20.8 0.0 collective-permute-done.9.other_beside
  20.8 0.0 collective-permute-done.8.other_far
  20.8 0.0 collective-permute-done.7.other_ends
  20.8 2.1 %products.1 = (f32[2,1,256,256]{3,2,1,0:T(8,128)S(1)}, bf16[2,1,256,256]{3,2,1,0:T(8,128)(2,1)S(1)}, f32[2,1,256,256]{3,2,1,0:T(8,128)S(1)}, bf16[2,1,256,256]{3...) custom-call(f32[512,512]{1,0:T(8,128)S(1)} %denominators.1.denom, ...), custom_call_target="tpu_custom_call" | custom-call | tf_op jit(solution)/shard_map/products/pallas_call | solution.py:301
  22.9 0.1 collective-permute-start.12
  23.0 1.0 %collective-permute-start.10 = (bf16[2,1,256,256]{3,2,1,0:T(8,128)(2,1)S(1)}, bf16[2,1,256,256]{3,2,1,0:T(8,128)(2,1)S(1)}, u32[]{:S(2)}, u32[]{:S(2)}) collective-permute-start(bf16[2,1,256,256]{3,2,1,0:T(8,128)(2,1)S(1)} %get-tuple-element.26), channel_id=1, source_target_pairs={{0,8},{8,0},{16,24},{24,16},{1,9},{9,1},{17,25},{25,17},{2,10},{10... | collective-permute-start | bytes 786440 | tf_op jit(solution)/shard_map/ppermute | solution.py:243
  24.0 1.1 %collective-permute-start.11 = (bf16[2,1,256,256]{3,2,1,0:T(8,128)(2,1)S(1)}, bf16[2,1,256,256]{3,2,1,0:T(8,128)(2,1)S(1)}, u32[]{:S(2)}, u32[]{:S(2)}) collective-permute-start(bf16[2,1,256,256]{3,2,1,0:T(8,128)(2,1)S(1)} %get-tuple-element.27), channel_id=1, source_target_pairs={{0,16},{8,24},{16,0},{24,8},{1,17},{9,25},{17,1},{25,9},{2,18},{10... | collective-permute-start | bytes 786440 | tf_op jit(solution)/shard_map/ppermute | solution.py:243
  25.1 0.0 collective-permute-done.12.received
  25.1 0.1 core_sums.1
  25.2 0.9 %collective-permute-start.13 = (bf16[2,256,128]{2,1,0:T(8,128)(2,1)S(1)}, bf16[2,256,128]{2,1,0:T(8,128)(2,1)S(1)}, u32[]{:S(2)}, u32[]{:S(2)}) collective-permute-start(bf16[2,256,128]{2,1,0:T(8,128)(2,1)S(1)} %get-tuple-element.30), channel_id=1, source_target_pairs={{0,2},{1,3},{2,0},{3,1},{4,6},{5,7},{6,4},{7,5},{8,10},{9,11},{10,... | collective-permute-start | bytes 393224 | tf_op jit(solution)/shard_map/ppermute | solution.py:246
  26.1 1.7 %collective-permute-start.16 = (bf16[2,256,128]{2,1,0:T(8,128)(2,1)S(1)}, bf16[2,256,128]{2,1,0:T(8,128)(2,1)S(1)}, u32[]{:S(2)}, u32[]{:S(2)}) collective-permute-start(bf16[2,256,128]{2,1,0:T(8,128)(2,1)S(1)} %get-tuple-element.40), channel_id=1, source_target_pairs={{0,4},{1,5},{2,6},{3,7},{4,0},{5,1},{6,2},{7,3},{8,12},{9,13},{10,... | collective-permute-start | bytes 393224 | tf_op jit(solution)/shard_map/ppermute | solution.py:246
  27.8 1.9 %collective-permute-start.17 = (bf16[2,256,128]{2,1,0:T(8,128)(2,1)S(1)}, bf16[2,256,128]{2,1,0:T(8,128)(2,1)S(1)}, u32[]{:S(2)}, u32[]{:S(2)}) collective-permute-start(bf16[2,256,128]{2,1,0:T(8,128)(2,1)S(1)} %get-tuple-element.41), channel_id=1, source_target_pairs={{0,6},{1,7},{2,4},{3,5},{4,2},{5,3},{6,0},{7,1},{8,14},{9,15},{10,... | collective-permute-start | bytes 393224 | tf_op jit(solution)/shard_map/ppermute | solution.py:246
  29.7 2.1 %collective-permute-done.10.received = bf16[2,1,256,256]{3,2,1,0:T(8,128)(2,1)S(1)} collective-permute-done((bf16[2,1,256,256]{3,2,1,0:T(8,128)(2,1)S(1)}, bf16[2,1,256,256]{3,2,1,0:T(8,128)(2,1)S(1)}, u32[]{:S(2)}, u32[]{:S(2)}) %collective-permute-start.10) | collective-permute-done | bytes 262176 | tf_op jit(solution)/shard_map/ppermute | solution.py:243
  31.7 0.7 %collective-permute-done.11.received = bf16[2,1,256,256]{3,2,1,0:T(8,128)(2,1)S(1)} collective-permute-done((bf16[2,1,256,256]{3,2,1,0:T(8,128)(2,1)S(1)}, bf16[2,1,256,256]{3,2,1,0:T(8,128)(2,1)S(1)}, u32[]{:S(2)}, u32[]{:S(2)}) %collective-permute-start.11) | collective-permute-done | bytes 262176 | tf_op jit(solution)/shard_map/ppermute | solution.py:243
  32.4 0.0 collective-permute-done.13.refs_0_
  32.5 1.1 %collective-permute-start.15 = (bf16[1,256,256]{2,1,0:T(8,128)(2,1)S(1)}, bf16[1,256,256]{2,1,0:T(8,128)(2,1)S(1)}, u32[]{:S(2)}, u32[]{:S(2)}) collective-permute-start(bf16[1,256,256]{2,1,0:T(8,128)(2,1)S(1)} %get-tuple-element.37), channel_id=1, source_target_pairs={{0,8},{8,0},{16,24},{24,16},{1,9},{9,1},{17,25},{25,17},{2,10},{10... | collective-permute-start | bytes 393224 | tf_op jit(solution)/shard_map/ppermute | solution.py:243
  33.7 1.6 %collective-permute-start.14 = (bf16[1,256,256]{2,1,0:T(8,128)(2,1)S(1)}, bf16[1,256,256]{2,1,0:T(8,128)(2,1)S(1)}, u32[]{:S(2)}, u32[]{:S(2)}) collective-permute-start(bf16[1,256,256]{2,1,0:T(8,128)(2,1)S(1)} %get-tuple-element.33), channel_id=1, source_target_pairs={{0,16},{8,24},{16,0},{24,8},{1,17},{9,25},{17,1},{25,9},{2,18},{10... | collective-permute-start | bytes 393224 | tf_op jit(solution)/shard_map/ppermute | solution.py:243
  35.2 3.4 %collective-permute-done.16.refs_1_ = bf16[2,256,128]{2,1,0:T(8,128)(2,1)S(1)} collective-permute-done((bf16[2,256,128]{2,1,0:T(8,128)(2,1)S(1)}, bf16[2,256,128]{2,1,0:T(8,128)(2,1)S(1)}, u32[]{:S(2)}, u32[]{:S(2)}) %collective-permute-start.16) | collective-permute-done | bytes 131104 | tf_op jit(solution)/shard_map/ppermute | solution.py:246
  38.6 0.0 collective-permute-done.17.refs_2_
  38.6 0.0 collective-permute-done.15.last_y
  38.6 0.0 collective-permute-done.14.last_x
  38.7 0.8 %results.1 = (bf16[2,256,2,128]{3,2,1,0:T(2,128)(2,1)}, bf16[2,256,128]{2,1,0:T(8,128)(2,1)}) custom-call(f32[1,256,256]{2,1,0:T(8,128)S(1)} %get-tuple-element.32.own_x, bf16[1,256,256]{2,1,0:T(8,128)(2,1)S(1)} %collective-permute-done.14.last_x, f32[1,256,256]{2,1,0:T(8,128)S(1)} %get-tuple-element.36.own_y, ...), custom_call_target="tpu_custom_call" | custom-call | tf_op jit(solution)/shard_map/results/pallas_call | solution.py:337
  (13 shorter events, 0.2 us)
Async XLA Ops:
  0.6 11.6 %collective-permute-start = (bf16[2,256,128]{2,1,0:T(8,128)(2,1)}, bf16[2,256,128]{2,1,0:T(8,128)(2,1)S(1)}, u32[]{:S(2)}, u32[]{:S(2)}) collective-permute-start(bf16[2,256,128]{2,1,0:T(8,128)(2,1)} %param.12), channel_id=1, source_target_pairs={{0,6},{1,7},{2,4},{3,5},{4,2},{5,3},{6,0},{7,1},{8,14},{9,15},{10,... | collective-permute-start | bytes 393224 | tf_op jit(solution)/shard_map/ppermute | solution.py:246
  5.7 8.0 %collective-permute-start.2 = (bf16[2,256,2,128]{3,2,1,0:T(2,128)(2,1)}, bf16[2,256,2,128]{3,2,1,0:T(2,128)(2,1)S(1)}, u32[]{:S(2)}, u32[]{:S(2)}) collective-permute-start(bf16[2,256,2,128]{3,2,1,0:T(2,128)(2,1)} %param.13), channel_id=1, source_target_pairs={{0,16},{8,24},{16,0},{24,8},{1,17},{9,25},{17,1},{25,9},{2,18},{10... | collective-permute-start | bytes 786440 | tf_op jit(solution)/shard_map/ppermute | solution.py:243
  7.3 8.2 %collective-permute-start.1 = (bf16[2,256,2,128]{3,2,1,0:T(2,128)(2,1)}, bf16[2,256,2,128]{3,2,1,0:T(2,128)(2,1)S(1)}, u32[]{:S(2)}, u32[]{:S(2)}) collective-permute-start(bf16[2,256,2,128]{3,2,1,0:T(2,128)(2,1)} %param.13), channel_id=1, source_target_pairs={{0,8},{8,0},{16,24},{24,16},{1,9},{9,1},{17,25},{25,17},{2,10},{10... | collective-permute-start | bytes 786440 | tf_op jit(solution)/shard_map/ppermute | solution.py:243
  8.8 8.5 %collective-permute-start.6 = (bf16[2,256,128]{2,1,0:T(8,128)(2,1)}, bf16[2,256,128]{2,1,0:T(8,128)(2,1)S(1)}, u32[]{:S(2)}, u32[]{:S(2)}) collective-permute-start(bf16[2,256,128]{2,1,0:T(8,128)(2,1)} %param.12), channel_id=1, source_target_pairs={{0,2},{1,3},{2,0},{3,1},{4,6},{5,7},{6,4},{7,5},{8,10},{9,11},{10,... | collective-permute-start | bytes 393224 | tf_op jit(solution)/shard_map/ppermute | solution.py:246
  8.8 8.5 %collective-permute-start.5 = (bf16[2,256,128]{2,1,0:T(8,128)(2,1)}, bf16[2,256,128]{2,1,0:T(8,128)(2,1)S(1)}, u32[]{:S(2)}, u32[]{:S(2)}) collective-permute-start(bf16[2,256,128]{2,1,0:T(8,128)(2,1)} %param.12), channel_id=1, source_target_pairs={{0,4},{1,5},{2,6},{3,7},{4,0},{5,1},{6,2},{7,3},{8,12},{9,13},{10,... | collective-permute-start | bytes 393224 | tf_op jit(solution)/shard_map/ppermute | solution.py:246
  9.5 1.2 %copy-start = (f32[1024]{0:T(1024)S(1)}, f32[1024]{0:T(1024)}, u32[]{:S(2)}) copy-start(f32[1024]{0:T(1024)} %vir_smem.1) | copy-start | bytes 12292
  9.5 1.2 %copy-start.3 = (s32[2]{0:T(128)S(1)}, s32[2]{0:T(128)}, u32[]{:S(2)}) copy-start(s32[2]{0:T(128)} %vir_offsets.1) | copy-start | bytes 28
  9.5 1.2 %copy-start.4 = (f32[128]{0:T(128)S(1)}, f32[128]{0:T(128)}, u32[]{:S(2)}) copy-start(f32[128]{0:T(128)} %occ_energy.1) | copy-start | bytes 1540
  10.7 0.7 %copy-start.1 = (s32[2,2]{1,0:T(2,128)S(1)}, s32[2,2]{1,0:T(2,128)}, u32[]{:S(2)}) copy-start(s32[2,2]{1,0:T(2,128)} %pairs.1) | copy-start | bytes 52
  10.7 0.7 %copy-start.2 = (s32[2]{0:T(128)S(1)}, s32[2]{0:T(128)}, u32[]{:S(2)}) copy-start(s32[2]{0:T(128)} %i_list.1) | copy-start | bytes 28
  11.4 0.9 %copy-start.5 = (bf16[2,256,128]{2,1,0:T(8,128)(2,1)S(1)}, bf16[2,256,128]{2,1,0:T(8,128)(2,1)}, u32[]{:S(2)}) copy-start(bf16[2,256,128]{2,1,0:T(8,128)(2,1)} %param.12) | copy-start | bytes 393220
  12.3 8.5 %collective-permute-start.7 = (bf16[2,2,256,128]{3,2,1,0:T(8,128)(2,1)S(1)}, bf16[2,2,256,128]{3,2,1,0:T(8,128)(2,1)S(1)}, u32[]{:S(2)}, u32[]{:S(2)}) collective-permute-start(bf16[2,2,256,128]{3,2,1,0:T(8,128)(2,1)S(1)} %pad_maximum_fusion.ends), channel_id=1, source_target_pairs={{0,1},{1,0},{2,3},{3,2},{4,5},{5,4},{6,7},{7,6},{8,9},{9,8},{10,11... | collective-permute-start | bytes 786440 | tf_op jit(solution)/shard_map/ppermute | solution.py:249
  13.9 5.0 %collective-permute-start.4 = (bf16[1,256,256]{2,1,0:T(8,128)(2,1)S(1)}, bf16[1,256,256]{2,1,0:T(8,128)(2,1)S(1)}, u32[]{:S(2)}, u32[]{:S(2)}) collective-permute-start(bf16[1,256,256]{2,1,0:T(8,128)(2,1)S(1)} %last_slots.1), channel_id=1, source_target_pairs={{0,8},{8,0},{16,24},{24,16},{1,9},{9,1},{17,25},{25,17},{2,10},{10... | collective-permute-start | bytes 393224 | tf_op jit(solution)/shard_map/ppermute | solution.py:243
  15.7 5.0 %collective-permute-start.3 = (bf16[1,256,256]{2,1,0:T(8,128)(2,1)S(1)}, bf16[1,256,256]{2,1,0:T(8,128)(2,1)S(1)}, u32[]{:S(2)}, u32[]{:S(2)}) collective-permute-start(bf16[1,256,256]{2,1,0:T(8,128)(2,1)S(1)} %first_slots.1), channel_id=1, source_target_pairs={{0,16},{8,24},{16,0},{24,8},{1,17},{9,25},{17,1},{25,9},{2,18},{10... | collective-permute-start | bytes 393224 | tf_op jit(solution)/shard_map/ppermute | solution.py:243
  17.3 3.5 %collective-permute-start.9 = (bf16[2,256,128]{2,1,0:T(8,128)(2,1)S(1)}, bf16[2,256,128]{2,1,0:T(8,128)(2,1)S(1)}, u32[]{:S(2)}, u32[]{:S(2)}) collective-permute-start(bf16[2,256,128]{2,1,0:T(8,128)(2,1)S(1)} %collective-permute-done.6.beside), channel_id=1, source_target_pairs={{0,1},{1,0},{2,3},{3,2},{4,5},{5,4},{6,7},{7,6},{8,9},{9,8},{10,11... | collective-permute-start | bytes 393224 | tf_op jit(solution)/shard_map/ppermute | solution.py:249
  17.3 3.5 %collective-permute-start.8 = (bf16[2,256,128]{2,1,0:T(8,128)(2,1)S(1)}, bf16[2,256,128]{2,1,0:T(8,128)(2,1)S(1)}, u32[]{:S(2)}, u32[]{:S(2)}) collective-permute-start(bf16[2,256,128]{2,1,0:T(8,128)(2,1)S(1)} %collective-permute-done.5.far), channel_id=1, source_target_pairs={{0,1},{1,0},{2,3},{3,2},{4,5},{5,4},{6,7},{7,6},{8,9},{9,8},{10,11... | collective-permute-start | bytes 393224 | tf_op jit(solution)/shard_map/ppermute | solution.py:249
  22.9 2.2 %collective-permute-start.12 = (bf16[4,2,256,128]{3,2,1,0:T(8,128)(2,1)S(1)}, bf16[4,2,256,128]{3,2,1,0:T(8,128)(2,1)S(1)}, u32[]{:S(2)}, u32[]{:S(2)}) collective-permute-start(bf16[4,2,256,128]{3,2,1,0:T(8,128)(2,1)S(1)} %get-tuple-element.29), channel_id=1, source_target_pairs={{0,1},{1,0},{2,3},{3,2},{4,5},{5,4},{6,7},{7,6},{8,9},{9,8},{10,11... | collective-permute-start | bytes 1572872 | tf_op jit(solution)/shard_map/ppermute | solution.py:249
  23.0 8.7 %collective-permute-start.10 = (bf16[2,1,256,256]{3,2,1,0:T(8,128)(2,1)S(1)}, bf16[2,1,256,256]{3,2,1,0:T(8,128)(2,1)S(1)}, u32[]{:S(2)}, u32[]{:S(2)}) collective-permute-start(bf16[2,1,256,256]{3,2,1,0:T(8,128)(2,1)S(1)} %get-tuple-element.26), channel_id=1, source_target_pairs={{0,8},{8,0},{16,24},{24,16},{1,9},{9,1},{17,25},{25,17},{2,10},{10... | collective-permute-start | bytes 786440 | tf_op jit(solution)/shard_map/ppermute | solution.py:243
  24.0 8.4 %collective-permute-start.11 = (bf16[2,1,256,256]{3,2,1,0:T(8,128)(2,1)S(1)}, bf16[2,1,256,256]{3,2,1,0:T(8,128)(2,1)S(1)}, u32[]{:S(2)}, u32[]{:S(2)}) collective-permute-start(bf16[2,1,256,256]{3,2,1,0:T(8,128)(2,1)S(1)} %get-tuple-element.27), channel_id=1, source_target_pairs={{0,16},{8,24},{16,0},{24,8},{1,17},{9,25},{17,1},{25,9},{2,18},{10... | collective-permute-start | bytes 786440 | tf_op jit(solution)/shard_map/ppermute | solution.py:243
  25.2 7.2 %collective-permute-start.13 = (bf16[2,256,128]{2,1,0:T(8,128)(2,1)S(1)}, bf16[2,256,128]{2,1,0:T(8,128)(2,1)S(1)}, u32[]{:S(2)}, u32[]{:S(2)}) collective-permute-start(bf16[2,256,128]{2,1,0:T(8,128)(2,1)S(1)} %get-tuple-element.30), channel_id=1, source_target_pairs={{0,2},{1,3},{2,0},{3,1},{4,6},{5,7},{6,4},{7,5},{8,10},{9,11},{10,... | collective-permute-start | bytes 393224 | tf_op jit(solution)/shard_map/ppermute | solution.py:246
  26.1 12.6 %collective-permute-start.16 = (bf16[2,256,128]{2,1,0:T(8,128)(2,1)S(1)}, bf16[2,256,128]{2,1,0:T(8,128)(2,1)S(1)}, u32[]{:S(2)}, u32[]{:S(2)}) collective-permute-start(bf16[2,256,128]{2,1,0:T(8,128)(2,1)S(1)} %get-tuple-element.40), channel_id=1, source_target_pairs={{0,4},{1,5},{2,6},{3,7},{4,0},{5,1},{6,2},{7,3},{8,12},{9,13},{10,... | collective-permute-start | bytes 393224 | tf_op jit(solution)/shard_map/ppermute | solution.py:246
  27.8 10.9 %collective-permute-start.17 = (bf16[2,256,128]{2,1,0:T(8,128)(2,1)S(1)}, bf16[2,256,128]{2,1,0:T(8,128)(2,1)S(1)}, u32[]{:S(2)}, u32[]{:S(2)}) collective-permute-start(bf16[2,256,128]{2,1,0:T(8,128)(2,1)S(1)} %get-tuple-element.41), channel_id=1, source_target_pairs={{0,6},{1,7},{2,4},{3,5},{4,2},{5,3},{6,0},{7,1},{8,14},{9,15},{10,... | collective-permute-start | bytes 393224 | tf_op jit(solution)/shard_map/ppermute | solution.py:246
  32.5 6.2 %collective-permute-start.15 = (bf16[1,256,256]{2,1,0:T(8,128)(2,1)S(1)}, bf16[1,256,256]{2,1,0:T(8,128)(2,1)S(1)}, u32[]{:S(2)}, u32[]{:S(2)}) collective-permute-start(bf16[1,256,256]{2,1,0:T(8,128)(2,1)S(1)} %get-tuple-element.37), channel_id=1, source_target_pairs={{0,8},{8,0},{16,24},{24,16},{1,9},{9,1},{17,25},{25,17},{2,10},{10... | collective-permute-start | bytes 393224 | tf_op jit(solution)/shard_map/ppermute | solution.py:243
  33.7 5.0 %collective-permute-start.14 = (bf16[1,256,256]{2,1,0:T(8,128)(2,1)S(1)}, bf16[1,256,256]{2,1,0:T(8,128)(2,1)S(1)}, u32[]{:S(2)}, u32[]{:S(2)}) collective-permute-start(bf16[1,256,256]{2,1,0:T(8,128)(2,1)S(1)} %get-tuple-element.33), channel_id=1, source_target_pairs={{0,16},{8,24},{16,0},{24,8},{1,17},{9,25},{17,1},{25,9},{2,18},{10... | collective-permute-start | bytes 393224 | tf_op jit(solution)/shard_map/ppermute | solution.py:243

commit v7 on v5

--- a/solution.py
+++ b/solution.py
@@ -66,12 +66,12 @@
     return (density, amp_grad)
 
 
-def denominators(
-    i_list, pairs, vir_offsets, occ_energy, vir_smem, vir_rows, denom
+def reciprocals(
+    i_list, pairs, vir_offsets, occ_energy, vir_smem, vir_rows, weights
 ):
     n_i, n_pair = i_list.shape[0], pairs.shape[0]
-    block_c = denom.shape[0] // n_pair
-    tile = denom.shape[1] // n_i
+    block_c = weights.shape[0] // n_pair
+    tile = weights.shape[1] // n_i
     width_b = tile // LANES
     row_pos = lax.axis_index("row")
     col_pos = lax.axis_index("col")
@@ -94,7 +94,7 @@
                 + occ_energy[pairs[pair, 1]]
             )
             rows = slice(pair * block_c, (pair + 1) * block_c)
-            denom[rows, slot * tile : (slot + 1) * tile] = occ + base
+            weights[rows, slot * tile : (slot + 1) * tile] = 1.0 / (occ + base)
 
 
 def first_slots(whole, part):
@@ -123,7 +123,7 @@
 
 
 def products(
-    denom,
+    weights,
     ints_full,
     ends,
     far,
@@ -161,7 +161,7 @@
             amp_full[rows, pl.ds(at_other, sub_d)] = other[pair]
 
     triples = jnp.dot(amp_full[...], ints_full[...], preferred_element_type=jnp.float32)
-    scaled = (triples / denom[...]).astype(jnp.bfloat16)
+    scaled = (triples * weights[...]).astype(jnp.bfloat16)
 
     low = core_pos == 0
     for step in range(n_chip):
@@ -262,13 +262,13 @@
             name=kernel.__name__,
         )(whole)
 
-    denom = pl.pallas_call(
-        denominators,
+    weights = pl.pallas_call(
+        reciprocals,
         out_shape=shape((n_pair * block_c, n_i * tile), f32),
         in_specs=[smem] * 5 + [vmem],
         out_specs=vmem,
         compiler_params=room(4),
-        name="denominators",
+        name="reciprocals",
     )(i_list, pairs, vir_offsets, occ_energy, vir_energy, vir_energy.reshape(-1, LANES))
     across, beside, far = [over_chips(amplitudes, step) for step in (3, 1, 2)]
     ints_x, ints_y = over_row(integrals, X_MASK), over_row(integrals, Y_MASK)
@@ -276,7 +276,7 @@
     flat_x, flat_y = flat(ints_x), flat(ints_y)
     ints_xy = over_row(part_of(first_slots, flat_x), Y_MASK)
     ints_yx = over_row(part_of(last_slots, flat_y), X_MASK)
-    across, ints_own, denom = lax.optimization_barrier((across, ints_own, denom))
+    across, ints_own, weights = lax.optimization_barrier((across, ints_own, weights))
     ends = jnp.stack([amplitudes, across])
     other_ends, other_far, other_beside = over_cores(ends), over_cores(far), over_cores(beside)
     ints_full = pl.pallas_call(
@@ -298,7 +298,7 @@
         scratch_shapes=[pltpu.VMEM((n_pair * block_c, width), bf16)],
         compiler_params=room(14),
         name="products",
-    )(denom, ints_full, ends, far, beside, other_ends, other_far, other_beside)
+    )(weights, ints_full, ends, far, beside, other_ends, other_far, other_beside)
     block = (n_pair, block_c, sub_d)
     grads = pl.pallas_call(
         functools.partial(core_sums, n_chip),

time: 39.7 us -> 39.7 us (level)
  no operation moved by 1% of the time
where the time goes in v7:
time: 39.7 us; the launch traced here: 39.5 us
  starting transfers between devices  22 us (55%)
  waiting for transfers between devices  10.5 us (26%)
  Pallas kernels  4.03 us (10%)
  local copies, waits for them, and re-layouts  2.18 us (5%)
  between operations  0.8 us (2%)
    ppermute x8, starting transfers between devices, over_row(): return lax.ppermute(value, 'row', [(k, k ^ mask) for k in range(n_row)])  11 us
    ppermute x6, starting transfers between devices, over_chips(): lax.ppermute(value, 'col', [(k, k ^ CORES * mask) for k in range(n_col)])  10.4 us
    ppermute x8, waiting for transfers between devices, over_row(): return lax.ppermute(value, 'row', [(k, k ^ mask) for k in range(n_row)])  7.03 us
    ppermute x6, waiting for transfers between devices, over_chips(): lax.ppermute(value, 'col', [(k, k ^ CORES * mask) for k in range(n_col)])  3.45 us
    pallas_call x1, Pallas kernels, exchanged(): pl.pallas_call(products, out_shape=[shape(dens_shape, f32), shape(dens_sh...  2.08 us
    reshape x3, local copies, waits for them, and re-layouts, flat(): return value.reshape(value.shape[:2] + (tile,))  1.5 us
    pallas_call x1, Pallas kernels, exchanged(): pl.pallas_call(reciprocals, out_shape=shape((n_pair * block_c, n_i * tile...  0.85 us
    pallas_call x1, Pallas kernels, exchanged(): pl.pallas_call(results, out_shape=[shape((n_i, block_d, width_b, width_a)...  0.81 us
  transfers between devices with their start and end apart: 18, of which 6 were waited for; matrix products, arithmetic and copies ran while one was open for 4% of the time, Pallas kernels for 3%

profile of v7, /device:TPU:0, one launch (start us, length us, event | category | flops | bytes accessed | tf_op | source)
XLA Modules:
  0.0 39.5 jit_solution(7294011977194174808)
XLA Ops:
  0.6 5.1 %collective-permute-start = (bf16[2,256,128]{2,1,0:T(8,128)(2,1)}, bf16[2,256,128]{2,1,0:T(8,128)(2,1)S(1)}, u32[]{:S(2)}, u32[]{:S(2)}) collective-permute-start(bf16[2,256,128]{2,1,0:T(8,128)(2,1)} %param.12), channel_id=1, source_target_pairs={{0,6},{1,7},{2,4},{3,5},{4,2},{5,3},{6,0},{7,1},{8,14},{9,15},{10,... | collective-permute-start | bytes 393224 | tf_op jit(solution)/shard_map/ppermute | solution.py:237
  5.7 1.5 %collective-permute-start.2 = (bf16[2,256,2,128]{3,2,1,0:T(2,128)(2,1)}, bf16[2,256,2,128]{3,2,1,0:T(2,128)(2,1)S(1)}, u32[]{:S(2)}, u32[]{:S(2)}) collective-permute-start(bf16[2,256,2,128]{3,2,1,0:T(2,128)(2,1)} %param.13), channel_id=1, source_target_pairs={{0,16},{8,24},{16,0},{24,8},{1,17},{9,25},{17,1},{25,9},{2,18},{10... | collective-permute-start | bytes 786440 | tf_op jit(solution)/shard_map/ppermute | solution.py:234
  7.3 1.5 %collective-permute-start.1 = (bf16[2,256,2,128]{3,2,1,0:T(2,128)(2,1)}, bf16[2,256,2,128]{3,2,1,0:T(2,128)(2,1)S(1)}, u32[]{:S(2)}, u32[]{:S(2)}) collective-permute-start(bf16[2,256,2,128]{3,2,1,0:T(2,128)(2,1)} %param.13), channel_id=1, source_target_pairs={{0,8},{8,0},{16,24},{24,16},{1,9},{9,1},{17,25},{25,17},{2,10},{10... | collective-permute-start | bytes 786440 | tf_op jit(solution)/shard_map/ppermute | solution.py:234
  8.8 0.0 collective-permute-start.6
  8.8 0.8 %collective-permute-start.5 = (bf16[2,256,128]{2,1,0:T(8,128)(2,1)}, bf16[2,256,128]{2,1,0:T(8,128)(2,1)S(1)}, u32[]{:S(2)}, u32[]{:S(2)}) collective-permute-start(bf16[2,256,128]{2,1,0:T(8,128)(2,1)} %param.12), channel_id=1, source_target_pairs={{0,4},{1,5},{2,6},{3,7},{4,0},{5,1},{6,2},{7,3},{8,12},{9,13},{10,... | collective-permute-start | bytes 393224 | tf_op jit(solution)/shard_map/ppermute | solution.py:237
  9.6 1.2 %reshape.16.own = bf16[2,256,256]{2,1,0:T(8,128)(2,1)S(1)} reshape(bf16[2,256,2,128]{3,2,1,0:T(2,128)(2,1)} %param.13) | data formatting | bytes 524288 | tf_op jit(solution)/shard_map/reshape | solution.py:251
  10.7 0.0 copy-start.1
  10.7 0.0 copy-start.2
  10.8 0.6 %copy-done.1 = s32[2,2]{1,0:T(2,128)S(1)} copy-done((s32[2,2]{1,0:T(2,128)S(1)}, s32[2,2]{1,0:T(2,128)}, u32[]{:S(2)}) %copy-start.1) | copy-done | bytes 40
  11.4 0.9 %reciprocals.1.weights = f32[512,512]{1,0:T(8,128)S(1)} custom-call(s32[2]{0:T(128)S(1)} %copy-done.2, s32[2,2]{1,0:T(2,128)S(1)} %copy-done.1, s32[2]{0:T(128)S(1)} %copy-done.3, f32[128]{0:T(128)S(1)} %copy-done.4, f32[1024]{0:T(1024)S(1)} %copy-done, f32[8,128]{1,0:T(8,128)S(1)} %bitcast.3), custom_call_target="tpu_custom_call" | custom-call | tf_op jit(solution)/shard_map/reciprocals/pallas_call | solution.py:265
  12.3 0.0 collective-permute-done
  12.3 0.0 copy-done.5
  12.3 0.1 collective-permute-start.7
  12.4 1.3 %collective-permute-done.2 = bf16[2,256,2,128]{3,2,1,0:T(2,128)(2,1)S(1)} collective-permute-done((bf16[2,256,2,128]{3,2,1,0:T(2,128)(2,1)}, bf16[2,256,2,128]{3,2,1,0:T(2,128)(2,1)S(1)}, u32[]{:S(2)}, u32[]{:S(2)}) %collective-permute-start.2) | collective-permute-done | bytes 262176 | tf_op jit(solution)/shard_map/ppermute | solution.py:234
  13.7 0.2 reshape.19.whole.near_y
  13.9 1.6 %collective-permute-start.4 = (bf16[1,256,256]{2,1,0:T(8,128)(2,1)S(1)}, bf16[1,256,256]{2,1,0:T(8,128)(2,1)S(1)}, u32[]{:S(2)}, u32[]{:S(2)}) collective-permute-start(bf16[1,256,256]{2,1,0:T(8,128)(2,1)S(1)} %last_slots.1), channel_id=1, source_target_pairs={{0,8},{8,0},{16,24},{24,16},{1,9},{9,1},{17,25},{25,17},{2,10},{10... | collective-permute-start | bytes 393224 | tf_op jit(solution)/shard_map/ppermute | solution.py:234
  15.5 0.0 collective-permute-done.1
  15.5 0.2 reshape.18.whole.near_x
  15.7 1.6 %collective-permute-start.3 = (bf16[1,256,256]{2,1,0:T(8,128)(2,1)S(1)}, bf16[1,256,256]{2,1,0:T(8,128)(2,1)S(1)}, u32[]{:S(2)}, u32[]{:S(2)}) collective-permute-start(bf16[1,256,256]{2,1,0:T(8,128)(2,1)S(1)} %first_slots.1), channel_id=1, source_target_pairs={{0,16},{8,24},{16,0},{24,8},{1,17},{9,25},{17,1},{25,9},{2,18},{10... | collective-permute-start | bytes 393224 | tf_op jit(solution)/shard_map/ppermute | solution.py:234
  17.2 0.0 collective-permute-done.6.beside
  17.3 0.0 collective-permute-start.9
  17.3 0.0 collective-permute-done.5.far
  17.3 0.5 %collective-permute-start.8 = (bf16[2,256,128]{2,1,0:T(8,128)(2,1)S(1)}, bf16[2,256,128]{2,1,0:T(8,128)(2,1)S(1)}, u32[]{:S(2)}, u32[]{:S(2)}) collective-permute-start(bf16[2,256,128]{2,1,0:T(8,128)(2,1)S(1)} %collective-permute-done.5.far), channel_id=1, source_target_pairs={{0,1},{1,0},{2,3},{3,2},{4,5},{5,4},{6,7},{7,6},{8,9},{9,8},{10,11... | collective-permute-start | bytes 393224 | tf_op jit(solution)/shard_map/ppermute | solution.py:240
  17.8 1.2 %collective-permute-done.4.far_yx = bf16[1,256,256]{2,1,0:T(8,128)(2,1)S(1)} collective-permute-done((bf16[1,256,256]{2,1,0:T(8,128)(2,1)S(1)}, bf16[1,256,256]{2,1,0:T(8,128)(2,1)S(1)}, u32[]{:S(2)}, u32[]{:S(2)}) %collective-permute-start.4) | collective-permute-done | bytes 131104 | tf_op jit(solution)/shard_map/ppermute | solution.py:234
  18.9 1.8 %collective-permute-done.3.far_xy = bf16[1,256,256]{2,1,0:T(8,128)(2,1)S(1)} collective-permute-done((bf16[1,256,256]{2,1,0:T(8,128)(2,1)S(1)}, bf16[1,256,256]{2,1,0:T(8,128)(2,1)S(1)}, u32[]{:S(2)}, u32[]{:S(2)}) %collective-permute-start.3) | collective-permute-done | bytes 131104 | tf_op jit(solution)/shard_map/ppermute | solution.py:234
  20.7 0.1 all_rows.1.ints_full
  20.8 0.0 collective-permute-done.9.other_beside
  20.8 0.0 collective-permute-done.8.other_far
  20.8 0.0 collective-permute-done.7.other_ends
  20.8 2.1 %products.1 = (f32[2,1,256,256]{3,2,1,0:T(8,128)S(1)}, bf16[2,1,256,256]{3,2,1,0:T(8,128)(2,1)S(1)}, f32[2,1,256,256]{3,2,1,0:T(8,128)S(1)}, bf16[2,1,256,256]{3...) custom-call(f32[512,512]{1,0:T(8,128)S(1)} %reciprocals.1.weights, ...), custom_call_target="tpu_custom_call" | custom-call | tf_op jit(solution)/shard_map/products/pallas_call | solution.py:292
  22.9 0.1 collective-permute-start.12
  23.0 1.0 %collective-permute-start.10 = (bf16[2,1,256,256]{3,2,1,0:T(8,128)(2,1)S(1)}, bf16[2,1,256,256]{3,2,1,0:T(8,128)(2,1)S(1)}, u32[]{:S(2)}, u32[]{:S(2)}) collective-permute-start(bf16[2,1,256,256]{3,2,1,0:T(8,128)(2,1)S(1)} %get-tuple-element.26), channel_id=1, source_target_pairs={{0,8},{8,0},{16,24},{24,16},{1,9},{9,1},{17,25},{25,17},{2,10},{10... | collective-permute-start | bytes 786440 | tf_op jit(solution)/shard_map/ppermute | solution.py:234
  24.0 1.1 %collective-permute-start.11 = (bf16[2,1,256,256]{3,2,1,0:T(8,128)(2,1)S(1)}, bf16[2,1,256,256]{3,2,1,0:T(8,128)(2,1)S(1)}, u32[]{:S(2)}, u32[]{:S(2)}) collective-permute-start(bf16[2,1,256,256]{3,2,1,0:T(8,128)(2,1)S(1)} %get-tuple-element.27), channel_id=1, source_target_pairs={{0,16},{8,24},{16,0},{24,8},{1,17},{9,25},{17,1},{25,9},{2,18},{10... | collective-permute-start | bytes 786440 | tf_op jit(solution)/shard_map/ppermute | solution.py:234
  25.1 0.0 collective-permute-done.12.received
  25.1 0.1 core_sums.1
  25.2 0.9 %collective-permute-start.13 = (bf16[2,256,128]{2,1,0:T(8,128)(2,1)S(1)}, bf16[2,256,128]{2,1,0:T(8,128)(2,1)S(1)}, u32[]{:S(2)}, u32[]{:S(2)}) collective-permute-start(bf16[2,256,128]{2,1,0:T(8,128)(2,1)S(1)} %get-tuple-element.30), channel_id=1, source_target_pairs={{0,2},{1,3},{2,0},{3,1},{4,6},{5,7},{6,4},{7,5},{8,10},{9,11},{10,... | collective-permute-start | bytes 393224 | tf_op jit(solution)/shard_map/ppermute | solution.py:237
  26.1 1.7 %collective-permute-start.16 = (bf16[2,256,128]{2,1,0:T(8,128)(2,1)S(1)}, bf16[2,256,128]{2,1,0:T(8,128)(2,1)S(1)}, u32[]{:S(2)}, u32[]{:S(2)}) collective-permute-start(bf16[2,256,128]{2,1,0:T(8,128)(2,1)S(1)} %get-tuple-element.40), channel_id=1, source_target_pairs={{0,4},{1,5},{2,6},{3,7},{4,0},{5,1},{6,2},{7,3},{8,12},{9,13},{10,... | collective-permute-start | bytes 393224 | tf_op jit(solution)/shard_map/ppermute | solution.py:237
  27.8 1.9 %collective-permute-start.17 = (bf16[2,256,128]{2,1,0:T(8,128)(2,1)S(1)}, bf16[2,256,128]{2,1,0:T(8,128)(2,1)S(1)}, u32[]{:S(2)}, u32[]{:S(2)}) collective-permute-start(bf16[2,256,128]{2,1,0:T(8,128)(2,1)S(1)} %get-tuple-element.41), channel_id=1, source_target_pairs={{0,6},{1,7},{2,4},{3,5},{4,2},{5,3},{6,0},{7,1},{8,14},{9,15},{10,... | collective-permute-start | bytes 393224 | tf_op jit(solution)/shard_map/ppermute | solution.py:237
  29.7 2.0 %collective-permute-done.10.received = bf16[2,1,256,256]{3,2,1,0:T(8,128)(2,1)S(1)} collective-permute-done((bf16[2,1,256,256]{3,2,1,0:T(8,128)(2,1)S(1)}, bf16[2,1,256,256]{3,2,1,0:T(8,128)(2,1)S(1)}, u32[]{:S(2)}, u32[]{:S(2)}) %collective-permute-start.10) | collective-permute-done | bytes 262176 | tf_op jit(solution)/shard_map/ppermute | solution.py:234
  31.7 0.7 %collective-permute-done.11.received = bf16[2,1,256,256]{3,2,1,0:T(8,128)(2,1)S(1)} collective-permute-done((bf16[2,1,256,256]{3,2,1,0:T(8,128)(2,1)S(1)}, bf16[2,1,256,256]{3,2,1,0:T(8,128)(2,1)S(1)}, u32[]{:S(2)}, u32[]{:S(2)}) %collective-permute-start.11) | collective-permute-done | bytes 262176 | tf_op jit(solution)/shard_map/ppermute | solution.py:234
  32.4 0.0 collective-permute-done.13.refs_0_
  32.5 1.1 %collective-permute-start.15 = (bf16[1,256,256]{2,1,0:T(8,128)(2,1)S(1)}, bf16[1,256,256]{2,1,0:T(8,128)(2,1)S(1)}, u32[]{:S(2)}, u32[]{:S(2)}) collective-permute-start(bf16[1,256,256]{2,1,0:T(8,128)(2,1)S(1)} %get-tuple-element.37), channel_id=1, source_target_pairs={{0,8},{8,0},{16,24},{24,16},{1,9},{9,1},{17,25},{25,17},{2,10},{10... | collective-permute-start | bytes 393224 | tf_op jit(solution)/shard_map/ppermute | solution.py:234
  33.6 1.6 %collective-permute-start.14 = (bf16[1,256,256]{2,1,0:T(8,128)(2,1)S(1)}, bf16[1,256,256]{2,1,0:T(8,128)(2,1)S(1)}, u32[]{:S(2)}, u32[]{:S(2)}) collective-permute-start(bf16[1,256,256]{2,1,0:T(8,128)(2,1)S(1)} %get-tuple-element.33), channel_id=1, source_target_pairs={{0,16},{8,24},{16,0},{24,8},{1,17},{9,25},{17,1},{25,9},{2,18},{10... | collective-permute-start | bytes 393224 | tf_op jit(solution)/shard_map/ppermute | solution.py:234
  35.2 3.4 %collective-permute-done.16.refs_1_ = bf16[2,256,128]{2,1,0:T(8,128)(2,1)S(1)} collective-permute-done((bf16[2,256,128]{2,1,0:T(8,128)(2,1)S(1)}, bf16[2,256,128]{2,1,0:T(8,128)(2,1)S(1)}, u32[]{:S(2)}, u32[]{:S(2)}) %collective-permute-start.16) | collective-permute-done | bytes 131104 | tf_op jit(solution)/shard_map/ppermute | solution.py:237
  38.6 0.0 collective-permute-done.17.refs_2_
  38.6 0.0 collective-permute-done.15.last_y
  38.7 0.0 collective-permute-done.14.last_x
  38.7 0.8 %results.1 = (bf16[2,256,2,128]{3,2,1,0:T(2,128)(2,1)}, bf16[2,256,128]{2,1,0:T(8,128)(2,1)}) custom-call(f32[1,256,256]{2,1,0:T(8,128)S(1)} %get-tuple-element.32.own_x, bf16[1,256,256]{2,1,0:T(8,128)(2,1)S(1)} %collective-permute-done.14.last_x, f32[1,256,256]{2,1,0:T(8,128)S(1)} %get-tuple-element.36.own_y, ...), custom_call_target="tpu_custom_call" | custom-call | tf_op jit(solution)/shard_map/results/pallas_call | solution.py:328
  (13 shorter events, 0.2 us)
Async XLA Ops:
  0.6 11.6 %collective-permute-start = (bf16[2,256,128]{2,1,0:T(8,128)(2,1)}, bf16[2,256,128]{2,1,0:T(8,128)(2,1)S(1)}, u32[]{:S(2)}, u32[]{:S(2)}) collective-permute-start(bf16[2,256,128]{2,1,0:T(8,128)(2,1)} %param.12), channel_id=1, source_target_pairs={{0,6},{1,7},{2,4},{3,5},{4,2},{5,3},{6,0},{7,1},{8,14},{9,15},{10,... | collective-permute-start | bytes 393224 | tf_op jit(solution)/shard_map/ppermute | solution.py:237
  5.7 8.0 %collective-permute-start.2 = (bf16[2,256,2,128]{3,2,1,0:T(2,128)(2,1)}, bf16[2,256,2,128]{3,2,1,0:T(2,128)(2,1)S(1)}, u32[]{:S(2)}, u32[]{:S(2)}) collective-permute-start(bf16[2,256,2,128]{3,2,1,0:T(2,128)(2,1)} %param.13), channel_id=1, source_target_pairs={{0,16},{8,24},{16,0},{24,8},{1,17},{9,25},{17,1},{25,9},{2,18},{10... | collective-permute-start | bytes 786440 | tf_op jit(solution)/shard_map/ppermute | solution.py:234
  7.3 8.2 %collective-permute-start.1 = (bf16[2,256,2,128]{3,2,1,0:T(2,128)(2,1)}, bf16[2,256,2,128]{3,2,1,0:T(2,128)(2,1)S(1)}, u32[]{:S(2)}, u32[]{:S(2)}) collective-permute-start(bf16[2,256,2,128]{3,2,1,0:T(2,128)(2,1)} %param.13), channel_id=1, source_target_pairs={{0,8},{8,0},{16,24},{24,16},{1,9},{9,1},{17,25},{25,17},{2,10},{10... | collective-permute-start | bytes 786440 | tf_op jit(solution)/shard_map/ppermute | solution.py:234
  8.8 8.5 %collective-permute-start.6 = (bf16[2,256,128]{2,1,0:T(8,128)(2,1)}, bf16[2,256,128]{2,1,0:T(8,128)(2,1)S(1)}, u32[]{:S(2)}, u32[]{:S(2)}) collective-permute-start(bf16[2,256,128]{2,1,0:T(8,128)(2,1)} %param.12), channel_id=1, source_target_pairs={{0,2},{1,3},{2,0},{3,1},{4,6},{5,7},{6,4},{7,5},{8,10},{9,11},{10,... | collective-permute-start | bytes 393224 | tf_op jit(solution)/shard_map/ppermute | solution.py:237
  8.8 8.5 %collective-permute-start.5 = (bf16[2,256,128]{2,1,0:T(8,128)(2,1)}, bf16[2,256,128]{2,1,0:T(8,128)(2,1)S(1)}, u32[]{:S(2)}, u32[]{:S(2)}) collective-permute-start(bf16[2,256,128]{2,1,0:T(8,128)(2,1)} %param.12), channel_id=1, source_target_pairs={{0,4},{1,5},{2,6},{3,7},{4,0},{5,1},{6,2},{7,3},{8,12},{9,13},{10,... | collective-permute-start | bytes 393224 | tf_op jit(solution)/shard_map/ppermute | solution.py:237
  9.5 1.2 %copy-start = (f32[1024]{0:T(1024)S(1)}, f32[1024]{0:T(1024)}, u32[]{:S(2)}) copy-start(f32[1024]{0:T(1024)} %vir_smem.1) | copy-start | bytes 12292
  9.5 1.2 %copy-start.3 = (s32[2]{0:T(128)S(1)}, s32[2]{0:T(128)}, u32[]{:S(2)}) copy-start(s32[2]{0:T(128)} %vir_offsets.1) | copy-start | bytes 28
  9.5 1.2 %copy-start.4 = (f32[128]{0:T(128)S(1)}, f32[128]{0:T(128)}, u32[]{:S(2)}) copy-start(f32[128]{0:T(128)} %occ_energy.1) | copy-start | bytes 1540
  10.7 0.7 %copy-start.1 = (s32[2,2]{1,0:T(2,128)S(1)}, s32[2,2]{1,0:T(2,128)}, u32[]{:S(2)}) copy-start(s32[2,2]{1,0:T(2,128)} %pairs.1) | copy-start | bytes 52
  10.7 0.7 %copy-start.2 = (s32[2]{0:T(128)S(1)}, s32[2]{0:T(128)}, u32[]{:S(2)}) copy-start(s32[2]{0:T(128)} %i_list.1) | copy-start | bytes 28
  11.4 0.9 %copy-start.5 = (bf16[2,256,128]{2,1,0:T(8,128)(2,1)S(1)}, bf16[2,256,128]{2,1,0:T(8,128)(2,1)}, u32[]{:S(2)}) copy-start(bf16[2,256,128]{2,1,0:T(8,128)(2,1)} %param.12) | copy-start | bytes 393220
  12.3 8.5 %collective-permute-start.7 = (bf16[2,2,256,128]{3,2,1,0:T(8,128)(2,1)S(1)}, bf16[2,2,256,128]{3,2,1,0:T(8,128)(2,1)S(1)}, u32[]{:S(2)}, u32[]{:S(2)}) collective-permute-start(bf16[2,2,256,128]{3,2,1,0:T(8,128)(2,1)S(1)} %pad_maximum_fusion.ends), channel_id=1, source_target_pairs={{0,1},{1,0},{2,3},{3,2},{4,5},{5,4},{6,7},{7,6},{8,9},{9,8},{10,11... | collective-permute-start | bytes 786440 | tf_op jit(solution)/shard_map/ppermute | solution.py:240
  13.9 5.0 %collective-permute-start.4 = (bf16[1,256,256]{2,1,0:T(8,128)(2,1)S(1)}, bf16[1,256,256]{2,1,0:T(8,128)(2,1)S(1)}, u32[]{:S(2)}, u32[]{:S(2)}) collective-permute-start(bf16[1,256,256]{2,1,0:T(8,128)(2,1)S(1)} %last_slots.1), channel_id=1, source_target_pairs={{0,8},{8,0},{16,24},{24,16},{1,9},{9,1},{17,25},{25,17},{2,10},{10... | collective-permute-start | bytes 393224 | tf_op jit(solution)/shard_map/ppermute | solution.py:234
  15.7 5.0 %collective-permute-start.3 = (bf16[1,256,256]{2,1,0:T(8,128)(2,1)S(1)}, bf16[1,256,256]{2,1,0:T(8,128)(2,1)S(1)}, u32[]{:S(2)}, u32[]{:S(2)}) collective-permute-start(bf16[1,256,256]{2,1,0:T(8,128)(2,1)S(1)} %first_slots.1), channel_id=1, source_target_pairs={{0,16},{8,24},{16,0},{24,8},{1,17},{9,25},{17,1},{25,9},{2,18},{10... | collective-permute-start | bytes 393224 | tf_op jit(solution)/shard_map/ppermute | solution.py:234
  17.3 3.5 %collective-permute-start.9 = (bf16[2,256,128]{2,1,0:T(8,128)(2,1)S(1)}, bf16[2,256,128]{2,1,0:T(8,128)(2,1)S(1)}, u32[]{:S(2)}, u32[]{:S(2)}) collective-permute-start(bf16[2,256,128]{2,1,0:T(8,128)(2,1)S(1)} %collective-permute-done.6.beside), channel_id=1, source_target_pairs={{0,1},{1,0},{2,3},{3,2},{4,5},{5,4},{6,7},{7,6},{8,9},{9,8},{10,11... | collective-permute-start | bytes 393224 | tf_op jit(solution)/shard_map/ppermute | solution.py:240
  17.3 3.5 %collective-permute-start.8 = (bf16[2,256,128]{2,1,0:T(8,128)(2,1)S(1)}, bf16[2,256,128]{2,1,0:T(8,128)(2,1)S(1)}, u32[]{:S(2)}, u32[]{:S(2)}) collective-permute-start(bf16[2,256,128]{2,1,0:T(8,128)(2,1)S(1)} %collective-permute-done.5.far), channel_id=1, source_target_pairs={{0,1},{1,0},{2,3},{3,2},{4,5},{5,4},{6,7},{7,6},{8,9},{9,8},{10,11... | collective-permute-start | bytes 393224 | tf_op jit(solution)/shard_map/ppermute | solution.py:240
  22.9 2.2 %collective-permute-start.12 = (bf16[4,2,256,128]{3,2,1,0:T(8,128)(2,1)S(1)}, bf16[4,2,256,128]{3,2,1,0:T(8,128)(2,1)S(1)}, u32[]{:S(2)}, u32[]{:S(2)}) collective-permute-start(bf16[4,2,256,128]{3,2,1,0:T(8,128)(2,1)S(1)} %get-tuple-element.29), channel_id=1, source_target_pairs={{0,1},{1,0},{2,3},{3,2},{4,5},{5,4},{6,7},{7,6},{8,9},{9,8},{10,11... | collective-permute-start | bytes 1572872 | tf_op jit(solution)/shard_map/ppermute | solution.py:240
  23.0 8.7 %collective-permute-start.10 = (bf16[2,1,256,256]{3,2,1,0:T(8,128)(2,1)S(1)}, bf16[2,1,256,256]{3,2,1,0:T(8,128)(2,1)S(1)}, u32[]{:S(2)}, u32[]{:S(2)}) collective-permute-start(bf16[2,1,256,256]{3,2,1,0:T(8,128)(2,1)S(1)} %get-tuple-element.26), channel_id=1, source_target_pairs={{0,8},{8,0},{16,24},{24,16},{1,9},{9,1},{17,25},{25,17},{2,10},{10... | collective-permute-start | bytes 786440 | tf_op jit(solution)/shard_map/ppermute | solution.py:234
  24.0 8.4 %collective-permute-start.11 = (bf16[2,1,256,256]{3,2,1,0:T(8,128)(2,1)S(1)}, bf16[2,1,256,256]{3,2,1,0:T(8,128)(2,1)S(1)}, u32[]{:S(2)}, u32[]{:S(2)}) collective-permute-start(bf16[2,1,256,256]{3,2,1,0:T(8,128)(2,1)S(1)} %get-tuple-element.27), channel_id=1, source_target_pairs={{0,16},{8,24},{16,0},{24,8},{1,17},{9,25},{17,1},{25,9},{2,18},{10... | collective-permute-start | bytes 786440 | tf_op jit(solution)/shard_map/ppermute | solution.py:234
  25.2 7.2 %collective-permute-start.13 = (bf16[2,256,128]{2,1,0:T(8,128)(2,1)S(1)}, bf16[2,256,128]{2,1,0:T(8,128)(2,1)S(1)}, u32[]{:S(2)}, u32[]{:S(2)}) collective-permute-start(bf16[2,256,128]{2,1,0:T(8,128)(2,1)S(1)} %get-tuple-element.30), channel_id=1, source_target_pairs={{0,2},{1,3},{2,0},{3,1},{4,6},{5,7},{6,4},{7,5},{8,10},{9,11},{10,... | collective-permute-start | bytes 393224 | tf_op jit(solution)/shard_map/ppermute | solution.py:237
  26.1 12.6 %collective-permute-start.16 = (bf16[2,256,128]{2,1,0:T(8,128)(2,1)S(1)}, bf16[2,256,128]{2,1,0:T(8,128)(2,1)S(1)}, u32[]{:S(2)}, u32[]{:S(2)}) collective-permute-start(bf16[2,256,128]{2,1,0:T(8,128)(2,1)S(1)} %get-tuple-element.40), channel_id=1, source_target_pairs={{0,4},{1,5},{2,6},{3,7},{4,0},{5,1},{6,2},{7,3},{8,12},{9,13},{10,... | collective-permute-start | bytes 393224 | tf_op jit(solution)/shard_map/ppermute | solution.py:237
  27.8 10.9 %collective-permute-start.17 = (bf16[2,256,128]{2,1,0:T(8,128)(2,1)S(1)}, bf16[2,256,128]{2,1,0:T(8,128)(2,1)S(1)}, u32[]{:S(2)}, u32[]{:S(2)}) collective-permute-start(bf16[2,256,128]{2,1,0:T(8,128)(2,1)S(1)} %get-tuple-element.41), channel_id=1, source_target_pairs={{0,6},{1,7},{2,4},{3,5},{4,2},{5,3},{6,0},{7,1},{8,14},{9,15},{10,... | collective-permute-start | bytes 393224 | tf_op jit(solution)/shard_map/ppermute | solution.py:237
  32.5 6.2 %collective-permute-start.15 = (bf16[1,256,256]{2,1,0:T(8,128)(2,1)S(1)}, bf16[1,256,256]{2,1,0:T(8,128)(2,1)S(1)}, u32[]{:S(2)}, u32[]{:S(2)}) collective-permute-start(bf16[1,256,256]{2,1,0:T(8,128)(2,1)S(1)} %get-tuple-element.37), channel_id=1, source_target_pairs={{0,8},{8,0},{16,24},{24,16},{1,9},{9,1},{17,25},{25,17},{2,10},{10... | collective-permute-start | bytes 393224 | tf_op jit(solution)/shard_map/ppermute | solution.py:234
  33.6 5.0 %collective-permute-start.14 = (bf16[1,256,256]{2,1,0:T(8,128)(2,1)S(1)}, bf16[1,256,256]{2,1,0:T(8,128)(2,1)S(1)}, u32[]{:S(2)}, u32[]{:S(2)}) collective-permute-start(bf16[1,256,256]{2,1,0:T(8,128)(2,1)S(1)} %get-tuple-element.33), channel_id=1, source_target_pairs={{0,16},{8,24},{16,0},{24,8},{1,17},{9,25},{17,1},{25,9},{2,18},{10... | collective-permute-start | bytes 393224 | tf_op jit(solution)/shard_map/ppermute | solution.py:234

commit v8 on v5

--- a/solution.py
+++ b/solution.py
@@ -320,8 +320,8 @@
         )(keep, received)
 
     from_x, from_y = over_row(send_x, X_MASK), over_row(send_y, Y_MASK)
-    grad_parts = [over_chips(grads[step], step) for step in range(1, n_chip)]
-    from_x, from_y, grad_parts[0] = lax.optimization_barrier((from_x, from_y, grad_parts[0]))
+    near, far, across = [over_chips(grads[step], step) for step in range(1, n_chip)]
+    from_x, from_y, near = lax.optimization_barrier((from_x, from_y, near))
     own_x, onward_x = summed(keep_x, from_x)
     own_y, onward_y = summed(keep_y, from_y)
     last_x, last_y = over_row(onward_x, Y_MASK), over_row(onward_y, X_MASK)
@@ -332,7 +332,7 @@
         out_specs=[vmem] * 2,
         compiler_params=room(6),
         name="results",
-    )(own_x, last_x, own_y, last_y, grads[0], *grad_parts)
+    )(own_x, last_x, own_y, last_y, grads[0], far, near, across)
     return density, amp_grad
 
 

time: 39.7 us -> 39.7 us (level)
  no operation moved by 1% of the time
where the time goes in v8:
time: 39.7 us; the launch traced here: 39.5 us
  starting transfers between devices  22 us (55%)
  waiting for transfers between devices  10.5 us (26%)
  Pallas kernels  3.96 us (10%)
  local copies, waits for them, and re-layouts  2.25 us (6%)
  between operations  0.8 us (2%)
    ppermute x8, starting transfers between devices, over_row(): return lax.ppermute(value, 'row', [(k, k ^ mask) for k in range(n_row)])  11 us
    ppermute x6, starting transfers between devices, over_chips(): lax.ppermute(value, 'col', [(k, k ^ CORES * mask) for k in range(n_col)])  10.4 us
    ppermute x8, waiting for transfers between devices, over_row(): return lax.ppermute(value, 'row', [(k, k ^ mask) for k in range(n_row)])  7.03 us
    ppermute x6, waiting for transfers between devices, over_chips(): lax.ppermute(value, 'col', [(k, k ^ CORES * mask) for k in range(n_col)])  3.44 us
    pallas_call x1, Pallas kernels, exchanged(): pl.pallas_call(products, out_shape=[shape(dens_shape, f32), shape(dens_sh...  2.09 us
    reshape x3, local copies, waits for them, and re-layouts, flat(): return value.reshape(value.shape[:2] + (tile,))  1.5 us
    pallas_call x1, Pallas kernels, exchanged(): pl.pallas_call(results, out_shape=[shape((n_i, block_d, width_b, width_a)...  0.81 us
  transfers between devices with their start and end apart: 18, of which 6 were waited for; matrix products, arithmetic and copies ran while one was open for 4% of the time, Pallas kernels for 3%

profile of v8, /device:TPU:0, one launch (start us, length us, event | category | flops | bytes accessed | tf_op | source)
XLA Modules:
  0.0 39.5 jit_solution(17249615965993312788)
XLA Ops:
  0.6 5.1 %collective-permute-start = (bf16[2,256,128]{2,1,0:T(8,128)(2,1)}, bf16[2,256,128]{2,1,0:T(8,128)(2,1)S(1)}, u32[]{:S(2)}, u32[]{:S(2)}) collective-permute-start(bf16[2,256,128]{2,1,0:T(8,128)(2,1)} %param.12), channel_id=1, source_target_pairs={{0,6},{1,7},{2,4},{3,5},{4,2},{5,3},{6,0},{7,1},{8,14},{9,15},{10,... | collective-permute-start | bytes 393224 | tf_op jit(solution)/shard_map/ppermute | solution.py:237
  5.7 1.5 %collective-permute-start.2 = (bf16[2,256,2,128]{3,2,1,0:T(2,128)(2,1)}, bf16[2,256,2,128]{3,2,1,0:T(2,128)(2,1)S(1)}, u32[]{:S(2)}, u32[]{:S(2)}) collective-permute-start(bf16[2,256,2,128]{3,2,1,0:T(2,128)(2,1)} %param.13), channel_id=1, source_target_pairs={{0,16},{8,24},{16,0},{24,8},{1,17},{9,25},{17,1},{25,9},{2,18},{10... | collective-permute-start | bytes 786440 | tf_op jit(solution)/shard_map/ppermute | solution.py:234
  7.3 1.5 %collective-permute-start.1 = (bf16[2,256,2,128]{3,2,1,0:T(2,128)(2,1)}, bf16[2,256,2,128]{3,2,1,0:T(2,128)(2,1)S(1)}, u32[]{:S(2)}, u32[]{:S(2)}) collective-permute-start(bf16[2,256,2,128]{3,2,1,0:T(2,128)(2,1)} %param.13), channel_id=1, source_target_pairs={{0,8},{8,0},{16,24},{24,16},{1,9},{9,1},{17,25},{25,17},{2,10},{10... | collective-permute-start | bytes 786440 | tf_op jit(solution)/shard_map/ppermute | solution.py:234
  8.8 0.0 collective-permute-start.6
  8.8 0.8 %collective-permute-start.5 = (bf16[2,256,128]{2,1,0:T(8,128)(2,1)}, bf16[2,256,128]{2,1,0:T(8,128)(2,1)S(1)}, u32[]{:S(2)}, u32[]{:S(2)}) collective-permute-start(bf16[2,256,128]{2,1,0:T(8,128)(2,1)} %param.12), channel_id=1, source_target_pairs={{0,4},{1,5},{2,6},{3,7},{4,0},{5,1},{6,2},{7,3},{8,12},{9,13},{10,... | collective-permute-start | bytes 393224 | tf_op jit(solution)/shard_map/ppermute | solution.py:237
  9.6 1.2 %reshape.16.own = bf16[2,256,256]{2,1,0:T(8,128)(2,1)S(1)} reshape(bf16[2,256,2,128]{3,2,1,0:T(2,128)(2,1)} %param.13) | data formatting | bytes 524288 | tf_op jit(solution)/shard_map/reshape | solution.py:251
  10.7 0.0 copy-start.1
  10.7 0.0 copy-start.2
  10.8 0.6 %copy-done.1 = s32[2,2]{1,0:T(2,128)S(1)} copy-done((s32[2,2]{1,0:T(2,128)S(1)}, s32[2,2]{1,0:T(2,128)}, u32[]{:S(2)}) %copy-start.1) | copy-done | bytes 40
  11.4 0.8 %denominators.1.denom = f32[512,512]{1,0:T(8,128)S(1)} custom-call(s32[2]{0:T(128)S(1)} %copy-done.2, s32[2,2]{1,0:T(2,128)S(1)} %copy-done.1, s32[2]{0:T(128)S(1)} %copy-done.3, f32[128]{0:T(128)S(1)} %copy-done.4, f32[1024]{0:T(1024)S(1)} %copy-done, f32[8,128]{1,0:T(8,128)S(1)} %bitcast.3), custom_call_target="tpu_custom_call" | custom-call | tf_op jit(solution)/shard_map/denominators/pallas_call | solution.py:265
  12.2 0.0 collective-permute-done
  12.2 0.1 copy-done.5
  12.3 0.1 collective-permute-start.7
  12.4 1.3 %collective-permute-done.2 = bf16[2,256,2,128]{3,2,1,0:T(2,128)(2,1)S(1)} collective-permute-done((bf16[2,256,2,128]{3,2,1,0:T(2,128)(2,1)}, bf16[2,256,2,128]{3,2,1,0:T(2,128)(2,1)S(1)}, u32[]{:S(2)}, u32[]{:S(2)}) %collective-permute-start.2) | collective-permute-done | bytes 262176 | tf_op jit(solution)/shard_map/ppermute | solution.py:234
  13.7 0.2 reshape.19.whole.near_y
  13.9 1.6 %collective-permute-start.4 = (bf16[1,256,256]{2,1,0:T(8,128)(2,1)S(1)}, bf16[1,256,256]{2,1,0:T(8,128)(2,1)S(1)}, u32[]{:S(2)}, u32[]{:S(2)}) collective-permute-start(bf16[1,256,256]{2,1,0:T(8,128)(2,1)S(1)} %last_slots.1), channel_id=1, source_target_pairs={{0,8},{8,0},{16,24},{24,16},{1,9},{9,1},{17,25},{25,17},{2,10},{10... | collective-permute-start | bytes 393224 | tf_op jit(solution)/shard_map/ppermute | solution.py:234
  15.5 0.0 collective-permute-done.1
  15.5 0.2 reshape.18.whole.near_x
  15.7 1.6 %collective-permute-start.3 = (bf16[1,256,256]{2,1,0:T(8,128)(2,1)S(1)}, bf16[1,256,256]{2,1,0:T(8,128)(2,1)S(1)}, u32[]{:S(2)}, u32[]{:S(2)}) collective-permute-start(bf16[1,256,256]{2,1,0:T(8,128)(2,1)S(1)} %first_slots.1), channel_id=1, source_target_pairs={{0,16},{8,24},{16,0},{24,8},{1,17},{9,25},{17,1},{25,9},{2,18},{10... | collective-permute-start | bytes 393224 | tf_op jit(solution)/shard_map/ppermute | solution.py:234
  17.2 0.0 collective-permute-done.6.beside
  17.3 0.0 collective-permute-start.9
  17.3 0.0 collective-permute-done.5.far
  17.3 0.5 %collective-permute-start.8 = (bf16[2,256,128]{2,1,0:T(8,128)(2,1)S(1)}, bf16[2,256,128]{2,1,0:T(8,128)(2,1)S(1)}, u32[]{:S(2)}, u32[]{:S(2)}) collective-permute-start(bf16[2,256,128]{2,1,0:T(8,128)(2,1)S(1)} %collective-permute-done.5.far), channel_id=1, source_target_pairs={{0,1},{1,0},{2,3},{3,2},{4,5},{5,4},{6,7},{7,6},{8,9},{9,8},{10,11... | collective-permute-start | bytes 393224 | tf_op jit(solution)/shard_map/ppermute | solution.py:240
  17.8 1.2 %collective-permute-done.4.far_yx = bf16[1,256,256]{2,1,0:T(8,128)(2,1)S(1)} collective-permute-done((bf16[1,256,256]{2,1,0:T(8,128)(2,1)S(1)}, bf16[1,256,256]{2,1,0:T(8,128)(2,1)S(1)}, u32[]{:S(2)}, u32[]{:S(2)}) %collective-permute-start.4) | collective-permute-done | bytes 131104 | tf_op jit(solution)/shard_map/ppermute | solution.py:234
  18.9 1.8 %collective-permute-done.3.far_xy = bf16[1,256,256]{2,1,0:T(8,128)(2,1)S(1)} collective-permute-done((bf16[1,256,256]{2,1,0:T(8,128)(2,1)S(1)}, bf16[1,256,256]{2,1,0:T(8,128)(2,1)S(1)}, u32[]{:S(2)}, u32[]{:S(2)}) %collective-permute-start.3) | collective-permute-done | bytes 131104 | tf_op jit(solution)/shard_map/ppermute | solution.py:234
  20.7 0.1 all_rows.1.ints_full
  20.8 0.0 collective-permute-done.9.other_beside
  20.8 0.0 collective-permute-done.8.other_far
  20.8 0.0 collective-permute-done.7.other_ends
  20.8 2.1 %products.1 = (f32[2,1,256,256]{3,2,1,0:T(8,128)S(1)}, bf16[2,1,256,256]{3,2,1,0:T(8,128)(2,1)S(1)}, f32[2,1,256,256]{3,2,1,0:T(8,128)S(1)}, bf16[2,1,256,256]{3...) custom-call(f32[512,512]{1,0:T(8,128)S(1)} %denominators.1.denom, ...), custom_call_target="tpu_custom_call" | custom-call | tf_op jit(solution)/shard_map/products/pallas_call | solution.py:292
  22.9 0.1 collective-permute-start.12
  23.0 1.0 %collective-permute-start.10 = (bf16[2,1,256,256]{3,2,1,0:T(8,128)(2,1)S(1)}, bf16[2,1,256,256]{3,2,1,0:T(8,128)(2,1)S(1)}, u32[]{:S(2)}, u32[]{:S(2)}) collective-permute-start(bf16[2,1,256,256]{3,2,1,0:T(8,128)(2,1)S(1)} %get-tuple-element.26), channel_id=1, source_target_pairs={{0,8},{8,0},{16,24},{24,16},{1,9},{9,1},{17,25},{25,17},{2,10},{10... | collective-permute-start | bytes 786440 | tf_op jit(solution)/shard_map/ppermute | solution.py:234
  24.0 1.1 %collective-permute-start.11 = (bf16[2,1,256,256]{3,2,1,0:T(8,128)(2,1)S(1)}, bf16[2,1,256,256]{3,2,1,0:T(8,128)(2,1)S(1)}, u32[]{:S(2)}, u32[]{:S(2)}) collective-permute-start(bf16[2,1,256,256]{3,2,1,0:T(8,128)(2,1)S(1)} %get-tuple-element.27), channel_id=1, source_target_pairs={{0,16},{8,24},{16,0},{24,8},{1,17},{9,25},{17,1},{25,9},{2,18},{10... | collective-permute-start | bytes 786440 | tf_op jit(solution)/shard_map/ppermute | solution.py:234
  25.1 0.0 collective-permute-done.12.received
  25.1 0.1 core_sums.1
  25.2 0.9 %collective-permute-start.13 = (bf16[2,256,128]{2,1,0:T(8,128)(2,1)S(1)}, bf16[2,256,128]{2,1,0:T(8,128)(2,1)S(1)}, u32[]{:S(2)}, u32[]{:S(2)}) collective-permute-start(bf16[2,256,128]{2,1,0:T(8,128)(2,1)S(1)} %get-tuple-element.30), channel_id=1, source_target_pairs={{0,2},{1,3},{2,0},{3,1},{4,6},{5,7},{6,4},{7,5},{8,10},{9,11},{10,... | collective-permute-start | bytes 393224 | tf_op jit(solution)/shard_map/ppermute | solution.py:237
  26.1 1.7 %collective-permute-start.16 = (bf16[2,256,128]{2,1,0:T(8,128)(2,1)S(1)}, bf16[2,256,128]{2,1,0:T(8,128)(2,1)S(1)}, u32[]{:S(2)}, u32[]{:S(2)}) collective-permute-start(bf16[2,256,128]{2,1,0:T(8,128)(2,1)S(1)} %get-tuple-element.39), channel_id=1, source_target_pairs={{0,4},{1,5},{2,6},{3,7},{4,0},{5,1},{6,2},{7,3},{8,12},{9,13},{10,... | collective-permute-start | bytes 393224 | tf_op jit(solution)/shard_map/ppermute | solution.py:237
  27.8 1.9 %collective-permute-start.17 = (bf16[2,256,128]{2,1,0:T(8,128)(2,1)S(1)}, bf16[2,256,128]{2,1,0:T(8,128)(2,1)S(1)}, u32[]{:S(2)}, u32[]{:S(2)}) collective-permute-start(bf16[2,256,128]{2,1,0:T(8,128)(2,1)S(1)} %get-tuple-element.41), channel_id=1, source_target_pairs={{0,6},{1,7},{2,4},{3,5},{4,2},{5,3},{6,0},{7,1},{8,14},{9,15},{10,... | collective-permute-start | bytes 393224 | tf_op jit(solution)/shard_map/ppermute | solution.py:237
  29.7 2.1 %collective-permute-done.10.received = bf16[2,1,256,256]{3,2,1,0:T(8,128)(2,1)S(1)} collective-permute-done((bf16[2,1,256,256]{3,2,1,0:T(8,128)(2,1)S(1)}, bf16[2,1,256,256]{3,2,1,0:T(8,128)(2,1)S(1)}, u32[]{:S(2)}, u32[]{:S(2)}) %collective-permute-start.10) | collective-permute-done | bytes 262176 | tf_op jit(solution)/shard_map/ppermute | solution.py:234
  31.7 0.7 %collective-permute-done.11.received = bf16[2,1,256,256]{3,2,1,0:T(8,128)(2,1)S(1)} collective-permute-done((bf16[2,1,256,256]{3,2,1,0:T(8,128)(2,1)S(1)}, bf16[2,1,256,256]{3,2,1,0:T(8,128)(2,1)S(1)}, u32[]{:S(2)}, u32[]{:S(2)}) %collective-permute-start.11) | collective-permute-done | bytes 262176 | tf_op jit(solution)/shard_map/ppermute | solution.py:234
  32.4 0.0 collective-permute-done.13.refs_1_
  32.5 1.1 %collective-permute-start.15 = (bf16[1,256,256]{2,1,0:T(8,128)(2,1)S(1)}, bf16[1,256,256]{2,1,0:T(8,128)(2,1)S(1)}, u32[]{:S(2)}, u32[]{:S(2)}) collective-permute-start(bf16[1,256,256]{2,1,0:T(8,128)(2,1)S(1)} %get-tuple-element.37), channel_id=1, source_target_pairs={{0,8},{8,0},{16,24},{24,16},{1,9},{9,1},{17,25},{25,17},{2,10},{10... | collective-permute-start | bytes 393224 | tf_op jit(solution)/shard_map/ppermute | solution.py:234
  33.7 1.6 %collective-permute-start.14 = (bf16[1,256,256]{2,1,0:T(8,128)(2,1)S(1)}, bf16[1,256,256]{2,1,0:T(8,128)(2,1)S(1)}, u32[]{:S(2)}, u32[]{:S(2)}) collective-permute-start(bf16[1,256,256]{2,1,0:T(8,128)(2,1)S(1)} %get-tuple-element.33), channel_id=1, source_target_pairs={{0,16},{8,24},{16,0},{24,8},{1,17},{9,25},{17,1},{25,9},{2,18},{10... | collective-permute-start | bytes 393224 | tf_op jit(solution)/shard_map/ppermute | solution.py:234
  35.2 3.4 %collective-permute-done.16.refs_0_ = bf16[2,256,128]{2,1,0:T(8,128)(2,1)S(1)} collective-permute-done((bf16[2,256,128]{2,1,0:T(8,128)(2,1)S(1)}, bf16[2,256,128]{2,1,0:T(8,128)(2,1)S(1)}, u32[]{:S(2)}, u32[]{:S(2)}) %collective-permute-start.16) | collective-permute-done | bytes 131104 | tf_op jit(solution)/shard_map/ppermute | solution.py:237
  38.6 0.0 collective-permute-done.17.refs_2_
  38.6 0.0 collective-permute-done.15.last_y
  38.6 0.0 collective-permute-done.14.last_x
  38.7 0.8 %results.1 = (bf16[2,256,2,128]{3,2,1,0:T(2,128)(2,1)}, bf16[2,256,128]{2,1,0:T(8,128)(2,1)}) custom-call(f32[1,256,256]{2,1,0:T(8,128)S(1)} %get-tuple-element.32.own_x, bf16[1,256,256]{2,1,0:T(8,128)(2,1)S(1)} %collective-permute-done.14.last_x, f32[1,256,256]{2,1,0:T(8,128)S(1)} %get-tuple-element.36.own_y, ...), custom_call_target="tpu_custom_call" | custom-call | tf_op jit(solution)/shard_map/results/pallas_call | solution.py:328
  (13 shorter events, 0.2 us)
Async XLA Ops:
  0.6 11.6 %collective-permute-start = (bf16[2,256,128]{2,1,0:T(8,128)(2,1)}, bf16[2,256,128]{2,1,0:T(8,128)(2,1)S(1)}, u32[]{:S(2)}, u32[]{:S(2)}) collective-permute-start(bf16[2,256,128]{2,1,0:T(8,128)(2,1)} %param.12), channel_id=1, source_target_pairs={{0,6},{1,7},{2,4},{3,5},{4,2},{5,3},{6,0},{7,1},{8,14},{9,15},{10,... | collective-permute-start | bytes 393224 | tf_op jit(solution)/shard_map/ppermute | solution.py:237
  5.7 8.0 %collective-permute-start.2 = (bf16[2,256,2,128]{3,2,1,0:T(2,128)(2,1)}, bf16[2,256,2,128]{3,2,1,0:T(2,128)(2,1)S(1)}, u32[]{:S(2)}, u32[]{:S(2)}) collective-permute-start(bf16[2,256,2,128]{3,2,1,0:T(2,128)(2,1)} %param.13), channel_id=1, source_target_pairs={{0,16},{8,24},{16,0},{24,8},{1,17},{9,25},{17,1},{25,9},{2,18},{10... | collective-permute-start | bytes 786440 | tf_op jit(solution)/shard_map/ppermute | solution.py:234
  7.3 8.2 %collective-permute-start.1 = (bf16[2,256,2,128]{3,2,1,0:T(2,128)(2,1)}, bf16[2,256,2,128]{3,2,1,0:T(2,128)(2,1)S(1)}, u32[]{:S(2)}, u32[]{:S(2)}) collective-permute-start(bf16[2,256,2,128]{3,2,1,0:T(2,128)(2,1)} %param.13), channel_id=1, source_target_pairs={{0,8},{8,0},{16,24},{24,16},{1,9},{9,1},{17,25},{25,17},{2,10},{10... | collective-permute-start | bytes 786440 | tf_op jit(solution)/shard_map/ppermute | solution.py:234
  8.8 8.5 %collective-permute-start.6 = (bf16[2,256,128]{2,1,0:T(8,128)(2,1)}, bf16[2,256,128]{2,1,0:T(8,128)(2,1)S(1)}, u32[]{:S(2)}, u32[]{:S(2)}) collective-permute-start(bf16[2,256,128]{2,1,0:T(8,128)(2,1)} %param.12), channel_id=1, source_target_pairs={{0,2},{1,3},{2,0},{3,1},{4,6},{5,7},{6,4},{7,5},{8,10},{9,11},{10,... | collective-permute-start | bytes 393224 | tf_op jit(solution)/shard_map/ppermute | solution.py:237
  8.8 8.5 %collective-permute-start.5 = (bf16[2,256,128]{2,1,0:T(8,128)(2,1)}, bf16[2,256,128]{2,1,0:T(8,128)(2,1)S(1)}, u32[]{:S(2)}, u32[]{:S(2)}) collective-permute-start(bf16[2,256,128]{2,1,0:T(8,128)(2,1)} %param.12), channel_id=1, source_target_pairs={{0,4},{1,5},{2,6},{3,7},{4,0},{5,1},{6,2},{7,3},{8,12},{9,13},{10,... | collective-permute-start | bytes 393224 | tf_op jit(solution)/shard_map/ppermute | solution.py:237
  9.5 1.2 %copy-start = (f32[1024]{0:T(1024)S(1)}, f32[1024]{0:T(1024)}, u32[]{:S(2)}) copy-start(f32[1024]{0:T(1024)} %vir_smem.1) | copy-start | bytes 12292
  9.5 1.2 %copy-start.3 = (s32[2]{0:T(128)S(1)}, s32[2]{0:T(128)}, u32[]{:S(2)}) copy-start(s32[2]{0:T(128)} %vir_offsets.1) | copy-start | bytes 28
  9.5 1.2 %copy-start.4 = (f32[128]{0:T(128)S(1)}, f32[128]{0:T(128)}, u32[]{:S(2)}) copy-start(f32[128]{0:T(128)} %occ_energy.1) | copy-start | bytes 1540
  10.7 0.7 %copy-start.1 = (s32[2,2]{1,0:T(2,128)S(1)}, s32[2,2]{1,0:T(2,128)}, u32[]{:S(2)}) copy-start(s32[2,2]{1,0:T(2,128)} %pairs.1) | copy-start | bytes 52
  10.7 0.7 %copy-start.2 = (s32[2]{0:T(128)S(1)}, s32[2]{0:T(128)}, u32[]{:S(2)}) copy-start(s32[2]{0:T(128)} %i_list.1) | copy-start | bytes 28
  11.4 0.9 %copy-start.5 = (bf16[2,256,128]{2,1,0:T(8,128)(2,1)S(1)}, bf16[2,256,128]{2,1,0:T(8,128)(2,1)}, u32[]{:S(2)}) copy-start(bf16[2,256,128]{2,1,0:T(8,128)(2,1)} %param.12) | copy-start | bytes 393220
  12.3 8.5 %collective-permute-start.7 = (bf16[2,2,256,128]{3,2,1,0:T(8,128)(2,1)S(1)}, bf16[2,2,256,128]{3,2,1,0:T(8,128)(2,1)S(1)}, u32[]{:S(2)}, u32[]{:S(2)}) collective-permute-start(bf16[2,2,256,128]{3,2,1,0:T(8,128)(2,1)S(1)} %pad_maximum_fusion.ends), channel_id=1, source_target_pairs={{0,1},{1,0},{2,3},{3,2},{4,5},{5,4},{6,7},{7,6},{8,9},{9,8},{10,11... | collective-permute-start | bytes 786440 | tf_op jit(solution)/shard_map/ppermute | solution.py:240
  13.9 5.0 %collective-permute-start.4 = (bf16[1,256,256]{2,1,0:T(8,128)(2,1)S(1)}, bf16[1,256,256]{2,1,0:T(8,128)(2,1)S(1)}, u32[]{:S(2)}, u32[]{:S(2)}) collective-permute-start(bf16[1,256,256]{2,1,0:T(8,128)(2,1)S(1)} %last_slots.1), channel_id=1, source_target_pairs={{0,8},{8,0},{16,24},{24,16},{1,9},{9,1},{17,25},{25,17},{2,10},{10... | collective-permute-start | bytes 393224 | tf_op jit(solution)/shard_map/ppermute | solution.py:234
  15.7 5.0 %collective-permute-start.3 = (bf16[1,256,256]{2,1,0:T(8,128)(2,1)S(1)}, bf16[1,256,256]{2,1,0:T(8,128)(2,1)S(1)}, u32[]{:S(2)}, u32[]{:S(2)}) collective-permute-start(bf16[1,256,256]{2,1,0:T(8,128)(2,1)S(1)} %first_slots.1), channel_id=1, source_target_pairs={{0,16},{8,24},{16,0},{24,8},{1,17},{9,25},{17,1},{25,9},{2,18},{10... | collective-permute-start | bytes 393224 | tf_op jit(solution)/shard_map/ppermute | solution.py:234
  17.3 3.5 %collective-permute-start.9 = (bf16[2,256,128]{2,1,0:T(8,128)(2,1)S(1)}, bf16[2,256,128]{2,1,0:T(8,128)(2,1)S(1)}, u32[]{:S(2)}, u32[]{:S(2)}) collective-permute-start(bf16[2,256,128]{2,1,0:T(8,128)(2,1)S(1)} %collective-permute-done.6.beside), channel_id=1, source_target_pairs={{0,1},{1,0},{2,3},{3,2},{4,5},{5,4},{6,7},{7,6},{8,9},{9,8},{10,11... | collective-permute-start | bytes 393224 | tf_op jit(solution)/shard_map/ppermute | solution.py:240
  17.3 3.5 %collective-permute-start.8 = (bf16[2,256,128]{2,1,0:T(8,128)(2,1)S(1)}, bf16[2,256,128]{2,1,0:T(8,128)(2,1)S(1)}, u32[]{:S(2)}, u32[]{:S(2)}) collective-permute-start(bf16[2,256,128]{2,1,0:T(8,128)(2,1)S(1)} %collective-permute-done.5.far), channel_id=1, source_target_pairs={{0,1},{1,0},{2,3},{3,2},{4,5},{5,4},{6,7},{7,6},{8,9},{9,8},{10,11... | collective-permute-start | bytes 393224 | tf_op jit(solution)/shard_map/ppermute | solution.py:240
  22.9 2.2 %collective-permute-start.12 = (bf16[4,2,256,128]{3,2,1,0:T(8,128)(2,1)S(1)}, bf16[4,2,256,128]{3,2,1,0:T(8,128)(2,1)S(1)}, u32[]{:S(2)}, u32[]{:S(2)}) collective-permute-start(bf16[4,2,256,128]{3,2,1,0:T(8,128)(2,1)S(1)} %get-tuple-element.29), channel_id=1, source_target_pairs={{0,1},{1,0},{2,3},{3,2},{4,5},{5,4},{6,7},{7,6},{8,9},{9,8},{10,11... | collective-permute-start | bytes 1572872 | tf_op jit(solution)/shard_map/ppermute | solution.py:240
  23.0 8.7 %collective-permute-start.10 = (bf16[2,1,256,256]{3,2,1,0:T(8,128)(2,1)S(1)}, bf16[2,1,256,256]{3,2,1,0:T(8,128)(2,1)S(1)}, u32[]{:S(2)}, u32[]{:S(2)}) collective-permute-start(bf16[2,1,256,256]{3,2,1,0:T(8,128)(2,1)S(1)} %get-tuple-element.26), channel_id=1, source_target_pairs={{0,8},{8,0},{16,24},{24,16},{1,9},{9,1},{17,25},{25,17},{2,10},{10... | collective-permute-start | bytes 786440 | tf_op jit(solution)/shard_map/ppermute | solution.py:234
  24.0 8.4 %collective-permute-start.11 = (bf16[2,1,256,256]{3,2,1,0:T(8,128)(2,1)S(1)}, bf16[2,1,256,256]{3,2,1,0:T(8,128)(2,1)S(1)}, u32[]{:S(2)}, u32[]{:S(2)}) collective-permute-start(bf16[2,1,256,256]{3,2,1,0:T(8,128)(2,1)S(1)} %get-tuple-element.27), channel_id=1, source_target_pairs={{0,16},{8,24},{16,0},{24,8},{1,17},{9,25},{17,1},{25,9},{2,18},{10... | collective-permute-start | bytes 786440 | tf_op jit(solution)/shard_map/ppermute | solution.py:234
  25.2 7.2 %collective-permute-start.13 = (bf16[2,256,128]{2,1,0:T(8,128)(2,1)S(1)}, bf16[2,256,128]{2,1,0:T(8,128)(2,1)S(1)}, u32[]{:S(2)}, u32[]{:S(2)}) collective-permute-start(bf16[2,256,128]{2,1,0:T(8,128)(2,1)S(1)} %get-tuple-element.30), channel_id=1, source_target_pairs={{0,2},{1,3},{2,0},{3,1},{4,6},{5,7},{6,4},{7,5},{8,10},{9,11},{10,... | collective-permute-start | bytes 393224 | tf_op jit(solution)/shard_map/ppermute | solution.py:237
  26.1 12.6 %collective-permute-start.16 = (bf16[2,256,128]{2,1,0:T(8,128)(2,1)S(1)}, bf16[2,256,128]{2,1,0:T(8,128)(2,1)S(1)}, u32[]{:S(2)}, u32[]{:S(2)}) collective-permute-start(bf16[2,256,128]{2,1,0:T(8,128)(2,1)S(1)} %get-tuple-element.39), channel_id=1, source_target_pairs={{0,4},{1,5},{2,6},{3,7},{4,0},{5,1},{6,2},{7,3},{8,12},{9,13},{10,... | collective-permute-start | bytes 393224 | tf_op jit(solution)/shard_map/ppermute | solution.py:237
  27.8 10.9 %collective-permute-start.17 = (bf16[2,256,128]{2,1,0:T(8,128)(2,1)S(1)}, bf16[2,256,128]{2,1,0:T(8,128)(2,1)S(1)}, u32[]{:S(2)}, u32[]{:S(2)}) collective-permute-start(bf16[2,256,128]{2,1,0:T(8,128)(2,1)S(1)} %get-tuple-element.41), channel_id=1, source_target_pairs={{0,6},{1,7},{2,4},{3,5},{4,2},{5,3},{6,0},{7,1},{8,14},{9,15},{10,... | collective-permute-start | bytes 393224 | tf_op jit(solution)/shard_map/ppermute | solution.py:237
  32.5 6.2 %collective-permute-start.15 = (bf16[1,256,256]{2,1,0:T(8,128)(2,1)S(1)}, bf16[1,256,256]{2,1,0:T(8,128)(2,1)S(1)}, u32[]{:S(2)}, u32[]{:S(2)}) collective-permute-start(bf16[1,256,256]{2,1,0:T(8,128)(2,1)S(1)} %get-tuple-element.37), channel_id=1, source_target_pairs={{0,8},{8,0},{16,24},{24,16},{1,9},{9,1},{17,25},{25,17},{2,10},{10... | collective-permute-start | bytes 393224 | tf_op jit(solution)/shard_map/ppermute | solution.py:234
  33.7 5.0 %collective-permute-start.14 = (bf16[1,256,256]{2,1,0:T(8,128)(2,1)S(1)}, bf16[1,256,256]{2,1,0:T(8,128)(2,1)S(1)}, u32[]{:S(2)}, u32[]{:S(2)}) collective-permute-start(bf16[1,256,256]{2,1,0:T(8,128)(2,1)S(1)} %get-tuple-element.33), channel_id=1, source_target_pairs={{0,16},{8,24},{16,0},{24,8},{1,17},{9,25},{17,1},{25,9},{2,18},{10... | collective-permute-start | bytes 393224 | tf_op jit(solution)/shard_map/ppermute | solution.py:234
